TPU v7x, 32 devices: a whole 2x2x4 slice. The times are simulated.
32 devices in a mesh: band: 8 (over z, y), batch: 4 (over x, core).
Axes of the slice: x: 2, y: 2, z: 4, core: 2. Of those that a mesh axis runs over, the one named last changes fastest.
Arguments:
- tiles: bfloat16 [8, 128, 128, 128], P('band'), may hold values from -256 to 256, as said below
- tile_row: int32 [8, 128], P('band'), may hold values from 0 to 3, as said below
- tile_col: int32 [8, 128], P('band'), may hold values from 0 to 15, as said below
- tile_count: int32 [8], P('band'), may hold values from 80 to 128, as said below
- cost: float32 [8, 2048], P('batch', 'band'), may hold values from -6 to 6
- bound_vec: float32 [4096], P('band'), may hold values from -6 to 6
- x_start: float32 [8, 2048], P('batch', 'band'), may hold values from 0 to 1
- y_start: float32 [8, 4096], P('batch', 'band'), may hold values from 0 to 1
Outputs:
- x_out: float32 [8, 2048], P('batch', 'band')
- y_out: float32 [8, 4096], P('batch', 'band')
Inputs may be any that keep to these rules, and one draw needn't show every extreme that they name: `tile_row`: within a band, tiles 0 to 3 lie in row blocks 0 to 3 in order. `tile_col`: the owner of column block k is band k // 2. Among a band's live tiles at most 32 have one owner, and the tiles of one owner stand in a row; tiles 0 to 1 of band b lie in column blocks b * 2 + t, so each band gives exactly 32 tiles to its own owner and every row block and column block holds a live tile. `tile_count`: one band in every draw is full. `tiles`: every entry has magnitude 0.1 or more.
All inputs are finite; a program needn't handle non-finite values.
Results may differ from a plain program's by a relative error of at most 0.0003.
Values sent between devices are 32-bit elements; how exact they have to be, the bound alone decides.
No kernel may reach another device: no remote copies, remote signals or barrier semaphores. Data moves between devices by JAX's collectives and lax.ppermute only.
A program may use at most 64 MiB of HBM per device.

v0:
```python
import jax
import jax.numpy as jnp
from jax import lax
from jax.sharding import PartitionSpec as P

ROWBLK = 4
COLBLK = 2


step_size = 0.0625
high = lax.Precision.HIGHEST


def row_peak_of(magnitude, select):
    row_max = jnp.max(magnitude, axis=2)
    return jnp.max(jnp.where(select[:, :, None], row_max[None], 0.0), axis=1)


def col_peak_of(magnitude, tile_rows, alive, slot_of, rscale, overflow):
    spread = rscale[tile_rows]
    peak = jnp.max(magnitude * spread[:, :, None], axis=1)
    peak = jnp.where(alive[:, None], peak, 0.0)
    return jnp.zeros((overflow, magnitude.shape[2]), jnp.float32).at[slot_of].max(peak, mode="drop")


def shards(tiles, tile_row, tile_col, tile_count, cost, bound_vec, x_start, y_start):
    blocks = tiles[0]
    tile_rows = tile_row[0]
    tile_cols = tile_col[0]
    live_count = tile_count[0]
    ntile = blocks.shape[0]
    tile_edge = blocks.shape[1]
    band_count = lax.axis_size("band")
    own_band = lax.axis_index("band")
    capacity = max(2, 2 * ntile // band_count)
    overflow = band_count * capacity
    indices = jnp.arange(ntile, dtype=jnp.int32)
    live = indices < live_count
    owner_of = tile_cols // COLBLK
    earlier = (
        (owner_of[:, None] == owner_of[None, :])
        & live[None, :]
        & (indices[None, :] < indices[:, None])
    )
    rank_in = jnp.sum(earlier.astype(jnp.int32), axis=1)
    slot_of = jnp.where(live, owner_of * capacity + rank_in, overflow)
    requests = (
        jnp.full((overflow,), -1, jnp.int32)
        .at[slot_of]
        .set(tile_cols, mode="drop")
        .reshape(band_count, capacity)
    )
    rowsel = (tile_rows[None, :] == jnp.arange(ROWBLK, dtype=jnp.int32)[:, None]) & live[None, :]
    rowsel_f = rowsel.astype(jnp.float32)
    widened = blocks.astype(jnp.float32)
    magnitude = jnp.abs(widened)
    quarter = ntile // lax.axis_size("batch")
    offset = lax.axis_index("batch") * quarter
    part_mag = lax.dynamic_slice_in_dim(magnitude, offset, quarter, 0)
    part_rows = lax.dynamic_slice_in_dim(tile_rows, offset, quarter, 0)
    part_live = lax.dynamic_slice_in_dim(live, offset, quarter, 0)
    part_slot = lax.dynamic_slice_in_dim(slot_of, offset, quarter, 0)
    part_sel = lax.dynamic_slice_in_dim(rowsel, offset, quarter, 1)
    row_peak = lax.pmax(row_peak_of(part_mag, part_sel), "batch")
    rscale = lax.rsqrt(row_peak)
    col_send = col_peak_of(part_mag, part_rows, part_live, part_slot, rscale, overflow)
    col_send = lax.pmax(col_send, "batch")
    got_ids, got_max = (
        lax.all_to_all(requests, "band", split_axis=0, concat_axis=0, tiled=True),
        lax.all_to_all(
            col_send.reshape(band_count, capacity, tile_edge),
            "band",
            split_axis=0,
            concat_axis=0,
            tiled=True,
        ),
    )
    local_id = got_ids - own_band * COLBLK
    owned = local_id[:, :, None] == jnp.arange(COLBLK, dtype=jnp.int32)[None, None, :]
    col_peak = jnp.max(jnp.where(owned[..., None], got_max[:, :, None, :], 0.0), axis=(0, 1))
    cscale = lax.rsqrt(col_peak).reshape(-1)
    rflat = rscale.reshape(-1)
    owned_f = owned.astype(jnp.float32)
    fetch_at = jnp.minimum(slot_of, overflow - 1)

    def forward(vec):
        columns = vec.shape[0]
        scaled = vec * cscale
        replies = jnp.einsum(
            "asc,kcj->askj", owned_f, scaled.reshape(columns, COLBLK, tile_edge), precision=high
        )
        returned = lax.all_to_all(replies, "band", split_axis=0, concat_axis=0, tiled=True).reshape(
            overflow, columns, tile_edge
        )
        picked = jnp.take(returned, fetch_at, axis=0)
        product = jnp.einsum("tij,tkj->tki", widened, picked, precision=high)
        product = jnp.where(live[:, None, None], product, 0.0)
        return (
            jnp.einsum("rt,tki->kri", rowsel_f, product, precision=high).reshape(columns, -1)
            * rflat
        )

    def adjoint(vec):
        columns = vec.shape[0]
        weighted = (vec * rflat).reshape(columns, ROWBLK, tile_edge)
        spread = jnp.einsum("rt,kri->tki", rowsel_f, weighted, precision=high)
        partial_value = jnp.einsum("tij,tki->tkj", widened, spread, precision=high)
        outgoing = (
            jnp.zeros((overflow, columns, tile_edge), jnp.float32)
            .at[slot_of]
            .add(partial_value, mode="drop")
        )
        incoming = lax.all_to_all(
            outgoing.reshape(band_count, capacity, columns, tile_edge),
            "band",
            split_axis=0,
            concat_axis=0,
            tiled=True,
        )
        summed = jnp.einsum("asc,askj->kcj", owned_f, incoming, precision=high)
        return summed.reshape(columns, -1) * cscale

    scost = cost * cscale
    sbound = bound_vec * rflat
    primal_one = jnp.maximum(0.0, x_start - step_size * (scost - adjoint(y_start)))
    dual_one = jnp.maximum(
        0.0, y_start + step_size * (sbound - forward(2.0 * primal_one - x_start))
    )
    primal_step = jnp.sum((primal_one - x_start) ** 2, axis=1, keepdims=True)
    dual_step = jnp.sum((dual_one - y_start) ** 2, axis=1, keepdims=True)
    primal_step, dual_step = lax.psum((primal_step, dual_step), "band")
    weight_ratio = jnp.sqrt((dual_step + 1e-06) / (primal_step + 1e-06))
    primal_two = jnp.maximum(
        0.0, primal_one - step_size / weight_ratio * (scost - adjoint(dual_one))
    )
    dual_two = jnp.maximum(
        0.0, dual_one + step_size * weight_ratio * (sbound - forward(2.0 * primal_two - primal_one))
    )
    return (primal_two, dual_two)


def solution(mesh):
    return jax.shard_map(
        shards,
        mesh=mesh,
        in_specs=(
            P("band", None, None, None),
            P("band", None),
            P("band", None),
            P("band"),
            P("batch", "band"),
            P("band"),
            P("batch", "band"),
            P("batch", "band"),
        ),
        out_specs=(P("batch", "band"), P("batch", "band")),
        check_vma=False,
    )
```

profile of v0, /device:TPU:0, one launch (start us, length us, event | category | flops | bytes accessed | tf_op | source)
XLA Modules:
  0.0 184.4 jit_solution(10617146375362840360)
XLA Ops:
  7.2 0.7 and_select_fusion.1
  7.8 0.7 fusion.49
  9.2 0.2 convert_reduce_fusion
  9.3 0.7 fusion.53
  10.0 1.1 scatter_custom_fusion
  11.1 0.7 all_to_all.21
  11.8 7.3 %all-to-all-start = ((s32[8,1,32]{2,1,0:T(1,128)}), s32[8,1,32]{2,1,0:T(1,128)S(1)}, u32[]{:S(2)}, u32[]{:S(2)}) async-start(s32[8,1,32]{2,1,0:T(1,128)} %all_to_all.21), calls=%async_computation | async-start | bytes 8192 | tf_op jit(solution)/shard_map/all_to_all | solution.py:69
  19.2 0.7 fusion.54
  19.9 0.7 fusion.41
  20.7 0.7 compare_and_fusion
  21.4 1.6 fusion
  23.1 6.3 %pmax.14 = f32[4,128]{1,0:T(4,128)S(1)} all-reduce(f32[4,128]{1,0:T(4,128)S(1)} %select_reduce_fusion.1), channel_id=1, replica_groups=mesh['band'=8,'batch'=4] {'batch'}, use_global_device_ids=true, to_apply=%region_4.5 | all-reduce | flops 512 | bytes 4096 | tf_op jit(solution)/shard_map/pmax | solution.py:64
  29.5 0.6 gather_fusion
  30.1 1.7 multiply_reduce_fusion
  31.8 1.4 scatter_custom_fusion.1
  33.2 0.7 broadcast_multiply_fusion.1
  33.9 0.3 fusion.46
  34.2 31.6 %all-reduce.3.cloned.1.call-done = f32[8,32,128]{2,1,0:T(8,128)} async-done(((f32[8,32,128]{2,1,0:T(8,128)}), f32[8,32,128]{2,1,0:T(8,128)}) %all-reduce.3.cloned.1.call-update) | async-done | bytes 131088 | tf_op jit(solution)/shard_map/pmax | solution.py:67
  65.8 5.5 %all-to-all-start.1 = ((f32[8,32,128]{2,1,0:T(8,128)}), f32[8,32,128]{2,1,0:T(8,128)S(1)}, u32[]{:S(2)}, u32[]{:S(2)}) async-start(f32[8,32,128]{2,1,0:T(8,128)} %all-reduce.3.cloned.1.call-done), calls=%async_computation.1 | async-start | bytes 262144 | tf_op jit(solution)/shard_map/all_to_all | solution.py:70
  71.3 5.1 %fusion.5 = f32[128,2,128]{2,1,0:T(2,128)S(1)} fusion(f32[128,2,128]{2,0,1:T(8,128)S(1)} %fusion.46, bf16[1,128,128,128]{3,2,1,0:T(8,128)(2,1)} %param.10), kind=kOutput, calls=%fused_computation.21 | convolution fusion | flops 50331648 | bytes 4456448 | tf_op jit(solution)/shard_map/tij,tki->tkj/dot_general | solution.py:107
  76.4 5.0 %scatter_fusion = f32[256,2,128]{2,1,0:T(2,128)S(1)} fusion(f32[256,2,128]{2,1,0:T(2,128)S(1)} %broadcast.187.clone, s32[128]{0:T(128)S(1)} %fusion.53, f32[128,2,128]{2,1,0:T(2,128)S(1)} %fusion.5), kind=kCustom, calls=%fused_computation.5 | custom fusion | flops 32768 | bytes 393728 | tf_op jit(solution)/shard_map/scatter-add | solution.py:111
  81.4 0.7 copy.41
  82.1 6.0 %all-to-all-start.2 = ((f32[8,32,2,128]{3,1,2,0:T(8,128)}), f32[8,32,2,128]{3,1,2,0:T(8,128)S(1)}, u32[]{:S(2)}, u32[]{:S(2)}) async-start(f32[8,32,2,128]{3,1,2,0:T(8,128)} %copy.41), calls=%async_computation.2 | async-start | bytes 524288 | tf_op jit(solution)/shard_map/all_to_all | solution.py:113
  88.1 0.1 select_reduce_fusion
  88.3 8.1 %all-to-all-done.2 = f32[8,32,2,128]{3,1,2,0:T(8,128)S(1)} async-done(((f32[8,32,2,128]{3,1,2,0:T(8,128)}), f32[8,32,2,128]{3,1,2,0:T(8,128)S(1)}, u32[]{:S(2)}, u32[]{:S(2)}) %all-to-all-start.2) | async-done | bytes 262176 | tf_op jit(solution)/shard_map/all_to_all | solution.py:113
  96.3 0.2 convolution_bitcast_fusion.3
  96.7 1.0 fusion.20
  97.8 3.4 %all-to-all-start.3 = ((f32[8,32,2,128]{3,1,2,0:T(8,128)}), f32[8,32,2,128]{3,1,2,0:T(8,128)S(1)}, u32[]{:S(2)}, u32[]{:S(2)}) async-start(f32[8,32,2,128]{3,1,2,0:T(8,128)} %fusion.20), calls=%async_computation.3 | async-start | bytes 524288 | tf_op jit(solution)/shard_map/all_to_all | solution.py:92
  101.2 8.1 %all-to-all-done.3 = f32[8,32,2,128]{3,1,2,0:T(8,128)S(1)} async-done(((f32[8,32,2,128]{3,1,2,0:T(8,128)}), f32[8,32,2,128]{3,1,2,0:T(8,128)S(1)}, u32[]{:S(2)}, u32[]{:S(2)}) %all-to-all-start.3) | async-done | bytes 262176 | tf_op jit(solution)/shard_map/all_to_all | solution.py:92
  109.3 0.2 copy.43
  109.6 0.7 gather_fusion.1
  110.3 8.4 %convolution_select_fusion.1 = f32[128,2,128]{2,1,0:T(2,128)S(1)} fusion(f32[128,2,128]{2,1,0:T(2,128)S(1)} %gather_fusion.1, pred[128]{0:T(512)(128)(4,1)S(1)} %get-tuple-element.13, pred[128]{0:T(512)(128)(4,1)S(1)} %iota_compare_fusion.3, bf16[1,128,128,128]{3,2,1,0:T(8,128)(2,1)} %param.10), kind=kOutput, calls=%fused_computation.11 | convolution fusion | flops 50397184 | bytes 4456704 | tf_op jit(solution)/shard_map/tij,tkj->tki/dot_general | solution.py:96
  118.7 0.2 convolution_bitcast_fusion.1
  119.0 0.3 fusion.43
  119.3 5.1 %fusion.2 = f32[128,2,128]{2,1,0:T(2,128)S(1)} fusion(f32[128,2,128]{2,0,1:T(8,128)S(1)} %fusion.43, bf16[1,128,128,128]{3,2,1,0:T(8,128)(2,1)} %param.10), kind=kOutput, calls=%fused_computation.18 | convolution fusion | flops 50331648 | bytes 4456448 | tf_op jit(solution)/shard_map/tij,tki->tkj/dot_general | solution.py:107
  124.5 5.0 %scatter_fusion.1 = f32[256,2,128]{2,1,0:T(2,128)S(1)} fusion(f32[256,2,128]{2,1,0:T(2,128)S(1)} %broadcast.187, s32[128]{0:T(128)S(1)} %fusion.53, f32[128,2,128]{2,1,0:T(2,128)S(1)} %fusion.2), kind=kCustom, calls=%fused_computation.6 | custom fusion | flops 32768 | bytes 393728 | tf_op jit(solution)/shard_map/scatter-add | solution.py:111
  129.4 0.7 copy.46
  130.2 3.4 %all-to-all-start.4 = ((f32[8,32,2,128]{3,1,2,0:T(8,128)}), f32[8,32,2,128]{3,1,2,0:T(8,128)S(1)}, u32[]{:S(2)}, u32[]{:S(2)}) async-start(f32[8,32,2,128]{3,1,2,0:T(8,128)} %copy.46), calls=%async_computation.4 | async-start | bytes 524288 | tf_op jit(solution)/shard_map/all_to_all | solution.py:113
  133.6 21.9 %all-reduce = (f32[2,1]{0,1:T(1,128)S(1)}, f32[2,1]{0,1:T(1,128)S(1)}) all-reduce(f32[2,1]{0,1:T(1,128)S(1)} %bitcast.167, f32[2,1]{0,1:T(1,128)S(1)} %bitcast.168), channel_id=1, replica_groups=mesh['band'=8,'batch'=4] {'band'}, use_global_device_ids=true, to_apply=%region_13.15 | all-reduce | flops 4 | bytes 32 | tf_op jit(solution)/shard_map/psum | solution.py:131
  155.5 0.2 convolution_bitcast_fusion.2
  155.7 0.7 subtract_multiply_fusion
  156.4 0.3 fusion.17
  156.7 10.6 %all_to_all.34 = f32[8,32,2,128]{3,1,2,0:T(8,128)S(1)} all-to-all(f32[8,32,2,128]{3,1,2,0:T(8,128)S(1)} %fusion.17), channel_id=1, replica_groups=mesh['band'=8,'batch'=4] {'band'}, dimensions={0} | all-to-all | bytes 524288 | tf_op jit(solution)/shard_map/all_to_all | solution.py:92
  167.4 0.2 copy.48
  167.6 0.7 gather_fusion.2
  168.4 8.4 %convolution_select_fusion = f32[128,2,128]{2,1,0:T(2,128)S(1)} fusion(f32[128,2,128]{2,1,0:T(2,128)S(1)} %gather_fusion.2, pred[128]{0:T(512)(128)(4,1)S(1)} %get-tuple-element.13, pred[128]{0:T(512)(128)(4,1)S(1)} %iota_compare_fusion.3, bf16[1,128,128,128]{3,2,1,0:T(8,128)(2,1)} %param.10), kind=kOutput, calls=%fused_computation.10 | convolution fusion | flops 50397184 | bytes 4456704 | tf_op jit(solution)/shard_map/tij,tkj->tki/dot_general | solution.py:96
  176.8 0.2 convolution_bitcast_fusion
  176.9 0.7 fusion.28
  (39 shorter events, 1.0 us)
Async XLA Ops:
  11.8 22.4 %all-to-all-start = ((s32[8,1,32]{2,1,0:T(1,128)}), s32[8,1,32]{2,1,0:T(1,128)S(1)}, u32[]{:S(2)}, u32[]{:S(2)}) async-start(s32[8,1,32]{2,1,0:T(1,128)} %all_to_all.21), calls=%async_computation | async-start | bytes 8192 | tf_op jit(solution)/shard_map/all_to_all | solution.py:69
  19.1 46.7 %all-reduce.3.cloned.1.call-start = ((), (), s32[]{:S(2)}) async-start(), calls=%async_computation.6 | async-start | bytes 262144 | tf_op jit(solution)/shard_map/pmax | solution.py:67
  30.0 66.5 %copy-start.1 = (f32[2,256]{1,0:T(2,128)S(1)}, f32[2,256]{1,0:T(2,128)}, u32[]{:S(2)}) copy-start(f32[2,256]{1,0:T(2,128)} %param.16) | copy-start | bytes 6148
  30.0 66.5 %copy-start.2 = (f32[2,256]{1,0:T(2,128)S(1)}, f32[2,256]{1,0:T(2,128)}, u32[]{:S(2)}) copy-start(f32[2,256]{1,0:T(2,128)} %param.14) | copy-start | bytes 6148
  31.8 69.4 %copy-start.3 = (f32[512]{0:T(512)S(1)}, f32[512]{0:T(512)}, u32[]{:S(2)}) copy-start(f32[512]{0:T(512)} %param.15) | copy-start | bytes 6148
  65.8 16.4 %all-to-all-start.1 = ((f32[8,32,128]{2,1,0:T(8,128)}), f32[8,32,128]{2,1,0:T(8,128)S(1)}, u32[]{:S(2)}, u32[]{:S(2)}) async-start(f32[8,32,128]{2,1,0:T(8,128)} %all-reduce.3.cloned.1.call-done), calls=%async_computation.1 | async-start | bytes 262144 | tf_op jit(solution)/shard_map/all_to_all | solution.py:70
  81.4 37.5 %copy-start = (f32[2,512]{1,0:T(2,128)S(1)}, f32[2,512]{1,0:T(2,128)}, u32[]{:S(2)}) copy-start(f32[2,512]{1,0:T(2,128)} %param.17) | copy-start | bytes 12292
  82.1 14.2 %all-to-all-start.2 = ((f32[8,32,2,128]{3,1,2,0:T(8,128)}), f32[8,32,2,128]{3,1,2,0:T(8,128)S(1)}, u32[]{:S(2)}, u32[]{:S(2)}) async-start(f32[8,32,2,128]{3,1,2,0:T(8,128)} %copy.41), calls=%async_computation.2 | async-start | bytes 524288 | tf_op jit(solution)/shard_map/all_to_all | solution.py:113
  97.8 11.6 %all-to-all-start.3 = ((f32[8,32,2,128]{3,1,2,0:T(8,128)}), f32[8,32,2,128]{3,1,2,0:T(8,128)S(1)}, u32[]{:S(2)}, u32[]{:S(2)}) async-start(f32[8,32,2,128]{3,1,2,0:T(8,128)} %fusion.20), calls=%async_computation.3 | async-start | bytes 524288 | tf_op jit(solution)/shard_map/all_to_all | solution.py:92
  130.2 25.3 %all-to-all-start.4 = ((f32[8,32,2,128]{3,1,2,0:T(8,128)}), f32[8,32,2,128]{3,1,2,0:T(8,128)S(1)}, u32[]{:S(2)}, u32[]{:S(2)}) async-start(f32[8,32,2,128]{3,1,2,0:T(8,128)} %copy.46), calls=%async_computation.4 | async-start | bytes 524288 | tf_op jit(solution)/shard_map/all_to_all | solution.py:113
Sparse Core Ops, SparseCore 0:
  33.3 32.3 all-reduce.2
where the time goes:
time: 185 us; the launch traced here: 184 us
  waiting for transfers between devices  47.8 us (26%)
  blocking collectives  38.8 us (21%)
  matrix products  29.6 us (16%)
  starting transfers between devices  25.6 us (14%)
  other arithmetic  21.6 us (12%)
  between operations  14.9 us (8%)
  local copies, waits for them, and re-layouts  6.14 us (3%)
    pmax x1, waiting for transfers between devices, shards(): col_send = lax.pmax(col_send, 'batch')  31.6 us
    psum x1, blocking collectives, shards(): primal_step, dual_step = lax.psum((primal_step, dual_step), 'band')  21.9 us
    dot_general x2, matrix products, forward(): product = jnp.einsum('tij,tkj->tki', widened, picked, precision=high)  16.8 us
    all_to_all x1, blocking collectives, forward(): lax.all_to_all(replies, 'band', split_axis=0, concat_axis=0, tiled=True)  10.6 us
    dot_general x2, matrix products, adjoint(): partial_value = jnp.einsum('tij,tki->tkj', widened, spread, precision=high)  10.1 us
    scatter-add x2, other arithmetic, adjoint(): outgoing = jnp.zeros((overflow, columns, tile_edge), jnp.float32).at[slot...  9.93 us
    all_to_all x2, starting transfers between devices, adjoint(): lax.all_to_all(outgoing.reshape(band_count, capacity, columns, tile_edge)...  9.37 us
    all_to_all x1, waiting for transfers between devices, forward(): lax.all_to_all(replies, 'band', split_axis=0, concat_axis=0, tiled=True)  8.12 us
  transfers between devices with their start and end apart: 6, of which 3 were waited for; matrix products, arithmetic and copies ran while one was open for 11% of the time, Pallas kernels for 0%

commit v1 on v0

v1 whole, which is shorter than its diff:
```python
import functools

import jax
import jax.numpy as jnp
from jax import lax
from jax.experimental import pallas as pl
from jax.experimental.pallas import tpu as pltpu
from jax.sharding import PartitionSpec as P

ROWBLK = 4
COLBLK = 2
EDGE = 128
VECS = 2
LEFT = 16
GROUP = 32
KEPT = 8

step_size = 0.0625


def split(value):
    high = value.astype(jnp.bfloat16).astype(jnp.float32)
    rest = value - high
    mid = rest.astype(jnp.bfloat16).astype(jnp.float32)
    low = (rest - mid).astype(jnp.bfloat16).astype(jnp.float32)
    return high, mid, low


def joined(rows):
    return rows[0:2] + rows[2:4] + rows[4:6]


def fetch(tiles_ref, held_ref, sems, g):
    group = pl.ds(g * GROUP, GROUP)
    return pltpu.make_async_copy(tiles_ref.at[group], held_ref.at[group], sems.at[g])


def row_of(rows_ref, count, t):
    return jnp.where(t < count, rows_ref[t], ROWBLK)


def products(multiply, place, stage_ref, into_ref, ntile):
    stage_ref[1] = jnp.zeros(stage_ref.shape[1:], jnp.float32)

    def group(g, carry):
        now = g % 2
        for u in range(GROUP):
            stage_ref[now, u] = multiply(g * GROUP + u)[0:KEPT]
        for u in range(GROUP):
            into_ref[place(jnp.maximum((g - 1) * GROUP + u, 0))] += stage_ref[1 - now, u]
        return carry

    groups = ntile // GROUP
    lax.fori_loop(0, groups, group, 0)
    for u in range(GROUP):
        into_ref[place(ntile - GROUP + u)] += stage_ref[(groups - 1) % 2, u]


def put_left(left32_ref, left_ref, index, value):
    for s, term in enumerate(split(value)):
        left32_ref[index, 2 * s : 2 * s + 2, :] = term
    left_ref[index] = left32_ref[index].astype(jnp.bfloat16)


def adjoint_start(sums_ref, cost_ref, band):
    sums_ref[...] = jnp.zeros_like(sums_ref)
    for j in range(COLBLK):
        sums_ref[band * COLBLK + j, 0:VECS, :] = -cost_ref[:, j * EDGE : (j + 1) * EDGE]


def adjoint_sum(sums_ref, v):
    blocks = sums_ref.shape[0]
    flat = sums_ref.reshape(blocks * KEPT, EDGE)
    return sum(flat[pl.ds(VECS * s + v, blocks, stride=KEPT), :] for s in range(3))


def forward_left(left32_ref, left_ref, v, value):
    blocks = left32_ref.shape[0]
    flat = left32_ref.reshape(blocks * LEFT, EDGE)
    for s, term in enumerate(split(value)):
        flat[pl.ds(VECS * s + v, blocks, stride=LEFT), :] = term


def forward_pass(rows_ref, cols_ref, live, held_ref, right_ref, stage_ref, out_ref):
    def multiply(t):
        return lax.dot_general(
            right_ref[cols_ref[t]],
            held_ref[t],
            (((1,), (1,)), ((), ())),
            preferred_element_type=jnp.float32,
        )

    out_ref[...] = jnp.zeros_like(out_ref)
    place = lambda t: row_of(rows_ref, live, t)
    products(multiply, place, stage_ref, out_ref, held_ref.shape[0])


def adjoint_pass(rows_ref, cols_ref, live, held_ref, left_ref, stage_ref, sums_ref):
    def multiply(t):
        r = row_of(rows_ref, live, t)
        return jnp.dot(left_ref[r], held_ref[t], preferred_element_type=jnp.float32)

    products(multiply, lambda t: cols_ref[t], stage_ref, sums_ref, held_ref.shape[0])


def scale_kernel(
    place_ref, rows_ref, cols_ref, count_ref, tiles_ref, y_ref, x_ref, cost_ref,
    send_ref, rscale_ref, held_ref,
    sems, peak_ref, spread_ref, left32_ref, left_ref, top_ref, stage_ref, sums_ref,
):
    ntile = held_ref.shape[0]
    blocks = top_ref.shape[0]
    live = count_ref[0]
    band = place_ref[0]
    groups = ntile // GROUP
    for g in range(groups):
        fetch(tiles_ref, held_ref, sems, g).start()
    peak_ref[...] = jnp.zeros_like(peak_ref)
    top_ref[...] = jnp.zeros_like(top_ref)
    left32_ref[...] = jnp.zeros_like(left32_ref)
    left_ref[ROWBLK] = jnp.zeros((LEFT, EDGE), jnp.bfloat16)
    spread_ref[ROWBLK] = jnp.zeros((EDGE, EDGE), jnp.float32)
    adjoint_start(sums_ref, cost_ref, band)

    def row_peaks(g, carry):
        fetch(tiles_ref, held_ref, sems, g).wait()
        for u in range(GROUP):
            t = g * GROUP + u
            r = row_of(rows_ref, live, t)
            peak_ref[r] = jnp.maximum(peak_ref[r], jnp.abs(held_ref[t]))
        return carry

    lax.fori_loop(0, groups, row_peaks, 0)

    for r in range(ROWBLK):
        peak = jnp.max(peak_ref[r].astype(jnp.float32), axis=1, keepdims=True)
        spread = jnp.broadcast_to(lax.rsqrt(peak), (EDGE, EDGE))
        spread_ref[r] = spread
        scale = spread.T[0:1, :]
        rscale_ref[r : r + 1, :] = scale
        put_left(left32_ref, left_ref, r, y_ref[:, r * EDGE : (r + 1) * EDGE] * scale)

    def multiply(t):
        r = row_of(rows_ref, live, t)
        c = cols_ref[t]
        tile = held_ref[t]
        scaled = jnp.abs(tile).astype(jnp.float32) * spread_ref[r]
        top_ref[c] = jnp.maximum(top_ref[c], jnp.max(scaled.reshape(EDGE // 8, 8, EDGE), axis=0))
        return jnp.dot(left_ref[r], tile, preferred_element_type=jnp.float32)

    products(multiply, lambda t: cols_ref[t], stage_ref, sums_ref, ntile)

    send_ref[0:blocks, :] = jnp.max(top_ref[...], axis=1)
    row = lax.broadcasted_iota(jnp.int32, (blocks, EDGE), 0)
    for v in range(VECS):
        send_ref[(1 + v) * blocks : (2 + v) * blocks, :] = adjoint_sum(sums_ref, v)
        own = jnp.zeros((blocks, EDGE), jnp.float32)
        for j in range(COLBLK):
            part = x_ref[v : v + 1, j * EDGE : (j + 1) * EDGE]
            own = jnp.where(row == band * COLBLK + j, part, own)
        send_ref[(3 + v) * blocks : (4 + v) * blocks, :] = own


def step_kernel(
    place_ref, rows_ref, cols_ref, count_ref, held_ref, got_ref, rscale_ref, y_ref, bound_ref, cost_ref,
    send_ref, x_one_ref, cscale_ref, y_one_ref, moved_ref,
    right32_ref, right_ref, out_ref, left32_ref, left_ref, stage_ref, sums_ref,
):
    blocks = right_ref.shape[0]
    live = count_ref[0]
    band = place_ref[0]
    right32_ref[...] = jnp.zeros_like(right32_ref)
    left32_ref[...] = jnp.zeros_like(left32_ref)
    left_ref[ROWBLK] = jnp.zeros((LEFT, EDGE), jnp.bfloat16)
    adjoint_start(sums_ref, cost_ref, band)

    cscale = lax.rsqrt(got_ref[0:blocks, :])
    cscale_ref[...] = cscale
    for v in range(VECS):
        total = got_ref[(1 + v) * blocks : (2 + v) * blocks, :]
        before = got_ref[(3 + v) * blocks : (4 + v) * blocks, :]
        after = jnp.maximum(0.0, before + step_size * (cscale * total))
        x_one_ref[v * blocks : (v + 1) * blocks, :] = after
        moved = jnp.sum(jnp.sum((after - before) ** 2, axis=0, keepdims=True), axis=1, keepdims=True)
        moved_ref[v : v + 1, :] = jnp.broadcast_to(moved, (1, EDGE))
        forward_left(right32_ref, right_ref, v, cscale * (2.0 * after - before))
    right_ref[...] = right32_ref[...].astype(jnp.bfloat16)

    forward_pass(rows_ref, cols_ref, live, held_ref, right_ref, stage_ref, out_ref)

    moved = jnp.zeros((VECS, EDGE), jnp.float32)
    for r in range(ROWBLK):
        span = slice(r * EDGE, (r + 1) * EDGE)
        scale = rscale_ref[r : r + 1, :]
        before = y_ref[:, span]
        after = jnp.maximum(
            0.0, before + step_size * (scale * (bound_ref[:, span] - joined(out_ref[r])))
        )
        y_one_ref[:, span] = after
        moved += (after - before) ** 2
        put_left(left32_ref, left_ref, r, after * scale)

    adjoint_pass(rows_ref, cols_ref, live, held_ref, left_ref, stage_ref, sums_ref)
    for v in range(VECS):
        send_ref[v * blocks : (v + 1) * blocks, :] = adjoint_sum(sums_ref, v)
    send_ref[VECS * blocks :, :] = jnp.zeros((8, EDGE), jnp.float32)
    send_ref[VECS * blocks : VECS * blocks + VECS, :] = moved


def last_kernel(
    place_ref, rows_ref, cols_ref, count_ref, held_ref, got_ref, rscale_ref, y_ref, bound_ref, x_one_ref, cscale_ref, moved_ref,
    x_out_ref, y_out_ref,
    right32_ref, right_ref, stage_ref, out_ref,
):
    blocks = right_ref.shape[0]
    live = count_ref[0]
    band = place_ref[0]
    right32_ref[...] = jnp.zeros_like(right32_ref)
    cscale = cscale_ref[...]
    row = lax.broadcasted_iota(jnp.int32, (blocks, EDGE), 0)
    dual = jnp.sum(got_ref[VECS * blocks : VECS * blocks + VECS, :], axis=1, keepdims=True)
    ratio = jnp.sqrt((dual + 1e-06) / (moved_ref[...] + 1e-06))
    for v in range(VECS):
        total = got_ref[v * blocks : (v + 1) * blocks, :]
        before = x_one_ref[v * blocks : (v + 1) * blocks, :]
        after = jnp.maximum(0.0, before + step_size / ratio[v : v + 1, :] * (cscale * total))
        for j in range(COLBLK):
            own = jnp.where(row == band * COLBLK + j, after, 0.0)
            x_out_ref[v : v + 1, j * EDGE : (j + 1) * EDGE] = jnp.sum(own, axis=0, keepdims=True)
        forward_left(right32_ref, right_ref, v, cscale * (2.0 * after - before))
    right_ref[...] = right32_ref[...].astype(jnp.bfloat16)

    forward_pass(rows_ref, cols_ref, live, held_ref, right_ref, stage_ref, out_ref)

    for r in range(ROWBLK):
        span = slice(r * EDGE, (r + 1) * EDGE)
        scale = rscale_ref[r : r + 1, :]
        y_out_ref[:, span] = jnp.maximum(
            0.0,
            y_ref[:, span]
            + step_size * ratio * (scale * (bound_ref[:, span] - joined(out_ref[r]))),
        )


def over_bands(value, combine):
    bands = lax.axis_size("band")
    hop = 1
    while hop < bands:
        other = lax.ppermute(value, "band", [(i, i ^ hop) for i in range(bands)])
        value = combine(value, other)
        hop *= 2
    return value


def shards(tiles, tile_row, tile_col, tile_count, cost, bound_vec, x_start, y_start):
    tiles = tiles[0]
    ntile = tiles.shape[0]
    bands = lax.axis_size("band")
    blocks = bands * COLBLK
    place = lax.axis_index("band").astype(jnp.int32).reshape(1)
    scalars = (place, tile_row[0], tile_col[0], tile_count)
    bound = bound_vec.reshape(1, -1)
    nrow = bound.shape[1]
    f32 = lambda *shape: jax.ShapeDtypeStruct(shape, jnp.float32)
    smem = [pl.BlockSpec(memory_space=pltpu.SMEM)] * 4
    hbm = [pl.BlockSpec(memory_space=pltpu.HBM)]
    vmem = lambda n: [pl.BlockSpec(memory_space=pltpu.VMEM)] * n
    left = [pltpu.VMEM((ROWBLK + 1, LEFT, EDGE), jnp.float32), pltpu.VMEM((ROWBLK + 1, LEFT, EDGE), jnp.bfloat16)]
    right = [pltpu.VMEM((blocks, LEFT, EDGE), jnp.float32), pltpu.VMEM((blocks, LEFT, EDGE), jnp.bfloat16)]
    rows_out = [pltpu.VMEM((ROWBLK + 1, KEPT, EDGE), jnp.float32)]
    sums = [pltpu.VMEM((blocks, KEPT, EDGE), jnp.float32)]
    stage = [pltpu.VMEM((2, GROUP, KEPT, EDGE), jnp.float32)]
    params = pltpu.CompilerParams(vmem_limit_bytes=32 * 1024 * 1024)

    send, rscale, held = pl.pallas_call(
        scale_kernel,
        out_shape=(f32(5 * blocks, EDGE), f32(ROWBLK, EDGE), pltpu.VMEM(tiles.shape, jnp.bfloat16)),
        in_specs=smem + hbm + vmem(3),
        out_specs=tuple(vmem(3)),
        scratch_shapes=[pltpu.SemaphoreType.DMA((ntile // GROUP,))]
        + [pltpu.VMEM((ROWBLK + 1, EDGE, EDGE), jnp.bfloat16), pltpu.VMEM((ROWBLK + 1, EDGE, EDGE), jnp.float32)]
        + left
        + [pltpu.VMEM((blocks, 8, EDGE), jnp.float32)]
        + stage
        + sums,
        compiler_params=params,
        name="scales",
    )(*scalars, pltpu.with_memory_space_constraint(tiles, pltpu.HBM), y_start, x_start, cost)

    is_peak = lax.broadcasted_iota(jnp.int32, send.shape, 0) < blocks
    got = over_bands(send, lambda a, b: jnp.where(is_peak, jnp.maximum(a, b), a + b))

    send, x_one, cscale, y_one, moved = pl.pallas_call(
        step_kernel,
        out_shape=(
            f32(VECS * blocks + 8, EDGE), f32(VECS * blocks, EDGE), f32(blocks, EDGE), f32(VECS, nrow), f32(VECS, EDGE),
        ),
        in_specs=smem + vmem(6),
        out_specs=tuple(vmem(5)),
        scratch_shapes=right + rows_out + left + stage + sums,
        compiler_params=params,
        name="first_step",
    )(*scalars, held, got, rscale, y_start, bound, cost)

    got = over_bands(send, lambda a, b: a + b)

    return pl.pallas_call(
        last_kernel,
        out_shape=(f32(*x_start.shape), f32(*y_start.shape)),
        in_specs=smem + vmem(8),
        out_specs=tuple(vmem(2)),
        scratch_shapes=right + stage + rows_out,
        compiler_params=params,
        name="second_step",
    )(*scalars, held, got, rscale, y_one, bound, x_one, cscale, moved)


def solution(mesh):
    return jax.shard_map(
        shards,
        mesh=mesh,
        in_specs=(
            P("band", None, None, None),
            P("band", None),
            P("band", None),
            P("band"),
            P("batch", "band"),
            P("band"),
            P("batch", "band"),
            P("batch", "band"),
        ),
        out_specs=(P("batch", "band"), P("batch", "band")),
        check_vma=False,
    )
```

time: 185 us -> 46.7 us (0.25)
  blocking collectives: 38.8 us -> 0 us
  waiting for transfers between devices: 47.8 us -> 11.3 us
  matrix products: 29.6 us -> 0 us
  other arithmetic: 21.6 us -> 0.25 us
  Pallas kernels: 0 us -> 14.8 us
  between operations: 14.9 us -> 1.36 us
  starting transfers between devices: 25.6 us -> 15.3 us
  local copies, waits for them, and re-layouts: 6.14 us -> 3.36 us
    pmax x1 -> x0, waiting for transfers between devices: 31.6 us -> none  [shards(): col_send = lax.pmax(col_send, 'batch')]
    dot_general x12 -> x0, matrix products: 29.6 us -> none  [the longest x2 16.8 us: forward(): product = jnp.einsum('tij,tkj->tki', widened, picked, precision=high)]
    all_to_all x5 -> x0, starting transfers between devices: 25.6 us -> none  [the longest x2 9.37 us: adjoint(): lax.all_to_all(outgoing.reshape(band_count, capacity, columns, tile_edge)...]
    psum x1 -> x0, blocking collectives: 21.9 us -> none  [shards(): primal_step, dual_step = lax.psum((primal_step, dual_step), 'band')]
    all_to_all x5 -> x0, waiting for transfers between devices: 16.2 us -> none  [the longest x1 8.12 us: forward(): lax.all_to_all(replies, 'band', split_axis=0, concat_axis=0, tiled=True)]
    ppermute x0 -> x6, starting transfers between devices: none -> 15.3 us  [over_bands(): other = lax.ppermute(value, 'band', [(i, i ^ hop) for i in range(bands)])]
    pallas_call x0 -> x3, Pallas kernels: none -> 14.8 us  [the longest x1 5.35 us: shards(): pl.pallas_call(scale_kernel, out_shape=(f32(5 * blocks, EDGE), f32(ROWBLK...]
    ppermute x0 -> x6, waiting for transfers between devices: none -> 11.3 us  [over_bands(): other = lax.ppermute(value, 'band', [(i, i ^ hop) for i in range(bands)])]
  transfers between devices with their start and end apart: 6 -> 6, of which waited for: 3 -> 6; matrix products, arithmetic and copies ran while one was open for 11% -> 0% of each run, Pallas kernels for 0% -> 0%
where the time goes in v1:
time: 46.7 us; the launch traced here: 46.4 us
  starting transfers between devices  15.3 us (33%)
  Pallas kernels  14.8 us (32%)
  waiting for transfers between devices  11.3 us (24%)
  local copies, waits for them, and re-layouts  3.36 us (7%)
  between operations  1.36 us (3%)
    ppermute x6, starting transfers between devices, over_bands(): other = lax.ppermute(value, 'band', [(i, i ^ hop) for i in range(bands)])  15.3 us
    ppermute x6, waiting for transfers between devices, over_bands(): other = lax.ppermute(value, 'band', [(i, i ^ hop) for i in range(bands)])  11.3 us
    pallas_call x1, Pallas kernels, shards(): pl.pallas_call(scale_kernel, out_shape=(f32(5 * blocks, EDGE), f32(ROWBLK...  5.35 us
    pallas_call x1, Pallas kernels, shards(): pl.pallas_call(step_kernel, out_shape=(f32(VECS * blocks + 8, EDGE), f32(...  5.33 us
    pallas_call x1, Pallas kernels, shards(): pl.pallas_call(last_kernel, out_shape=(f32(*x_start.shape), f32(*y_start....  4.11 us
    unnamed x12, local copies, waits for them, and re-layouts  3.36 us
  transfers between devices with their start and end apart: 6, of which 6 were waited for; matrix products, arithmetic and copies ran while one was open for 0% of the time, Pallas kernels for 0%

profile of v1, /device:TPU:0, one launch (start us, length us, event | category | flops | bytes accessed | tf_op | source)
XLA Modules:
  0.0 46.4 jit_solution(1182019847796584616)
XLA Ops:
  0.6 0.0 copy-start.1
  1.3 0.0 copy-start
  1.3 0.7 %copy-done = f32[2,512]{1,0:T(2,128)S(1)} copy-done((f32[2,512]{1,0:T(2,128)S(1)}, f32[2,512]{1,0:T(2,128)}, u32[]{:S(2)}) %copy-start) | copy-done | bytes 4120
  2.0 0.0 copy-start.2
  2.0 0.7 %copy-done.2 = f32[2,256]{1,0:T(2,128)S(1)} copy-done((f32[2,256]{1,0:T(2,128)S(1)}, f32[2,256]{1,0:T(2,128)}, u32[]{:S(2)}) %copy-start.2) | copy-done | bytes 2072
  2.7 0.0 copy-start.3
  2.7 0.7 %copy-done.3 = s32[1,128]{1,0:T(1,128)S(1)} copy-done((s32[1,128]{1,0:T(1,128)S(1)}, s32[1,128]{1,0:T(1,128)}, u32[]{:S(2)}) %copy-start.3) | copy-done | bytes 536
  3.3 0.0 copy-start.4
  3.3 0.7 %copy-done.4 = s32[1,128]{1,0:T(1,128)S(1)} copy-done((s32[1,128]{1,0:T(1,128)S(1)}, s32[1,128]{1,0:T(1,128)}, u32[]{:S(2)}) %copy-start.4) | copy-done | bytes 536
  4.0 0.0 copy-start.5
  4.0 0.7 %copy-done.5 = f32[2,256]{1,0:T(2,128)S(1)} copy-done((f32[2,256]{1,0:T(2,128)S(1)}, f32[2,256]{1,0:T(2,128)}, u32[]{:S(2)}) %copy-start.5) | copy-done | bytes 2072
  4.7 5.3 %scales.1 = (f32[80,128]{1,0:T(8,128)S(1)}, f32[4,128]{1,0:T(4,128)S(1)}, bf16[128,128,128]{2,1,0:T(8,128)(2,1)S(1)}) custom-call(s32[1]{0:T(128)} %bitcast.place_ref, s32[128]{0:T(128)S(1)} %bitcast.7, s32[128]{0:T(128)S(1)} %bitcast.10, s32[1]{0:T(128)S(6)} %copy.10.count_ref, bf16[128,128,128]{2,1,0:T(8,128)(2,1)} %bitcast.13, f32[2,512]{1,0:T(2,128)S(1)} %copy-done, ...), custom_call_target="tpu_custom_call" | custom-call | tf_op jit(solution)/shard_map/scales/pallas_call | solution.py:275
  10.0 3.0 %collective-permute-start = (f32[80,128]{1,0:T(8,128)S(1)}, f32[80,128]{1,0:T(8,128)S(1)}, u32[]{:S(2)}, u32[]{:S(2)}) collective-permute-start(f32[80,128]{1,0:T(8,128)S(1)} %get-tuple-element.11), channel_id=1, source_target_pairs={{0,4},{4,0},{8,12},{12,8},{16,20},{20,16},{24,28},{28,24},{1,5},{5... | collective-permute-start | bytes 122888 | tf_op jit(solution)/shard_map/ppermute | solution.py:249
  13.1 2.0 %collective-permute-done = f32[80,128]{1,0:T(8,128)S(1)} collective-permute-done((f32[80,128]{1,0:T(8,128)S(1)}, f32[80,128]{1,0:T(8,128)S(1)}, u32[]{:S(2)}, u32[]{:S(2)}) %collective-permute-start) | collective-permute-done | bytes 40992 | tf_op jit(solution)/shard_map/ppermute | solution.py:249
  15.0 0.1 add_select_fusion.2
  15.1 2.1 %collective-permute-start.1 = (f32[80,128]{1,0:T(8,128)S(1)}, f32[80,128]{1,0:T(8,128)S(1)}, u32[]{:S(2)}, u32[]{:S(2)}) collective-permute-start(f32[80,128]{1,0:T(8,128)S(1)} %add_select_fusion.2), channel_id=1, source_target_pairs={{0,8},{4,12},{8,0},{12,4},{16,24},{20,28},{24,16},{28,20},{1,9},{5... | collective-permute-start | bytes 122888 | tf_op jit(solution)/shard_map/ppermute | solution.py:249
  17.3 2.0 %collective-permute-done.1 = f32[80,128]{1,0:T(8,128)S(1)} collective-permute-done((f32[80,128]{1,0:T(8,128)S(1)}, f32[80,128]{1,0:T(8,128)S(1)}, u32[]{:S(2)}, u32[]{:S(2)}) %collective-permute-start.1) | collective-permute-done | bytes 40992 | tf_op jit(solution)/shard_map/ppermute | solution.py:249
  19.2 0.1 add_select_fusion.1
  19.3 3.1 %collective-permute-start.2 = (f32[80,128]{1,0:T(8,128)S(1)}, f32[80,128]{1,0:T(8,128)S(1)}, u32[]{:S(2)}, u32[]{:S(2)}) collective-permute-start(f32[80,128]{1,0:T(8,128)S(1)} %add_select_fusion.1), channel_id=1, source_target_pairs={{0,16},{4,20},{8,24},{12,28},{16,0},{20,4},{24,8},{28,12},{1,17},{... | collective-permute-start | bytes 122888 | tf_op jit(solution)/shard_map/ppermute | solution.py:249
  22.4 2.0 %collective-permute-done.2 = f32[80,128]{1,0:T(8,128)S(1)} collective-permute-done((f32[80,128]{1,0:T(8,128)S(1)}, f32[80,128]{1,0:T(8,128)S(1)}, u32[]{:S(2)}, u32[]{:S(2)}) %collective-permute-start.2) | collective-permute-done | bytes 40992 | tf_op jit(solution)/shard_map/ppermute | solution.py:249
  24.4 0.1 add_select_fusion.got_ref
  24.5 0.0 copy-done.1
  24.5 5.3 %first_step.1 = (f32[40,128]{1,0:T(8,128)S(1)}, f32[32,128]{1,0:T(8,128)S(1)}, f32[16,128]{1,0:T(8,128)S(1)}, f32[2,512]{1,0:T(2,128)S(1)}, f32[2,128]{1,0:T(2,128)S(1)}) custom-call(s32[1]{0:T(128)} %bitcast.place_ref, s32[128]{0:T(128)S(1)} %bitcast.8, s32[128]{0:T(128)S(1)} %bitcast.11, s32[1]{0:T(128)S(6)} %copy.10.count_ref, ...), custom_call_target="tpu_custom_call" | custom-call | tf_op jit(solution)/shard_map/first_step/pallas_call | solution.py:293
  29.9 2.0 %collective-permute-start.3 = (f32[40,128]{1,0:T(8,128)S(1)}, f32[40,128]{1,0:T(8,128)S(1)}, u32[]{:S(2)}, u32[]{:S(2)}) collective-permute-start(f32[40,128]{1,0:T(8,128)S(1)} %get-tuple-element.13), channel_id=1, source_target_pairs={{0,4},{4,0},{8,12},{12,8},{16,20},{20,16},{24,28},{28,24},{1,5},{5... | collective-permute-start | bytes 61448 | tf_op jit(solution)/shard_map/ppermute | solution.py:249
  31.9 1.9 %collective-permute-done.3 = f32[40,128]{1,0:T(8,128)S(1)} collective-permute-done((f32[40,128]{1,0:T(8,128)S(1)}, f32[40,128]{1,0:T(8,128)S(1)}, u32[]{:S(2)}, u32[]{:S(2)}) %collective-permute-start.3) | collective-permute-done | bytes 20512 | tf_op jit(solution)/shard_map/ppermute | solution.py:249
  33.7 2.0 %collective-permute-start.4 = (f32[40,128]{1,0:T(8,128)S(1)}, f32[40,128]{1,0:T(8,128)S(1)}, u32[]{:S(2)}, u32[]{:S(2)}) collective-permute-start(f32[40,128]{1,0:T(8,128)S(1)} %add.21), channel_id=1, source_target_pairs={{0,8},{4,12},{8,0},{12,4},{16,24},{20,28},{24,16},{28,20},{1,9},{5... | collective-permute-start | bytes 61448 | tf_op jit(solution)/shard_map/ppermute | solution.py:249
  35.7 1.8 %collective-permute-done.4 = f32[40,128]{1,0:T(8,128)S(1)} collective-permute-done((f32[40,128]{1,0:T(8,128)S(1)}, f32[40,128]{1,0:T(8,128)S(1)}, u32[]{:S(2)}, u32[]{:S(2)}) %collective-permute-start.4) | collective-permute-done | bytes 20512 | tf_op jit(solution)/shard_map/ppermute | solution.py:249
  37.5 3.0 %collective-permute-start.5 = (f32[40,128]{1,0:T(8,128)S(1)}, f32[40,128]{1,0:T(8,128)S(1)}, u32[]{:S(2)}, u32[]{:S(2)}) collective-permute-start(f32[40,128]{1,0:T(8,128)S(1)} %add.22), channel_id=1, source_target_pairs={{0,16},{4,20},{8,24},{12,28},{16,0},{20,4},{24,8},{28,12},{1,17},{... | collective-permute-start | bytes 61448 | tf_op jit(solution)/shard_map/ppermute | solution.py:249
  40.5 1.8 %collective-permute-done.5 = f32[40,128]{1,0:T(8,128)S(1)} collective-permute-done((f32[40,128]{1,0:T(8,128)S(1)}, f32[40,128]{1,0:T(8,128)S(1)}, u32[]{:S(2)}, u32[]{:S(2)}) %collective-permute-start.5) | collective-permute-done | bytes 20512 | tf_op jit(solution)/shard_map/ppermute | solution.py:249
  42.3 4.1 %second_step.1 = (f32[2,256]{1,0:T(2,128)}, f32[2,512]{1,0:T(2,128)}) custom-call(s32[1]{0:T(128)} %bitcast.place_ref, s32[128]{0:T(128)S(1)} %bitcast.9, s32[128]{0:T(128)S(1)} %bitcast.12, s32[1]{0:T(128)S(6)} %copy.10.count_ref, bf16[128,128,128]{2,1,0:T(8,128)(2,1)S(1)} %get-tuple-element.10.held_ref, f32[40,128]{1,0:T(8,128)S(1)} %add.23.got_ref, ...), custom_call_target="tpu_custom_call" | custom-call | tf_op jit(solution)/shard_map/second_step/pallas_call | solution.py:307
  (4 shorter events, 0.0 us)
Async XLA Ops:
  0.6 23.9 %copy-start.1 = (f32[512]{0:T(512)S(1)}, f32[512]{0:T(512)}, u32[]{:S(2)}) copy-start(f32[512]{0:T(512)} %param.13) | copy-start | bytes 6148
  1.3 0.7 %copy-start = (f32[2,512]{1,0:T(2,128)S(1)}, f32[2,512]{1,0:T(2,128)}, u32[]{:S(2)}) copy-start(f32[2,512]{1,0:T(2,128)} %y_ref.3) | copy-start | bytes 12292
  2.0 0.7 %copy-start.2 = (f32[2,256]{1,0:T(2,128)S(1)}, f32[2,256]{1,0:T(2,128)}, u32[]{:S(2)}) copy-start(f32[2,256]{1,0:T(2,128)} %cost_ref.3) | copy-start | bytes 6148
  2.7 0.7 %copy-start.3 = (s32[1,128]{1,0:T(1,128)S(1)}, s32[1,128]{1,0:T(1,128)}, u32[]{:S(2)}) copy-start(s32[1,128]{1,0:T(1,128)} %param.9) | copy-start | bytes 1540
  3.3 0.7 %copy-start.4 = (s32[1,128]{1,0:T(1,128)S(1)}, s32[1,128]{1,0:T(1,128)}, u32[]{:S(2)}) copy-start(s32[1,128]{1,0:T(1,128)} %param.10) | copy-start | bytes 1540
  4.0 0.7 %copy-start.5 = (f32[2,256]{1,0:T(2,128)S(1)}, f32[2,256]{1,0:T(2,128)}, u32[]{:S(2)}) copy-start(f32[2,256]{1,0:T(2,128)} %x_ref.1) | copy-start | bytes 6148
  10.0 5.0 %collective-permute-start = (f32[80,128]{1,0:T(8,128)S(1)}, f32[80,128]{1,0:T(8,128)S(1)}, u32[]{:S(2)}, u32[]{:S(2)}) collective-permute-start(f32[80,128]{1,0:T(8,128)S(1)} %get-tuple-element.11), channel_id=1, source_target_pairs={{0,4},{4,0},{8,12},{12,8},{16,20},{20,16},{24,28},{28,24},{1,5},{5... | collective-permute-start | bytes 122888 | tf_op jit(solution)/shard_map/ppermute | solution.py:249
  15.1 4.1 %collective-permute-start.1 = (f32[80,128]{1,0:T(8,128)S(1)}, f32[80,128]{1,0:T(8,128)S(1)}, u32[]{:S(2)}, u32[]{:S(2)}) collective-permute-start(f32[80,128]{1,0:T(8,128)S(1)} %add_select_fusion.2), channel_id=1, source_target_pairs={{0,8},{4,12},{8,0},{12,4},{16,24},{20,28},{24,16},{28,20},{1,9},{5... | collective-permute-start | bytes 122888 | tf_op jit(solution)/shard_map/ppermute | solution.py:249
  19.3 5.1 %collective-permute-start.2 = (f32[80,128]{1,0:T(8,128)S(1)}, f32[80,128]{1,0:T(8,128)S(1)}, u32[]{:S(2)}, u32[]{:S(2)}) collective-permute-start(f32[80,128]{1,0:T(8,128)S(1)} %add_select_fusion.1), channel_id=1, source_target_pairs={{0,16},{4,20},{8,24},{12,28},{16,0},{20,4},{24,8},{28,12},{1,17},{... | collective-permute-start | bytes 122888 | tf_op jit(solution)/shard_map/ppermute | solution.py:249
  29.9 3.8 %collective-permute-start.3 = (f32[40,128]{1,0:T(8,128)S(1)}, f32[40,128]{1,0:T(8,128)S(1)}, u32[]{:S(2)}, u32[]{:S(2)}) collective-permute-start(f32[40,128]{1,0:T(8,128)S(1)} %get-tuple-element.13), channel_id=1, source_target_pairs={{0,4},{4,0},{8,12},{12,8},{16,20},{20,16},{24,28},{28,24},{1,5},{5... | collective-permute-start | bytes 61448 | tf_op jit(solution)/shard_map/ppermute | solution.py:249
  33.7 3.8 %collective-permute-start.4 = (f32[40,128]{1,0:T(8,128)S(1)}, f32[40,128]{1,0:T(8,128)S(1)}, u32[]{:S(2)}, u32[]{:S(2)}) collective-permute-start(f32[40,128]{1,0:T(8,128)S(1)} %add.21), channel_id=1, source_target_pairs={{0,8},{4,12},{8,0},{12,4},{16,24},{20,28},{24,16},{28,20},{1,9},{5... | collective-permute-start | bytes 61448 | tf_op jit(solution)/shard_map/ppermute | solution.py:249
  37.5 4.8 %collective-permute-start.5 = (f32[40,128]{1,0:T(8,128)S(1)}, f32[40,128]{1,0:T(8,128)S(1)}, u32[]{:S(2)}, u32[]{:S(2)}) collective-permute-start(f32[40,128]{1,0:T(8,128)S(1)} %add.22), channel_id=1, source_target_pairs={{0,16},{4,20},{8,24},{12,28},{16,0},{20,4},{24,8},{28,12},{1,17},{... | collective-permute-start | bytes 61448 | tf_op jit(solution)/shard_map/ppermute | solution.py:249

commit v2 on v0

v2 whole, which is shorter than its diff:
```python
import functools

import jax
import jax.numpy as jnp
from jax import lax
from jax.experimental import pallas as pl
from jax.experimental.pallas import tpu as pltpu
from jax.sharding import PartitionSpec as P

ROWBLK = 4
COLBLK = 2
EDGE = 128
VECS = 4
TERMS = 2
KEPT = VECS * TERMS
LEFT = 16
FETCH = 16
GROUP = 32

step_size = 0.0625


def split(value):
    high = value.astype(jnp.bfloat16).astype(jnp.float32)
    return high, (value - high).astype(jnp.bfloat16).astype(jnp.float32)


def joined(rows):
    return rows[0:VECS] + rows[VECS : 2 * VECS]


def leads():
    return lax.axis_index("batch") % 2 == 1


def products(multiply, place, stage_ref, into_ref, ntile):
    stage_ref[1] = jnp.zeros(stage_ref.shape[1:], jnp.float32)

    def group(g, carry):
        now = g % 2
        for u in range(GROUP):
            stage_ref[now, u] = multiply(g * GROUP + u)[0:KEPT]
        for u in range(GROUP):
            into_ref[place(jnp.maximum((g - 1) * GROUP + u, 0))] += stage_ref[1 - now, u]
        return carry

    groups = ntile // GROUP
    lax.fori_loop(0, groups, group, 0)
    for u in range(GROUP):
        into_ref[place(ntile - GROUP + u)] += stage_ref[(groups - 1) % 2, u]


def put_left(left32_ref, left_ref, index, value):
    for s, term in enumerate(split(value)):
        left32_ref[index, VECS * s : VECS * (s + 1), :] = term
    left_ref[index] = left32_ref[index].astype(jnp.bfloat16)


def clear_left(left32_ref, left_ref):
    left32_ref[...] = jnp.zeros_like(left32_ref)
    left_ref[ROWBLK] = jnp.zeros((LEFT, EDGE), jnp.bfloat16)


def adjoint_start(sums_ref, costs, band):
    sums_ref[...] = jnp.zeros_like(sums_ref)
    for j in range(COLBLK):
        sums_ref[band * COLBLK + j, 0:VECS, :] = -costs[:, j * EDGE : (j + 1) * EDGE]


def adjoint_sum(sums_ref, v):
    blocks = sums_ref.shape[0]
    flat = sums_ref.reshape(blocks * KEPT, EDGE)
    return sum(flat[pl.ds(VECS * s + v, blocks, stride=KEPT), :] for s in range(TERMS))


def adjoint_pass(meta_ref, held_ref, left_ref, stage_ref, sums_ref):
    def multiply(t):
        return jnp.dot(left_ref[meta_ref[0, t]], held_ref[t], preferred_element_type=jnp.float32)

    products(multiply, lambda t: meta_ref[1, t], stage_ref, sums_ref, held_ref.shape[0])


def forward_left(right32_ref, v, value):
    blocks = right32_ref.shape[0]
    flat = right32_ref.reshape(blocks * LEFT, EDGE)
    for s, term in enumerate(split(value)):
        flat[pl.ds(VECS * s + v, blocks, stride=LEFT), :] = term


def forward_pass(meta_ref, turned_ref, right_ref, stage_ref, out_ref):
    def multiply(t):
        return jnp.dot(right_ref[meta_ref[1, t]], turned_ref[t], preferred_element_type=jnp.float32)

    out_ref[...] = jnp.zeros_like(out_ref)
    products(multiply, lambda t: meta_ref[0, t], stage_ref, out_ref, turned_ref.shape[0])


def scale_kernel(
    rows_ref, cols_ref, count_ref, tiles_ref, y_ref, x_ref, cost_ref,
    held_ref, meta_out_ref, spread_ref, rscale_ref, own_ref,
    sems, small_sems, rows_v_ref, rows_s_ref, count_s_ref, peak_ref,
):
    ntile = held_ref.shape[0]
    nrow, ncol = y_ref.shape[1], x_ref.shape[1]
    later = [
        pltpu.make_async_copy(y_ref, own_ref.at[:, 0:nrow], small_sems.at[4]),
        pltpu.make_async_copy(x_ref, own_ref.at[:, nrow : nrow + ncol], small_sems.at[5]),
        pltpu.make_async_copy(cost_ref, own_ref.at[:, nrow + ncol :], small_sems.at[6]),
    ]
    for copy in later:
        copy.start()

    def fetch(g):
        part = pl.ds(g * FETCH, FETCH)
        return pltpu.make_async_copy(tiles_ref.at[part], held_ref.at[part], sems.at[g])

    @pl.when(leads())
    def _():
        small = [
            pltpu.make_async_copy(rows_ref, rows_s_ref, small_sems.at[0]),
            pltpu.make_async_copy(rows_ref, rows_v_ref, small_sems.at[1]),
            pltpu.make_async_copy(cols_ref, meta_out_ref.at[1:2], small_sems.at[2]),
            pltpu.make_async_copy(count_ref, count_s_ref, small_sems.at[3]),
        ]
        for copy in small:
            copy.start()
        for g in range(ntile // FETCH):
            fetch(g).start()
        peak_ref[...] = jnp.zeros_like(peak_ref)
        spread_ref[ROWBLK] = jnp.zeros((EDGE, EDGE), jnp.float32)
        for copy in small:
            copy.wait()
        live = count_s_ref[0]
        index = lax.broadcasted_iota(jnp.int32, (1, ntile), 1)
        meta_out_ref[0:1, :] = jnp.where(index < live, rows_v_ref[...], ROWBLK)

        def row_peaks(g, carry):
            fetch(g).wait()
            for u in range(FETCH):
                t = g * FETCH + u
                r = jnp.where(t < live, rows_s_ref[0, t], ROWBLK)
                peak_ref[r] = jnp.maximum(peak_ref[r], jnp.abs(held_ref[t]))
            return carry

        lax.fori_loop(0, ntile // FETCH, row_peaks, 0)
        for r in range(ROWBLK):
            peak = jnp.max(peak_ref[r].astype(jnp.float32), axis=1, keepdims=True)
            spread = jnp.broadcast_to(lax.rsqrt(peak), (EDGE, EDGE))
            spread_ref[r] = spread
            rscale_ref[r : r + 1, :] = spread.T[0:1, :]

    for copy in later:
        copy.wait()


def columns_kernel(meta_ref, held_ref, spread_ref, top_out_ref, top_ref):
    @pl.when(leads())
    def _():
        top_ref[...] = jnp.zeros_like(top_ref)

        def group(g, carry):
            for u in range(FETCH):
                t = g * FETCH + u
                c = meta_ref[1, t]
                scaled = jnp.abs(held_ref[t]).astype(jnp.float32) * spread_ref[meta_ref[0, t]]
                peak = jnp.max(scaled.reshape(EDGE // 8, 8, EDGE), axis=0)
                top_ref[c] = jnp.maximum(top_ref[c], peak)
            return carry

        lax.fori_loop(0, held_ref.shape[0] // FETCH, group, 0)
        top_out_ref[...] = jnp.max(top_ref[...], axis=1)


def turn_kernel(held_ref, turned_ref):
    @pl.when(leads())
    def _():
        def group(g, carry):
            for u in range(FETCH):
                turned_ref[g * FETCH + u] = held_ref[g * FETCH + u].T
            return carry

        lax.fori_loop(0, held_ref.shape[0] // FETCH, group, 0)


def start_kernel(
    meta_ref, held_ref, rscale_ref, top_ref, mine_ref, other_ref,
    send_ref, both_ref,
    left32_ref, left_ref, stage_ref, sums_ref,
):
    blocks = sums_ref.shape[0]
    nrow = ROWBLK * EDGE
    ncol = COLBLK * EDGE

    @pl.when(leads())
    def _():
        both = jnp.concatenate([mine_ref[...], other_ref[...]], axis=0)
        both_ref[...] = both
        clear_left(left32_ref, left_ref)
        adjoint_start(sums_ref, both[:, nrow + ncol :], lax.axis_index("band"))
        for r in range(ROWBLK):
            put_left(
                left32_ref, left_ref, r, both[:, r * EDGE : (r + 1) * EDGE] * rscale_ref[r : r + 1, :]
            )
        send_ref[0:blocks, :] = top_ref[...]
        for j in range(COLBLK):
            at = (1 + VECS) * blocks + j * VECS
            send_ref[at : at + VECS, :] = both[:, nrow + j * EDGE : nrow + (j + 1) * EDGE]
        adjoint_pass(meta_ref, held_ref, left_ref, stage_ref, sums_ref)
        for v in range(VECS):
            send_ref[(1 + v) * blocks : (2 + v) * blocks, :] = adjoint_sum(sums_ref, v)


def combined(refs, blocks):
    peak = functools.reduce(jnp.maximum, [ref[0:blocks, :] for ref in refs])
    rows = slice(blocks, (1 + VECS) * blocks)
    return peak, functools.reduce(jnp.add, [ref[rows, :] for ref in refs])


def merge_kernel(blocks, *refs):
    refs, out_ref = refs[:-1], refs[-1]
    head = (1 + VECS) * blocks
    peak, total = combined(refs, blocks)
    out_ref[0:blocks, :] = peak
    out_ref[blocks:head, :] = total
    more = refs[0].shape[0] - head
    for i, ref in enumerate(refs):
        out_ref[head + i * more : head + (i + 1) * more, :] = ref[head:, :]


def step_kernel(
    offsets, parts, meta_ref, held_ref, turned_ref, *rest,
):
    got_refs = rest[:parts]
    (
        rscale_ref, both_ref, bound_ref,
        send_ref, x_one_ref, cscale_ref, y_one_ref, moved_ref,
        start_ref, right32_ref, right_ref, out_ref, left32_ref, left_ref, stage_ref, sums_ref,
    ) = rest[parts:]
    blocks = right_ref.shape[0]
    head = (1 + VECS) * blocks

    @pl.when(leads())
    def _():
        band = lax.axis_index("band")
        right32_ref[...] = jnp.zeros_like(right32_ref)
        clear_left(left32_ref, left_ref)
        adjoint_start(sums_ref, both_ref[:, (ROWBLK + COLBLK) * EDGE :], band)
        per = len(offsets) // parts
        for m, offset in enumerate(offsets):
            for j in range(COLBLK):
                at = head + (m % per) * COLBLK * VECS + j * VECS
                place = (band ^ offset) * COLBLK + j
                start_ref[place, 0:VECS, :] = got_refs[m // per][at : at + VECS, :]
        start = start_ref.reshape(blocks * 8, EDGE)

        peak, totals = combined(got_refs, blocks)
        cscale = lax.rsqrt(peak)
        cscale_ref[...] = cscale
        for v in range(VECS):
            before = start[pl.ds(v, blocks, stride=8), :]
            after = jnp.maximum(
                0.0, before + step_size * (cscale * totals[v * blocks : (v + 1) * blocks])
            )
            x_one_ref[v * blocks : (v + 1) * blocks, :] = after
            moved = jnp.sum(
                jnp.sum((after - before) ** 2, axis=0, keepdims=True), axis=1, keepdims=True
            )
            moved_ref[v : v + 1, :] = jnp.broadcast_to(moved, (1, EDGE))
            forward_left(right32_ref, v, cscale * (2.0 * after - before))
        right_ref[...] = right32_ref[...].astype(jnp.bfloat16)

        forward_pass(meta_ref, turned_ref, right_ref, stage_ref, out_ref)

        moved = jnp.zeros((VECS, EDGE), jnp.float32)
        for r in range(ROWBLK):
            span = slice(r * EDGE, (r + 1) * EDGE)
            scale = rscale_ref[r : r + 1, :]
            before = both_ref[:, span]
            after = jnp.maximum(
                0.0, before + step_size * (scale * (bound_ref[:, span] - joined(out_ref[r])))
            )
            y_one_ref[:, span] = after
            moved += (after - before) ** 2
            put_left(left32_ref, left_ref, r, after * scale)

        adjoint_pass(meta_ref, held_ref, left_ref, stage_ref, sums_ref)
        for v in range(VECS):
            send_ref[v * blocks : (v + 1) * blocks, :] = adjoint_sum(sums_ref, v)
        send_ref[VECS * blocks :, :] = jnp.zeros((8, EDGE), jnp.float32)
        send_ref[VECS * blocks : VECS * blocks + VECS, :] = moved


def last_kernel(parts, meta_ref, turned_ref, *rest):
    got_refs = rest[:parts]
    (
        rscale_ref, y_ref, bound_ref, x_one_ref, cscale_ref, moved_ref,
        mine_ref, other_ref,
        right32_ref, right_ref, out_ref, stage_ref,
    ) = rest[parts:]
    blocks = right_ref.shape[0]
    half = VECS // 2
    ncol = COLBLK * EDGE

    @pl.when(leads())
    def _():
        band = lax.axis_index("band")
        right32_ref[...] = jnp.zeros_like(right32_ref)
        cscale = cscale_ref[...]
        row = lax.broadcasted_iota(jnp.int32, (blocks, EDGE), 0)
        got = functools.reduce(jnp.add, [ref[...] for ref in got_refs])
        dual = jnp.sum(got[VECS * blocks : VECS * blocks + VECS], axis=1, keepdims=True)
        ratio = jnp.sqrt((dual + 1e-06) / (moved_ref[...] + 1e-06))
        for v in range(VECS):
            before = x_one_ref[v * blocks : (v + 1) * blocks, :]
            after = jnp.maximum(
                0.0,
                before
                + step_size / ratio[v : v + 1, :] * (cscale * got[v * blocks : (v + 1) * blocks]),
            )
            to_ref = mine_ref if v < half else other_ref
            for j in range(COLBLK):
                own = jnp.where(row == band * COLBLK + j, after, 0.0)
                to_ref[v % half : v % half + 1, j * EDGE : (j + 1) * EDGE] = jnp.sum(
                    own, axis=0, keepdims=True
                )
            forward_left(right32_ref, v, cscale * (2.0 * after - before))
        right_ref[...] = right32_ref[...].astype(jnp.bfloat16)

        forward_pass(meta_ref, turned_ref, right_ref, stage_ref, out_ref)

        for r in range(ROWBLK):
            span = slice(r * EDGE, (r + 1) * EDGE)
            scale = rscale_ref[r : r + 1, :]
            after = jnp.maximum(
                0.0,
                y_ref[:, span]
                + step_size * ratio * (scale * (bound_ref[:, span] - joined(out_ref[r]))),
            )
            place = slice(ncol + r * EDGE, ncol + (r + 1) * EDGE)
            mine_ref[:, place] = after[0:half]
            other_ref[:, place] = after[half:]


def finish_kernel(mine_ref, got_ref, x_ref, y_ref, sems):
    ncol = x_ref.shape[1]

    def give(from_ref):
        copies = [
            pltpu.make_async_copy(from_ref.at[:, 0:ncol], x_ref, sems.at[0]),
            pltpu.make_async_copy(from_ref.at[:, ncol:], y_ref, sems.at[1]),
        ]
        for copy in copies:
            copy.start()
        for copy in copies:
            copy.wait()

    pl.when(leads())(lambda: give(mine_ref))
    pl.when(jnp.logical_not(leads()))(lambda: give(got_ref))


def swap(value):
    count = lax.axis_size("batch")
    return lax.ppermute(value, "batch", [(i, i ^ 1) for i in range(count)])


def from_band(value, hop):
    bands, batches = lax.axis_size("band"), lax.axis_size("batch")
    pairs = []
    for band in range(bands):
        for batch in range(batches):
            if batch % 2 == 1:
                to = (band ^ hop) * batches + batch
            else:
                to = band * batches + (batch + 2) % batches if batches % 4 == 0 else (band ^ hop) * batches + batch
            pairs.append((band * batches + batch, to))
    return lax.ppermute(value, ("band", "batch"), pairs)


def rounds_of(bands):
    rounds, bit = [], 1
    while bit < bands:
        if bit * 2 < bands:
            rounds.append((bit, 2 * bit, 3 * bit))
        else:
            rounds.append((bit,))
        bit *= 4
    return rounds


def shards(tiles, tile_row, tile_col, tile_count, cost, bound_vec, x_start, y_start):
    tiles = tiles[0]
    ntile = tiles.shape[0]
    bands = lax.axis_size("band")
    blocks = bands * COLBLK
    bound = bound_vec.reshape(1, -1)
    nrow = bound.shape[1]
    f32 = lambda *shape: jax.ShapeDtypeStruct(shape, jnp.float32)
    v32 = lambda *shape: pltpu.VMEM(shape, jnp.float32)
    v16 = lambda *shape: pltpu.VMEM(shape, jnp.bfloat16)
    smem = [pl.BlockSpec(memory_space=pltpu.SMEM)]
    hbm = lambda n: [pl.BlockSpec(memory_space=pltpu.HBM)] * n
    vmem = lambda n: [pl.BlockSpec(memory_space=pltpu.VMEM)] * n
    left = [v32(ROWBLK + 1, LEFT, EDGE), v16(ROWBLK + 1, LEFT, EDGE)]
    right = [v32(blocks, LEFT, EDGE), v16(blocks, LEFT, EDGE)]
    rows_out = [v32(ROWBLK + 1, KEPT, EDGE)]
    sums = [v32(blocks, KEPT, EDGE)]
    stage = [v32(2, GROUP, KEPT, EDGE)]
    params = pltpu.CompilerParams(vmem_limit_bytes=32 * 1024 * 1024)
    in_hbm = lambda value: pltpu.with_memory_space_constraint(value, pltpu.HBM)

    held, meta, spread, rscale, mine = pl.pallas_call(
        scale_kernel,
        out_shape=(
            pltpu.VMEM(tiles.shape, jnp.bfloat16), pltpu.VMEM((2, ntile), jnp.int32),
            v32(ROWBLK + 1, EDGE, EDGE), v32(ROWBLK, EDGE),
            v32(y_start.shape[0], nrow + 2 * COLBLK * EDGE),
        ),
        in_specs=hbm(2) + [pl.BlockSpec(memory_space=pl.ANY)] + hbm(4),
        out_specs=tuple(vmem(5)),
        scratch_shapes=[
            pltpu.SemaphoreType.DMA((ntile // FETCH,)),
            pltpu.SemaphoreType.DMA((7,)),
            pltpu.VMEM((1, ntile), jnp.int32),
            pltpu.SMEM((1, ntile), jnp.int32),
            pltpu.SMEM((1,), jnp.int32),
            v16(ROWBLK + 1, EDGE, EDGE),
        ],
        compiler_params=params,
        name="row_scales",
    )(in_hbm(tile_row), in_hbm(tile_col), tile_count, *map(in_hbm, (tiles, y_start, x_start, cost)))

    other = swap(mine)

    top = pl.pallas_call(
        columns_kernel,
        out_shape=v32(blocks, EDGE),
        in_specs=smem + vmem(2),
        out_specs=vmem(1)[0],
        scratch_shapes=[v32(blocks, 8, EDGE)],
        compiler_params=params,
        cost_estimate=pl.CostEstimate(flops=0, bytes_accessed=tiles.nbytes, transcendentals=0),
        name="columns",
    )(meta, held, spread)

    turned = pl.pallas_call(
        turn_kernel,
        out_shape=v16(*tiles.shape),
        in_specs=vmem(1),
        out_specs=vmem(1)[0],
        compiler_params=params,
        cost_estimate=pl.CostEstimate(flops=0, bytes_accessed=tiles.nbytes, transcendentals=0),
        name="turn",
    )(held)

    message, both = pl.pallas_call(
        start_kernel,
        out_shape=(f32((1 + VECS) * blocks + COLBLK * VECS, EDGE), v32(VECS, mine.shape[1])),
        in_specs=smem + vmem(5),
        out_specs=tuple(vmem(2)),
        scratch_shapes=left + stage + sums,
        compiler_params=params,
        name="start",
    )(meta, held, rscale, top, mine, other)

    rounds = rounds_of(bands)
    offsets = [0]
    for index, hops in enumerate(rounds):
        messages = [message] + [from_band(message, hop) for hop in hops]
        offsets = [hop ^ offset for hop in (0, *hops) for offset in offsets]
        if index < len(rounds) - 1:
            message = pl.pallas_call(
                functools.partial(merge_kernel, blocks),
                out_shape=f32((1 + VECS) * blocks + COLBLK * VECS * len(offsets), EDGE),
                in_specs=vmem(len(messages)),
                out_specs=vmem(1)[0],
                compiler_params=params,
                name="merge",
            )(*messages)

    message, x_one, cscale, y_one, moved = pl.pallas_call(
        functools.partial(step_kernel, offsets, len(messages)),
        out_shape=(
            f32(VECS * blocks + 8, EDGE), v32(VECS * blocks, EDGE), v32(blocks, EDGE), v32(VECS, nrow), v32(VECS, EDGE),
        ),
        in_specs=smem + vmem(5 + len(messages)),
        out_specs=tuple(vmem(5)),
        scratch_shapes=[v32(blocks, 8, EDGE)] + right + rows_out + left + stage + sums,
        compiler_params=params,
        name="first_step",
    )(meta, held, turned, *messages, rscale, both, bound)

    for index, hops in enumerate(rounds):
        messages = [message] + [from_band(message, hop) for hop in hops]
        if index < len(rounds) - 1:
            message = functools.reduce(jnp.add, messages)

    half = VECS // 2
    width = COLBLK * EDGE + nrow
    mine, other = pl.pallas_call(
        functools.partial(last_kernel, len(messages)),
        out_shape=(v32(half, width), v32(half, width)),
        in_specs=smem + vmem(7 + len(messages)),
        out_specs=tuple(vmem(2)),
        scratch_shapes=right + rows_out + stage,
        compiler_params=params,
        name="second_step",
    )(meta, turned, *messages, rscale, y_one, bound, x_one, cscale, moved)

    return pl.pallas_call(
        finish_kernel,
        out_shape=(f32(*x_start.shape), f32(*y_start.shape)),
        in_specs=vmem(2),
        out_specs=tuple(hbm(2)),
        scratch_shapes=[pltpu.SemaphoreType.DMA((2,))],
        compiler_params=params,
        name="finish",
    )(mine, pltpu.with_memory_space_constraint(swap(other), pltpu.VMEM))


def solution(mesh):
    return jax.shard_map(
        shards,
        mesh=mesh,
        in_specs=(
            P("band", None, None, None),
            P("band", None),
            P("band", None),
            P("band"),
            P("batch", "band"),
            P("band"),
            P("batch", "band"),
            P("batch", "band"),
        ),
        out_specs=(P("batch", "band"), P("batch", "band")),
        check_vma=False,
    )
```

time: 185 us -> 36.6 us (0.20)
  blocking collectives: 38.8 us -> 0 us
  waiting for transfers between devices: 47.8 us -> 11 us
  matrix products: 29.6 us -> 0 us
  other arithmetic: 21.6 us -> 0.01 us
  between operations: 14.9 us -> 1.34 us
  local copies, waits for them, and re-layouts: 6.14 us -> 0.01 us
  starting transfers between devices: 25.6 us -> 20.3 us
  Pallas kernels: 0 us -> 3.74 us
    pmax x1 -> x0, waiting for transfers between devices: 31.6 us -> none  [shards(): col_send = lax.pmax(col_send, 'batch')]
    dot_general x12 -> x0, matrix products: 29.6 us -> none  [the longest x2 16.8 us: forward(): product = jnp.einsum('tij,tkj->tki', widened, picked, precision=high)]
    all_to_all x5 -> x0, starting transfers between devices: 25.6 us -> none  [the longest x2 9.37 us: adjoint(): lax.all_to_all(outgoing.reshape(band_count, capacity, columns, tile_edge)...]
    psum x1 -> x0, blocking collectives: 21.9 us -> none  [shards(): primal_step, dual_step = lax.psum((primal_step, dual_step), 'band')]
    ppermute x0 -> x10, starting transfers between devices: none -> 20.3 us  [the longest x8 11.3 us: from_band(): return lax.ppermute(value, ('band', 'batch'), pairs)]
    all_to_all x5 -> x0, waiting for transfers between devices: 16.2 us -> none  [the longest x1 8.12 us: forward(): lax.all_to_all(replies, 'band', split_axis=0, concat_axis=0, tiled=True)]
    ppermute x0 -> x10, waiting for transfers between devices: none -> 11 us  [the longest x8 9.96 us: from_band(): return lax.ppermute(value, ('band', 'batch'), pairs)]
    all_to_all x1 -> x0, blocking collectives: 10.6 us -> none  [forward(): lax.all_to_all(replies, 'band', split_axis=0, concat_axis=0, tiled=True)]
  transfers between devices with their start and end apart: 6 -> 10, of which waited for: 3 -> 9; matrix products, arithmetic and copies ran while one was open for 11% -> 0% of each run, Pallas kernels for 0% -> 2%
where the time goes in v2:
time: 36.6 us; the launch traced here: 36.4 us
  starting transfers between devices  20.3 us (55%)
  waiting for transfers between devices  11 us (30%)
  Pallas kernels  3.74 us (10%)
  between operations  1.34 us (4%)
    ppermute x8, starting transfers between devices, from_band(): return lax.ppermute(value, ('band', 'batch'), pairs)  11.3 us
    ppermute x8, waiting for transfers between devices, from_band(): return lax.ppermute(value, ('band', 'batch'), pairs)  9.96 us
    ppermute x2, starting transfers between devices, swap(): return lax.ppermute(value, 'batch', [(i, i ^ 1) for i in range(count)])  8.99 us
    ppermute x2, waiting for transfers between devices, swap(): return lax.ppermute(value, 'batch', [(i, i ^ 1) for i in range(count)])  1.08 us
    pallas_call x1, Pallas kernels, shards(): pl.pallas_call(scale_kernel, out_shape=(pltpu.VMEM(tiles.shape, jnp.bfloa...  0.85 us
  transfers between devices with their start and end apart: 10, of which 9 were waited for; matrix products, arithmetic and copies ran while one was open for 0% of the time, Pallas kernels for 2%

profile of v2, /device:TPU:0, one launch (start us, length us, event | category | flops | bytes accessed | tf_op | source)
XLA Modules:
  0.0 36.4 jit_solution(16918189539488794447)
XLA Ops:
  1.3 0.8 %row_scales.1 = (bf16[128,128,128]{2,1,0:T(8,128)(2,1)S(1)}, s32[2,128]{1,0:T(2,128)S(1)}, f32[5,128,128]{2,1,0:T(8,128)S(1)}, f32[4,128]{1,0:T(4,128)S(1)}, f32[2,1024]{1,0:T(2,128)S(1)}) custom-call(s32[1,128]{1,0:T(1,128)} %rows_ref.1, s32[1,128]{1,0:T(1,128)} %cols_ref.1, s32[1]{0:T(128)S(6)} %copy.10.count_ref, bf16[128,128,128]{2,1,0:T(8,128)(2,1)} %bitcast.4, ...), custom_call_target="tpu_custom_call" | custom-call | tf_op jit(solution)/shard_map/row_scales/pallas_call | solution.py:411
  2.1 3.0 %collective-permute-start = (f32[2,1024]{1,0:T(2,128)S(1)}, f32[2,1024]{1,0:T(2,128)S(1)}, u32[]{:S(2)}, u32[]{:S(2)}) collective-permute-start(f32[2,1024]{1,0:T(2,128)S(1)} %get-tuple-element.20.mine_ref), channel_id=1, source_target_pairs={{0,1},{1,0},{2,3},{3,2},{4,5},{5,4},{6,7},{7,6},{8,9},{9,8},{10,11... | collective-permute-start | bytes 24584 | tf_op jit(solution)/shard_map/ppermute | solution.py:363
  5.1 0.6 %columns.1.top_ref = f32[16,128]{1,0:T(8,128)S(1)} custom-call(s32[2,128]{1,0:T(2,128)S(1)} %get-tuple-element.16.meta_ref, bf16[128,128,128]{2,1,0:T(8,128)(2,1)S(1)} %get-tuple-element.17.held_ref, f32[5,128,128]{2,1,0:T(8,128)S(1)} %get-tuple-element.19.spread_ref), custom_call_target="tpu_custom_call" | custom-call | bytes 4194304 | tf_op jit(solution)/shard_map/columns/pallas_call | solution.py:434
  5.7 0.3 collective-permute-done.other_ref
  5.9 0.6 %start.1 = (f32[88,128]{1,0:T(8,128)S(1)}, f32[4,1024]{1,0:T(4,128)S(1)}) custom-call(s32[2,128]{1,0:T(2,128)S(1)} %get-tuple-element.16.meta_ref, bf16[128,128,128]{2,1,0:T(8,128)(2,1)S(1)} %get-tuple-element.17.held_ref, f32[4,128]{1,0:T(4,128)S(1)} %get-tuple-element.18.rscale_ref.rest_2_, f32[16,128]{1,0:T(8,128)S(1)} %columns.1.top_ref, ...), custom_call_target="tpu_custom_call" | custom-call | tf_op jit(solution)/shard_map/start/pallas_call | solution.py:455
  6.5 2.4 %collective-permute-start.3 = (f32[88,128]{1,0:T(8,128)S(1)}, f32[88,128]{1,0:T(8,128)S(1)}, u32[]{:S(2)}, u32[]{:S(2)}) collective-permute-start(f32[88,128]{1,0:T(8,128)S(1)} %get-tuple-element.21.refs_0_), channel_id=1, source_target_pairs={{0,2},{1,13},{2,0},{3,15},{4,6},{5,9},{6,4},{7,11},{8,10},{9,5},{1... | collective-permute-start | bytes 135176 | tf_op jit(solution)/shard_map/ppermute | solution.py:376
  8.9 0.1 collective-permute-start.2
  9.0 1.9 %collective-permute-start.1 = (f32[88,128]{1,0:T(8,128)S(1)}, f32[88,128]{1,0:T(8,128)S(1)}, u32[]{:S(2)}, u32[]{:S(2)}) collective-permute-start(f32[88,128]{1,0:T(8,128)S(1)} %get-tuple-element.21.refs_0_), channel_id=1, source_target_pairs={{0,2},{1,5},{2,0},{3,7},{4,6},{5,1},{6,4},{7,3},{8,10},{9,13},{10,... | collective-permute-start | bytes 135176 | tf_op jit(solution)/shard_map/ppermute | solution.py:376
  10.9 0.0 collective-permute-done.3.refs_3_
  10.9 2.0 %collective-permute-done.2.refs_2_ = f32[88,128]{1,0:T(8,128)S(1)} collective-permute-done((f32[88,128]{1,0:T(8,128)S(1)}, f32[88,128]{1,0:T(8,128)S(1)}, u32[]{:S(2)}, u32[]{:S(2)}) %collective-permute-start.2) | collective-permute-done | bytes 45088 | tf_op jit(solution)/shard_map/ppermute | solution.py:376
  12.9 0.5 %collective-permute-done.1.refs_1_ = f32[88,128]{1,0:T(8,128)S(1)} collective-permute-done((f32[88,128]{1,0:T(8,128)S(1)}, f32[88,128]{1,0:T(8,128)S(1)}, u32[]{:S(2)}, u32[]{:S(2)}) %collective-permute-start.1) | collective-permute-done | bytes 45088 | tf_op jit(solution)/shard_map/ppermute | solution.py:376
  13.4 0.0 copy-start
  13.4 1.6 %collective-permute-start.4 = (f32[112,128]{1,0:T(8,128)S(1)}, f32[112,128]{1,0:T(8,128)S(1)}, u32[]{:S(2)}, u32[]{:S(2)}) collective-permute-start(f32[112,128]{1,0:T(8,128)S(1)} %merge.1.rest_0_), channel_id=1, source_target_pairs={{0,2},{1,17},{2,0},{3,19},{4,6},{5,21},{6,4},{7,23},{8,10},{9,25},... | collective-permute-start | bytes 172040 | tf_op jit(solution)/shard_map/ppermute | solution.py:376
  15.0 2.6 %collective-permute-done.4.rest_1_ = f32[112,128]{1,0:T(8,128)S(1)} collective-permute-done((f32[112,128]{1,0:T(8,128)S(1)}, f32[112,128]{1,0:T(8,128)S(1)}, u32[]{:S(2)}, u32[]{:S(2)}) %collective-permute-start.4) | collective-permute-done | bytes 57376 | tf_op jit(solution)/shard_map/ppermute | solution.py:376
  17.7 0.0 copy-done
  17.7 0.6 %first_step.1 = (f32[72,128]{1,0:T(8,128)S(1)}, f32[64,128]{1,0:T(8,128)S(1)}, f32[16,128]{1,0:T(8,128)S(1)}, f32[4,512]{1,0:T(4,128)S(1)}, f32[4,128]{1,0:T(4,128)S(1)}) custom-call(s32[2,128]{1,0:T(2,128)S(1)} %get-tuple-element.16.meta_ref, bf16[128,128,128]{2,1,0:T(8,128)(2,1)S(1)} %get-tuple-element.17.held_ref, ...), custom_call_target="tpu_custom_call" | custom-call | tf_op jit(solution)/shard_map/first_step/pallas_call | solution.py:480
  18.3 1.6 %collective-permute-start.7 = (f32[72,128]{1,0:T(8,128)S(1)}, f32[72,128]{1,0:T(8,128)S(1)}, u32[]{:S(2)}, u32[]{:S(2)}) collective-permute-start(f32[72,128]{1,0:T(8,128)S(1)} %get-tuple-element.23), channel_id=1, source_target_pairs={{0,2},{1,13},{2,0},{3,15},{4,6},{5,9},{6,4},{7,11},{8,10},{9,5},{1... | collective-permute-start | bytes 110600 | tf_op jit(solution)/shard_map/ppermute | solution.py:376
  19.9 0.5 %collective-permute-start.6 = (f32[72,128]{1,0:T(8,128)S(1)}, f32[72,128]{1,0:T(8,128)S(1)}, u32[]{:S(2)}, u32[]{:S(2)}) collective-permute-start(f32[72,128]{1,0:T(8,128)S(1)} %get-tuple-element.23), channel_id=1, source_target_pairs={{0,2},{1,9},{2,0},{3,11},{4,6},{5,13},{6,4},{7,15},{8,10},{9,1},{1... | collective-permute-start | bytes 110600 | tf_op jit(solution)/shard_map/ppermute | solution.py:376
  20.3 1.5 %collective-permute-start.5 = (f32[72,128]{1,0:T(8,128)S(1)}, f32[72,128]{1,0:T(8,128)S(1)}, u32[]{:S(2)}, u32[]{:S(2)}) collective-permute-start(f32[72,128]{1,0:T(8,128)S(1)} %get-tuple-element.23), channel_id=1, source_target_pairs={{0,2},{1,5},{2,0},{3,7},{4,6},{5,1},{6,4},{7,3},{8,10},{9,13},{10,... | collective-permute-start | bytes 110600 | tf_op jit(solution)/shard_map/ppermute | solution.py:376
  21.9 0.4 %collective-permute-done.7 = f32[72,128]{1,0:T(8,128)S(1)} collective-permute-done((f32[72,128]{1,0:T(8,128)S(1)}, f32[72,128]{1,0:T(8,128)S(1)}, u32[]{:S(2)}, u32[]{:S(2)}) %collective-permute-start.7) | collective-permute-done | bytes 36896 | tf_op jit(solution)/shard_map/ppermute | solution.py:376
  22.3 1.5 %collective-permute-done.6 = f32[72,128]{1,0:T(8,128)S(1)} collective-permute-done((f32[72,128]{1,0:T(8,128)S(1)}, f32[72,128]{1,0:T(8,128)S(1)}, u32[]{:S(2)}, u32[]{:S(2)}) %collective-permute-start.6) | collective-permute-done | bytes 36896 | tf_op jit(solution)/shard_map/ppermute | solution.py:376
  23.8 0.5 %collective-permute-done.5 = f32[72,128]{1,0:T(8,128)S(1)} collective-permute-done((f32[72,128]{1,0:T(8,128)S(1)}, f32[72,128]{1,0:T(8,128)S(1)}, u32[]{:S(2)}, u32[]{:S(2)}) %collective-permute-start.5) | collective-permute-done | bytes 36896 | tf_op jit(solution)/shard_map/ppermute | solution.py:376
  24.3 1.6 %collective-permute-start.8 = (f32[72,128]{1,0:T(8,128)S(1)}, f32[72,128]{1,0:T(8,128)S(1)}, u32[]{:S(2)}, u32[]{:S(2)}) collective-permute-start(f32[72,128]{1,0:T(8,128)S(1)} %add_add_fusion.rest_0_), channel_id=1, source_target_pairs={{0,2},{1,17},{2,0},{3,19},{4,6},{5,21},{6,4},{7,23},{8,10},{9,25},... | collective-permute-start | bytes 110600 | tf_op jit(solution)/shard_map/ppermute | solution.py:376
  25.9 2.4 %collective-permute-done.8.rest_1_ = f32[72,128]{1,0:T(8,128)S(1)} collective-permute-done((f32[72,128]{1,0:T(8,128)S(1)}, f32[72,128]{1,0:T(8,128)S(1)}, u32[]{:S(2)}, u32[]{:S(2)}) %collective-permute-start.8) | collective-permute-done | bytes 36896 | tf_op jit(solution)/shard_map/ppermute | solution.py:376
  28.3 0.6 %second_step.1 = (f32[2,768]{1,0:T(2,128)S(1)}, f32[2,768]{1,0:T(2,128)S(1)}) custom-call(s32[2,128]{1,0:T(2,128)S(1)} %get-tuple-element.16.meta_ref, bf16[128,128,128]{2,1,0:T(8,128)(2,1)S(1)} %turn.1.turned_ref, f32[72,128]{1,0:T(8,128)S(1)} %add_add_fusion.rest_0_, f32[72,128]{1,0:T(8,128)S(1)} %collective-permute-done.8.rest_1_, ...), custom_call_target="tpu_custom_call" | custom-call | tf_op jit(solution)/shard_map/second_step/pallas_call | solution.py:499
  28.9 6.0 %collective-permute-start.9 = (f32[2,768]{1,0:T(2,128)S(1)}, f32[2,768]{1,0:T(2,128)S(1)}, u32[]{:S(2)}, u32[]{:S(2)}) collective-permute-start(f32[2,768]{1,0:T(2,128)S(1)} %get-tuple-element.29), channel_id=1, source_target_pairs={{0,1},{1,0},{2,3},{3,2},{4,5},{5,4},{6,7},{7,6},{8,9},{9,8},{10,11... | collective-permute-start | bytes 18440 | tf_op jit(solution)/shard_map/ppermute | solution.py:363
  35.0 0.8 %collective-permute-done.9.got_ref = f32[2,768]{1,0:T(2,128)S(1)} collective-permute-done((f32[2,768]{1,0:T(2,128)S(1)}, f32[2,768]{1,0:T(2,128)S(1)}, u32[]{:S(2)}, u32[]{:S(2)}) %collective-permute-start.9) | collective-permute-done | bytes 6176 | tf_op jit(solution)/shard_map/ppermute | solution.py:363
  35.8 0.6 %finish.1 = (f32[2,256]{1,0:T(2,128)}, f32[2,512]{1,0:T(2,128)}) custom-call(f32[2,768]{1,0:T(2,128)S(1)} %get-tuple-element.28.mine_ref, f32[2,768]{1,0:T(2,128)S(1)} %collective-permute-done.9.got_ref), custom_call_target="tpu_custom_call" | custom-call | tf_op jit(solution)/shard_map/finish/pallas_call | solution.py:509
  (3 shorter events, 0.0 us)
Async XLA Ops:
  2.1 3.8 %collective-permute-start = (f32[2,1024]{1,0:T(2,128)S(1)}, f32[2,1024]{1,0:T(2,128)S(1)}, u32[]{:S(2)}, u32[]{:S(2)}) collective-permute-start(f32[2,1024]{1,0:T(2,128)S(1)} %get-tuple-element.20.mine_ref), channel_id=1, source_target_pairs={{0,1},{1,0},{2,3},{3,2},{4,5},{5,4},{6,7},{7,6},{8,9},{9,8},{10,11... | collective-permute-start | bytes 24584 | tf_op jit(solution)/shard_map/ppermute | solution.py:363
  6.5 4.4 %collective-permute-start.3 = (f32[88,128]{1,0:T(8,128)S(1)}, f32[88,128]{1,0:T(8,128)S(1)}, u32[]{:S(2)}, u32[]{:S(2)}) collective-permute-start(f32[88,128]{1,0:T(8,128)S(1)} %get-tuple-element.21.refs_0_), channel_id=1, source_target_pairs={{0,2},{1,13},{2,0},{3,15},{4,6},{5,9},{6,4},{7,11},{8,10},{9,5},{1... | collective-permute-start | bytes 135176 | tf_op jit(solution)/shard_map/ppermute | solution.py:376
  8.9 4.0 %collective-permute-start.2 = (f32[88,128]{1,0:T(8,128)S(1)}, f32[88,128]{1,0:T(8,128)S(1)}, u32[]{:S(2)}, u32[]{:S(2)}) collective-permute-start(f32[88,128]{1,0:T(8,128)S(1)} %get-tuple-element.21.refs_0_), channel_id=1, source_target_pairs={{0,2},{1,9},{2,0},{3,11},{4,6},{5,13},{6,4},{7,15},{8,10},{9,1},{1... | collective-permute-start | bytes 135176 | tf_op jit(solution)/shard_map/ppermute | solution.py:376
  9.0 4.5 %collective-permute-start.1 = (f32[88,128]{1,0:T(8,128)S(1)}, f32[88,128]{1,0:T(8,128)S(1)}, u32[]{:S(2)}, u32[]{:S(2)}) collective-permute-start(f32[88,128]{1,0:T(8,128)S(1)} %get-tuple-element.21.refs_0_), channel_id=1, source_target_pairs={{0,2},{1,5},{2,0},{3,7},{4,6},{5,1},{6,4},{7,3},{8,10},{9,13},{10,... | collective-permute-start | bytes 135176 | tf_op jit(solution)/shard_map/ppermute | solution.py:376
  13.4 4.3 %copy-start = (f32[512]{0:T(512)S(1)}, f32[512]{0:T(512)}, u32[]{:S(2)}) copy-start(f32[512]{0:T(512)} %param.13) | copy-start | bytes 6148
  13.4 4.2 %collective-permute-start.4 = (f32[112,128]{1,0:T(8,128)S(1)}, f32[112,128]{1,0:T(8,128)S(1)}, u32[]{:S(2)}, u32[]{:S(2)}) collective-permute-start(f32[112,128]{1,0:T(8,128)S(1)} %merge.1.rest_0_), channel_id=1, source_target_pairs={{0,2},{1,17},{2,0},{3,19},{4,6},{5,21},{6,4},{7,23},{8,10},{9,25},... | collective-permute-start | bytes 172040 | tf_op jit(solution)/shard_map/ppermute | solution.py:376
  18.3 4.0 %collective-permute-start.7 = (f32[72,128]{1,0:T(8,128)S(1)}, f32[72,128]{1,0:T(8,128)S(1)}, u32[]{:S(2)}, u32[]{:S(2)}) collective-permute-start(f32[72,128]{1,0:T(8,128)S(1)} %get-tuple-element.23), channel_id=1, source_target_pairs={{0,2},{1,13},{2,0},{3,15},{4,6},{5,9},{6,4},{7,11},{8,10},{9,5},{1... | collective-permute-start | bytes 110600 | tf_op jit(solution)/shard_map/ppermute | solution.py:376
  19.9 4.0 %collective-permute-start.6 = (f32[72,128]{1,0:T(8,128)S(1)}, f32[72,128]{1,0:T(8,128)S(1)}, u32[]{:S(2)}, u32[]{:S(2)}) collective-permute-start(f32[72,128]{1,0:T(8,128)S(1)} %get-tuple-element.23), channel_id=1, source_target_pairs={{0,2},{1,9},{2,0},{3,11},{4,6},{5,13},{6,4},{7,15},{8,10},{9,1},{1... | collective-permute-start | bytes 110600 | tf_op jit(solution)/shard_map/ppermute | solution.py:376
  20.3 4.0 %collective-permute-start.5 = (f32[72,128]{1,0:T(8,128)S(1)}, f32[72,128]{1,0:T(8,128)S(1)}, u32[]{:S(2)}, u32[]{:S(2)}) collective-permute-start(f32[72,128]{1,0:T(8,128)S(1)} %get-tuple-element.23), channel_id=1, source_target_pairs={{0,2},{1,5},{2,0},{3,7},{4,6},{5,1},{6,4},{7,3},{8,10},{9,13},{10,... | collective-permute-start | bytes 110600 | tf_op jit(solution)/shard_map/ppermute | solution.py:376
  24.3 4.0 %collective-permute-start.8 = (f32[72,128]{1,0:T(8,128)S(1)}, f32[72,128]{1,0:T(8,128)S(1)}, u32[]{:S(2)}, u32[]{:S(2)}) collective-permute-start(f32[72,128]{1,0:T(8,128)S(1)} %add_add_fusion.rest_0_), channel_id=1, source_target_pairs={{0,2},{1,17},{2,0},{3,19},{4,6},{5,21},{6,4},{7,23},{8,10},{9,25},... | collective-permute-start | bytes 110600 | tf_op jit(solution)/shard_map/ppermute | solution.py:376
  28.9 6.9 %collective-permute-start.9 = (f32[2,768]{1,0:T(2,128)S(1)}, f32[2,768]{1,0:T(2,128)S(1)}, u32[]{:S(2)}, u32[]{:S(2)}) collective-permute-start(f32[2,768]{1,0:T(2,128)S(1)} %get-tuple-element.29), channel_id=1, source_target_pairs={{0,1},{1,0},{2,3},{3,2},{4,5},{5,4},{6,7},{7,6},{8,9},{9,8},{10,11... | collective-permute-start | bytes 18440 | tf_op jit(solution)/shard_map/ppermute | solution.py:363

commit v3 on v2

v3 whole, which is shorter than its diff:
```python
import functools

import jax
import jax.numpy as jnp
from jax import lax
from jax.experimental import pallas as pl
from jax.experimental.pallas import tpu as pltpu
from jax.sharding import PartitionSpec as P

ROWBLK = 4
COLBLK = 2
EDGE = 128
VECS = 4
TERMS = 2
KEPT = VECS * TERMS
FETCH = 16

step_size = 0.0625


def split(value):
    high = value.astype(jnp.bfloat16).astype(jnp.float32)
    return high, (value - high).astype(jnp.bfloat16).astype(jnp.float32)


def joined(rows):
    return rows[0:VECS] + rows[VECS : 2 * VECS]


def leads():
    return lax.axis_index("batch") % 2 == 1


def pair_blocks(ref, index, rows):
    count = ref.shape[0] // 2
    empty = jnp.zeros_like(rows)
    ref[index] = jnp.concatenate([rows, empty], axis=0).astype(jnp.bfloat16)
    ref[count + index] = jnp.concatenate([empty, rows], axis=0).astype(jnp.bfloat16)


def put_left(left_ref, index, value):
    pair_blocks(left_ref, index, jnp.concatenate(split(value), axis=0))


def clear_left(left_ref):
    pair_blocks(left_ref, ROWBLK, jnp.zeros((KEPT, EDGE), jnp.float32))


def adjoint_start(sums_refs, costs, band):
    for ref in sums_refs:
        ref[...] = jnp.zeros_like(ref)
    for j in range(COLBLK):
        sums_refs[0][band * COLBLK + j, 0:VECS, :] = -costs[:, j * EDGE : (j + 1) * EDGE]


def adjoint_sum(sums_refs, v):
    blocks = sums_refs[0].shape[0]
    total = 0.0
    for ref in sums_refs:
        flat = ref.reshape(blocks * KEPT, EDGE)
        for s in range(TERMS):
            total += flat[pl.ds(VECS * s + v, blocks, stride=KEPT), :]
    return total


def forward_left(right32_ref, v, value):
    blocks = right32_ref.shape[0]
    flat = right32_ref.reshape(blocks * KEPT, EDGE)
    for s, term in enumerate(split(value)):
        flat[pl.ds(VECS * s + v, blocks, stride=KEPT), :] = term


def tile_pass(meta_ref, tiles_refs, left_ref, of_row, into_refs, each=None):
    count = left_ref.shape[0] // 2
    first = 0
    for tiles_ref in tiles_refs:
        ntile = tiles_ref.shape[0]
        for t in range(0, ntile, 2):
            rows = [meta_ref[0, first + t], meta_ref[0, first + t + 1]]
            cols = [meta_ref[1, first + t], meta_ref[1, first + t + 1]]
            source, place = (rows, cols) if of_row else (cols, rows)
            left = jnp.concatenate([left_ref[source[0]], left_ref[count + source[1]]], axis=1)
            pair = tiles_ref[t : t + 2].reshape(2 * EDGE, EDGE)
            product = jnp.dot(left, pair, preferred_element_type=jnp.float32)
            for u in range(2):
                part = product[u * KEPT : (u + 1) * KEPT]
                into_refs[u][place[u]] += jnp.where(rows[u] < ROWBLK, part, 0.0)
                if each is not None:
                    each(tiles_ref[t + u], rows[u], cols[u], u)
        first += ntile


def fetch(tiles_ref, held_ref, sems, first, g):
    from_part, to_part = pl.ds(g * FETCH, FETCH), pl.ds((g - first) * FETCH, FETCH)
    return pltpu.make_async_copy(tiles_ref.at[from_part], held_ref.at[to_part], sems.at[g - first])


def row_peaks(row_at, held_ref, peak_refs, first, g):
    for u in range(FETCH):
        t = g * FETCH + u
        r = row_at(t)
        ref = peak_refs[u % 2]
        ref[r] = jnp.maximum(ref[r], jnp.abs(held_ref[t - first * FETCH]))


def pack_kernel(
    rows_ref, cols_ref, y_ref, x_ref, cost_ref, tiles_ref,
    meta_ref, own_ref, held_ref, even_ref, odd_ref,
    small_sems, sems, rows_s_ref,
):
    nrow, ncol = y_ref.shape[1], x_ref.shape[1]
    groups = held_ref.shape[0] // FETCH
    copies = [
        pltpu.make_async_copy(rows_ref, rows_s_ref, small_sems.at[0]),
        pltpu.make_async_copy(rows_ref, meta_ref.at[0:1], small_sems.at[1]),
        pltpu.make_async_copy(cols_ref, meta_ref.at[1:2], small_sems.at[2]),
        pltpu.make_async_copy(y_ref, own_ref.at[:, 0:nrow], small_sems.at[3]),
        pltpu.make_async_copy(x_ref, own_ref.at[:, nrow : nrow + ncol], small_sems.at[4]),
        pltpu.make_async_copy(cost_ref, own_ref.at[:, nrow + ncol :], small_sems.at[5]),
    ]
    for copy in copies:
        copy.start()

    @pl.when(leads())
    def _():
        for g in range(groups):
            fetch(tiles_ref, held_ref, sems, 0, g).start()
        for ref in (even_ref, odd_ref):
            ref[...] = jnp.zeros_like(ref)

    for copy in copies:
        copy.wait()

    @pl.when(leads())
    def _():
        def group(g, carry):
            fetch(tiles_ref, held_ref, sems, 0, g).wait()
            row_peaks(lambda t: rows_s_ref[0, t], held_ref, (even_ref, odd_ref), 0, g)
            return carry

        lax.fori_loop(0, groups, group, 0)


def scale_kernel(
    meta_ref, count_ref, even_in_ref, odd_in_ref, tiles_ref,
    meta_out_ref, held_ref, spread_ref, rscale_ref,
    meta_sem, sems, meta_s_ref, even_ref, odd_ref,
):
    groups = tiles_ref.shape[0] // FETCH
    first = groups - held_ref.shape[0] // FETCH

    @pl.when(leads())
    def _():
        for g in range(first, groups):
            fetch(tiles_ref, held_ref, sems, first, g).start()
        index = lax.broadcasted_iota(jnp.int32, (1, tiles_ref.shape[0]), 1)
        meta_out_ref[0:1, :] = jnp.where(index < count_ref[...], meta_ref[0:1, :], ROWBLK)
        meta_out_ref[1:2, :] = meta_ref[1:2, :]
        copy = pltpu.make_async_copy(meta_out_ref, meta_s_ref, meta_sem)
        copy.start()
        even_ref[...] = even_in_ref[...]
        odd_ref[...] = odd_in_ref[...]
        spread_ref[ROWBLK] = jnp.zeros((EDGE, EDGE), jnp.float32)
        copy.wait()

        def group(g, carry):
            fetch(tiles_ref, held_ref, sems, first, g).wait()
            row_peaks(lambda t: meta_s_ref[0, t], held_ref, (even_ref, odd_ref), first, g)
            return carry

        lax.fori_loop(first, groups, group, 0)
        for r in range(ROWBLK):
            peak = jnp.maximum(even_ref[r], odd_ref[r]).astype(jnp.float32)
            scale = lax.rsqrt(jnp.max(peak, axis=1, keepdims=True))
            spread_ref[r] = jnp.broadcast_to(scale, (EDGE, EDGE))
            rscale_ref[r : r + 1, :] = lax.rsqrt(jnp.max(peak.T, axis=0, keepdims=True))


def turn_kernel(one_ref, two_ref, turned_ref):
    @pl.when(leads())
    def _():
        first = 0
        for ref in (one_ref, two_ref):
            for t in range(ref.shape[0]):
                turned_ref[first + t] = ref[t].T
            first += ref.shape[0]


def start_kernel(
    meta_ref, one_ref, two_ref, spread_ref, rscale_ref, mine_ref, other_ref,
    send_ref, both_ref,
    left_ref, top_ref, top_two_ref, sums_ref, sums_two_ref,
):
    blocks = sums_ref.shape[0]
    sums_refs = (sums_ref, sums_two_ref)
    top_refs = (top_ref, top_two_ref)
    nrow = ROWBLK * EDGE
    ncol = COLBLK * EDGE

    @pl.when(leads())
    def _():
        both = jnp.concatenate([mine_ref[...], other_ref[...]], axis=0)
        both_ref[...] = both
        for ref in top_refs:
            ref[...] = jnp.zeros_like(ref)
        clear_left(left_ref)
        adjoint_start(sums_refs, both[:, nrow + ncol :], lax.axis_index("band"))
        for r in range(ROWBLK):
            put_left(left_ref, r, both[:, r * EDGE : (r + 1) * EDGE] * rscale_ref[r : r + 1, :])
        for j in range(COLBLK):
            at = (1 + VECS) * blocks + j * VECS
            send_ref[at : at + VECS, :] = both[:, nrow + j * EDGE : nrow + (j + 1) * EDGE]

        def column_peaks(tile, r, c, u):
            scaled = jnp.abs(tile).astype(jnp.float32) * spread_ref[r]
            peak = jnp.max(scaled.reshape(EDGE // 8, 8, EDGE), axis=0)
            top_refs[u][c] = jnp.maximum(top_refs[u][c], peak)

        tile_pass(meta_ref, (one_ref, two_ref), left_ref, True, sums_refs, column_peaks)
        send_ref[0:blocks, :] = jnp.max(jnp.maximum(top_ref[...], top_two_ref[...]), axis=1)
        for v in range(VECS):
            send_ref[(1 + v) * blocks : (2 + v) * blocks, :] = adjoint_sum(sums_refs, v)


def combined(refs, blocks):
    peak = functools.reduce(jnp.maximum, [ref[0:blocks, :] for ref in refs])
    rows = slice(blocks, (1 + VECS) * blocks)
    return peak, functools.reduce(jnp.add, [ref[rows, :] for ref in refs])


def merge_kernel(blocks, *refs):
    refs, out_ref = refs[:-1], refs[-1]
    head = (1 + VECS) * blocks
    peak, total = combined(refs, blocks)
    out_ref[0:blocks, :] = peak
    out_ref[blocks:head, :] = total
    more = refs[0].shape[0] - head
    for i, ref in enumerate(refs):
        out_ref[head + i * more : head + (i + 1) * more, :] = ref[head:, :]


def step_kernel(
    offsets, parts, meta_ref, one_ref, two_ref, turned_ref, *rest,
):
    got_refs = rest[:parts]
    (
        rscale_ref, both_ref, bound_ref,
        send_ref, x_one_ref, cscale_ref, y_one_ref, moved_ref,
        start_ref, right32_ref, right_ref, out_ref, out_two_ref, left_ref, sums_ref, sums_two_ref,
    ) = rest[parts:]
    blocks = right32_ref.shape[0]
    head = (1 + VECS) * blocks
    sums_refs = (sums_ref, sums_two_ref)

    @pl.when(leads())
    def _():
        band = lax.axis_index("band")
        clear_left(left_ref)
        adjoint_start(sums_refs, both_ref[:, (ROWBLK + COLBLK) * EDGE :], band)
        per = len(offsets) // parts
        for m, offset in enumerate(offsets):
            for j in range(COLBLK):
                at = head + (m % per) * COLBLK * VECS + j * VECS
                place = (band ^ offset) * COLBLK + j
                start_ref[place, 0:VECS, :] = got_refs[m // per][at : at + VECS, :]
        start = start_ref.reshape(blocks * 8, EDGE)

        peak, totals = combined(got_refs, blocks)
        cscale = lax.rsqrt(peak)
        cscale_ref[...] = cscale
        for v in range(VECS):
            before = start[pl.ds(v, blocks, stride=8), :]
            after = jnp.maximum(
                0.0, before + step_size * (cscale * totals[v * blocks : (v + 1) * blocks])
            )
            x_one_ref[v * blocks : (v + 1) * blocks, :] = after
            moved = jnp.sum(
                jnp.sum((after - before) ** 2, axis=0, keepdims=True), axis=1, keepdims=True
            )
            moved_ref[v : v + 1, :] = jnp.broadcast_to(moved, (1, EDGE))
            forward_left(right32_ref, v, cscale * (2.0 * after - before))
        for c in range(blocks):
            pair_blocks(right_ref, c, right32_ref[c])

        for ref in (out_ref, out_two_ref):
            ref[...] = jnp.zeros_like(ref)
        tile_pass(meta_ref, (turned_ref,), right_ref, False, (out_ref, out_two_ref))

        moved = jnp.zeros((VECS, EDGE), jnp.float32)
        for r in range(ROWBLK):
            span = slice(r * EDGE, (r + 1) * EDGE)
            scale = rscale_ref[r : r + 1, :]
            before = both_ref[:, span]
            after = jnp.maximum(
                0.0, before + step_size * (scale * (bound_ref[:, span] - joined(out_ref[r] + out_two_ref[r])))
            )
            y_one_ref[:, span] = after
            moved += (after - before) ** 2
            put_left(left_ref, r, after * scale)

        tile_pass(meta_ref, (one_ref, two_ref), left_ref, True, sums_refs)
        for v in range(VECS):
            send_ref[v * blocks : (v + 1) * blocks, :] = adjoint_sum(sums_refs, v)
        send_ref[VECS * blocks :, :] = jnp.zeros((8, EDGE), jnp.float32)
        send_ref[VECS * blocks : VECS * blocks + VECS, :] = moved


def last_kernel(parts, meta_ref, turned_ref, *rest):
    got_refs = rest[:parts]
    (
        rscale_ref, y_ref, bound_ref, x_one_ref, cscale_ref, moved_ref,
        mine_ref, other_ref,
        right32_ref, right_ref, out_ref, out_two_ref,
    ) = rest[parts:]
    blocks = right32_ref.shape[0]
    half = VECS // 2
    ncol = COLBLK * EDGE

    @pl.when(leads())
    def _():
        band = lax.axis_index("band")
        cscale = cscale_ref[...]
        row = lax.broadcasted_iota(jnp.int32, (blocks, EDGE), 0)
        got = functools.reduce(jnp.add, [ref[...] for ref in got_refs])
        dual = jnp.sum(got[VECS * blocks : VECS * blocks + VECS], axis=1, keepdims=True)
        ratio = jnp.sqrt((dual + 1e-06) / (moved_ref[...] + 1e-06))
        for v in range(VECS):
            before = x_one_ref[v * blocks : (v + 1) * blocks, :]
            after = jnp.maximum(
                0.0,
                before
                + step_size / ratio[v : v + 1, :] * (cscale * got[v * blocks : (v + 1) * blocks]),
            )
            to_ref = mine_ref if v < half else other_ref
            for j in range(COLBLK):
                own = jnp.where(row == band * COLBLK + j, after, 0.0)
                to_ref[v % half : v % half + 1, j * EDGE : (j + 1) * EDGE] = jnp.sum(
                    own, axis=0, keepdims=True
                )
            forward_left(right32_ref, v, cscale * (2.0 * after - before))
        for c in range(blocks):
            pair_blocks(right_ref, c, right32_ref[c])

        for ref in (out_ref, out_two_ref):
            ref[...] = jnp.zeros_like(ref)
        tile_pass(meta_ref, (turned_ref,), right_ref, False, (out_ref, out_two_ref))

        for r in range(ROWBLK):
            span = slice(r * EDGE, (r + 1) * EDGE)
            scale = rscale_ref[r : r + 1, :]
            after = jnp.maximum(
                0.0,
                y_ref[:, span]
                + step_size * ratio * (scale * (bound_ref[:, span] - joined(out_ref[r] + out_two_ref[r]))),
            )
            place = slice(ncol + r * EDGE, ncol + (r + 1) * EDGE)
            mine_ref[:, place] = after[0:half]
            other_ref[:, place] = after[half:]


def finish_kernel(mine_ref, got_ref, x_ref, y_ref, sems):
    ncol = x_ref.shape[1]

    def give(from_ref):
        copies = [
            pltpu.make_async_copy(from_ref.at[:, 0:ncol], x_ref, sems.at[0]),
            pltpu.make_async_copy(from_ref.at[:, ncol:], y_ref, sems.at[1]),
        ]
        for copy in copies:
            copy.start()
        for copy in copies:
            copy.wait()

    pl.when(leads())(lambda: give(mine_ref))
    pl.when(jnp.logical_not(leads()))(lambda: give(got_ref))


def swap(value):
    count = lax.axis_size("batch")
    return lax.ppermute(value, "batch", [(i, i ^ 1) for i in range(count)])


def from_band(value, hop):
    bands, batches = lax.axis_size("band"), lax.axis_size("batch")
    pairs = []
    for band in range(bands):
        for batch in range(batches):
            if batch % 2 == 1:
                to = (band ^ hop) * batches + batch
            else:
                to = band * batches + (batch + 2) % batches if batches % 4 == 0 else (band ^ hop) * batches + batch
            pairs.append((band * batches + batch, to))
    return lax.ppermute(value, ("band", "batch"), pairs)


def rounds_of(bands):
    rounds, bit = [], 1
    while bit < bands:
        if bit * 2 < bands:
            rounds.append((bit, 2 * bit, 3 * bit))
        else:
            rounds.append((bit,))
        bit *= 4
    return rounds


def shards(tiles, tile_row, tile_col, tile_count, cost, bound_vec, x_start, y_start):
    tiles = tiles[0]
    ntile = tiles.shape[0]
    bands = lax.axis_size("band")
    blocks = bands * COLBLK
    bound = bound_vec.reshape(1, -1)
    nrow = bound.shape[1]
    f32 = lambda *shape: jax.ShapeDtypeStruct(shape, jnp.float32)
    v32 = lambda *shape: pltpu.VMEM(shape, jnp.float32)
    v16 = lambda *shape: pltpu.VMEM(shape, jnp.bfloat16)
    smem = [pl.BlockSpec(memory_space=pltpu.SMEM)]
    hbm = lambda n: [pl.BlockSpec(memory_space=pltpu.HBM)] * n
    vmem = lambda n: [pl.BlockSpec(memory_space=pltpu.VMEM)] * n
    left = [v16(2 * (ROWBLK + 1), 2 * KEPT, EDGE)]
    right = [v32(blocks, KEPT, EDGE), v16(2 * blocks, 2 * KEPT, EDGE)]
    rows_out = [v32(ROWBLK + 1, KEPT, EDGE)] * 2
    sums = [v32(blocks, KEPT, EDGE)] * 2
    params = pltpu.CompilerParams(vmem_limit_bytes=32 * 1024 * 1024)
    in_hbm = lambda value: pltpu.with_memory_space_constraint(value, pltpu.HBM)

    early = ntile * 3 // 8
    small = (tile_row, tile_col, y_start, x_start, cost)
    peaks = [v16(ROWBLK + 1, EDGE, EDGE)] * 2
    tiles = in_hbm(tiles)
    meta, mine, one, *tops = pl.pallas_call(
        pack_kernel,
        out_shape=(
            pltpu.VMEM((2, ntile), jnp.int32), v32(VECS // 2, nrow + 2 * COLBLK * EDGE), v16(early, EDGE, EDGE), *peaks,
        ),
        in_specs=hbm(6),
        out_specs=tuple(vmem(5)),
        scratch_shapes=[
            pltpu.SemaphoreType.DMA((6,)),
            pltpu.SemaphoreType.DMA((early // FETCH,)),
            pltpu.SMEM((1, ntile), jnp.int32),
        ],
        compiler_params=params,
        name="pack",
    )(*map(in_hbm, small), tiles)
    other = swap(mine)

    late = ntile - early
    meta, two, spread, rscale = pl.pallas_call(
        scale_kernel,
        out_shape=(
            pltpu.VMEM((2, ntile), jnp.int32), v16(late, EDGE, EDGE), v32(ROWBLK + 1, EDGE, EDGE), v32(ROWBLK, EDGE),
        ),
        in_specs=vmem(4) + hbm(1),
        out_specs=tuple(vmem(4)),
        scratch_shapes=[
            pltpu.SemaphoreType.DMA,
            pltpu.SemaphoreType.DMA((late // FETCH,)),
            pltpu.SMEM((2, ntile), jnp.int32),
            *peaks,
        ],
        compiler_params=params,
        cost_estimate=pl.CostEstimate(flops=0, bytes_accessed=tiles.nbytes, transcendentals=0),
        name="row_scales",
    )(meta, tile_count.reshape(1, 1), *tops, tiles)

    turned = pl.pallas_call(
        turn_kernel,
        out_shape=v16(*tiles.shape),
        in_specs=vmem(2),
        out_specs=vmem(1)[0],
        compiler_params=params,
        cost_estimate=pl.CostEstimate(flops=0, bytes_accessed=tiles.nbytes, transcendentals=0),
        name="turn",
    )(one, two)

    message, both = pl.pallas_call(
        start_kernel,
        out_shape=(f32((1 + VECS) * blocks + COLBLK * VECS, EDGE), v32(VECS, mine.shape[1])),
        in_specs=smem + vmem(6),
        out_specs=tuple(vmem(2)),
        scratch_shapes=left + [v32(blocks, 8, EDGE)] * 2 + sums,
        compiler_params=params,
        name="start",
    )(meta, one, two, spread, rscale, mine, other)

    rounds = rounds_of(bands)
    offsets = [0]
    for index, hops in enumerate(rounds):
        messages = [message] + [from_band(message, hop) for hop in hops]
        offsets = [hop ^ offset for hop in (0, *hops) for offset in offsets]
        if index < len(rounds) - 1:
            message = pl.pallas_call(
                functools.partial(merge_kernel, blocks),
                out_shape=f32((1 + VECS) * blocks + COLBLK * VECS * len(offsets), EDGE),
                in_specs=vmem(len(messages)),
                out_specs=vmem(1)[0],
                compiler_params=params,
                name="merge",
            )(*messages)

    message, x_one, cscale, y_one, moved = pl.pallas_call(
        functools.partial(step_kernel, offsets, len(messages)),
        out_shape=(
            f32(VECS * blocks + 8, EDGE), v32(VECS * blocks, EDGE), v32(blocks, EDGE), v32(VECS, nrow), v32(VECS, EDGE),
        ),
        in_specs=smem + vmem(6 + len(messages)),
        out_specs=tuple(vmem(5)),
        scratch_shapes=[v32(blocks, 8, EDGE)] + right + rows_out + left + sums,
        compiler_params=params,
        name="first_step",
    )(meta, one, two, turned, *messages, rscale, both, bound)

    for index, hops in enumerate(rounds):
        messages = [message] + [from_band(message, hop) for hop in hops]
        if index < len(rounds) - 1:
            message = functools.reduce(jnp.add, messages)

    half = VECS // 2
    width = COLBLK * EDGE + nrow
    mine, other = pl.pallas_call(
        functools.partial(last_kernel, len(messages)),
        out_shape=(v32(half, width), v32(half, width)),
        in_specs=smem + vmem(7 + len(messages)),
        out_specs=tuple(vmem(2)),
        scratch_shapes=right + rows_out,
        compiler_params=params,
        name="second_step",
    )(meta, turned, *messages, rscale, y_one, bound, x_one, cscale, moved)

    return pl.pallas_call(
        finish_kernel,
        out_shape=(f32(*x_start.shape), f32(*y_start.shape)),
        in_specs=vmem(2),
        out_specs=tuple(hbm(2)),
        scratch_shapes=[pltpu.SemaphoreType.DMA((2,))],
        compiler_params=params,
        name="finish",
    )(mine, pltpu.with_memory_space_constraint(swap(other), pltpu.VMEM))


def solution(mesh):
    return jax.shard_map(
        shards,
        mesh=mesh,
        in_specs=(
            P("band", None, None, None),
            P("band", None),
            P("band", None),
            P("band"),
            P("batch", "band"),
            P("band"),
            P("batch", "band"),
            P("batch", "band"),
        ),
        out_specs=(P("batch", "band"), P("batch", "band")),
        check_vma=False,
    )
```

time: 36.6 us -> 32.1 us (0.88)
  starting transfers between devices: 20.3 us -> 16.4 us
  Pallas kernels: 3.74 us -> 3.22 us
    ppermute x2, starting transfers between devices: 8.99 us -> 5.17 us  [swap(): return lax.ppermute(value, 'batch', [(i, i ^ 1) for i in range(count)])]
    pallas_call x3, Pallas kernels: 1.41 us -> 0.9 us  [the longest x1 0.83 us: shards(): pl.pallas_call(pack_kernel, out_shape=(pltpu.VMEM((2, ntile), jnp.int32),...]
  transfers between devices with their start and end apart: 10 -> 10, of which waited for: 9 -> 9; matrix products, arithmetic and copies ran while one was open for 0% -> 0% of each run, Pallas kernels for 2% -> 0%
where the time goes in v3:
time: 32.1 us; the launch traced here: 31.9 us
  starting transfers between devices  16.4 us (51%)
  waiting for transfers between devices  10.9 us (34%)
  Pallas kernels  3.22 us (10%)
  between operations  1.34 us (4%)
    ppermute x8, starting transfers between devices, from_band(): return lax.ppermute(value, ('band', 'batch'), pairs)  11.3 us
    ppermute x8, waiting for transfers between devices, from_band(): return lax.ppermute(value, ('band', 'batch'), pairs)  9.96 us
    ppermute x2, starting transfers between devices, swap(): return lax.ppermute(value, 'batch', [(i, i ^ 1) for i in range(count)])  5.17 us
    ppermute x2, waiting for transfers between devices, swap(): return lax.ppermute(value, 'batch', [(i, i ^ 1) for i in range(count)])  0.92 us
    pallas_call x1, Pallas kernels, shards(): pl.pallas_call(pack_kernel, out_shape=(pltpu.VMEM((2, ntile), jnp.int32),...  0.83 us
  transfers between devices with their start and end apart: 10, of which 9 were waited for; matrix products, arithmetic and copies ran while one was open for 0% of the time, Pallas kernels for 0%

profile of v3, /device:TPU:0, one launch (start us, length us, event | category | flops | bytes accessed | tf_op | source)
XLA Modules:
  0.0 31.9 jit_solution(3206168731210904062)
XLA Ops:
  0.6 0.8 %pack.1 = (s32[2,128]{1,0:T(2,128)S(1)}, f32[2,1024]{1,0:T(2,128)S(1)}, bf16[48,128,128]{2,1,0:T(8,128)(2,1)S(1)}, bf16[5,128,128]{2,1,0:T(8,128)(2,1)S(1)}, bf16[5,128,128]{2,1,0:T(8,128)(2,1)S(1)}) custom-call(s32[1,128]{1,0:T(1,128)} %rows_ref.1, s32[1,128]{1,0:T(1,128)} %cols_ref.1, f32[2,512]{1,0:T(2,128)} %y_ref.1, f32[2,256]{1,0:T(2,128)} %x_ref.1, ...), custom_call_target="tpu_custom_call" | custom-call | tf_op jit(solution)/shard_map/pack/pallas_call | solution.py:431
  1.5 1.4 %collective-permute-start = (f32[2,1024]{1,0:T(2,128)S(1)}, f32[2,1024]{1,0:T(2,128)S(1)}, u32[]{:S(2)}, u32[]{:S(2)}) collective-permute-start(f32[2,1024]{1,0:T(2,128)S(1)} %get-tuple-element.28.mine_ref), channel_id=1, source_target_pairs={{0,1},{1,0},{2,3},{3,2},{4,5},{5,4},{6,7},{7,6},{8,9},{9,8},{10,11... | collective-permute-start | bytes 24584 | tf_op jit(solution)/shard_map/ppermute | solution.py:380
  3.5 0.1 row_scales.1
  3.6 0.1 collective-permute-done.other_ref
  3.7 0.6 %start.1 = (f32[88,128]{1,0:T(8,128)S(1)}, f32[4,1024]{1,0:T(4,128)S(1)}) custom-call(s32[2,128]{1,0:T(2,128)S(1)} %get-tuple-element.23.meta_ref, bf16[48,128,128]{2,1,0:T(8,128)(2,1)S(1)} %get-tuple-element.24.one_ref, bf16[80,128,128]{2,1,0:T(8,128)(2,1)S(1)} %get-tuple-element.25.two_ref, f32[5,128,128]{2,1,0:T(8,128)S(1)} %get-tuple-element.26.spread_ref, ...), custom_call_target="tpu_custom_call" | custom-call | tf_op jit(solution)/shard_map/start/pallas_call | solution.py:477
  4.3 2.4 %collective-permute-start.3 = (f32[88,128]{1,0:T(8,128)S(1)}, f32[88,128]{1,0:T(8,128)S(1)}, u32[]{:S(2)}, u32[]{:S(2)}) collective-permute-start(f32[88,128]{1,0:T(8,128)S(1)} %get-tuple-element.29.refs_0_), channel_id=1, source_target_pairs={{0,2},{1,13},{2,0},{3,15},{4,6},{5,9},{6,4},{7,11},{8,10},{9,5},{1... | collective-permute-start | bytes 135176 | tf_op jit(solution)/shard_map/ppermute | solution.py:393
  6.7 0.1 collective-permute-start.2
  6.7 1.9 %collective-permute-start.1 = (f32[88,128]{1,0:T(8,128)S(1)}, f32[88,128]{1,0:T(8,128)S(1)}, u32[]{:S(2)}, u32[]{:S(2)}) collective-permute-start(f32[88,128]{1,0:T(8,128)S(1)} %get-tuple-element.29.refs_0_), channel_id=1, source_target_pairs={{0,2},{1,5},{2,0},{3,7},{4,6},{5,1},{6,4},{7,3},{8,10},{9,13},{10,... | collective-permute-start | bytes 135176 | tf_op jit(solution)/shard_map/ppermute | solution.py:393
  8.7 0.0 collective-permute-done.3.refs_3_
  8.7 2.0 %collective-permute-done.2.refs_2_ = f32[88,128]{1,0:T(8,128)S(1)} collective-permute-done((f32[88,128]{1,0:T(8,128)S(1)}, f32[88,128]{1,0:T(8,128)S(1)}, u32[]{:S(2)}, u32[]{:S(2)}) %collective-permute-start.2) | collective-permute-done | bytes 45088 | tf_op jit(solution)/shard_map/ppermute | solution.py:393
  10.7 0.5 %collective-permute-done.1.refs_1_ = f32[88,128]{1,0:T(8,128)S(1)} collective-permute-done((f32[88,128]{1,0:T(8,128)S(1)}, f32[88,128]{1,0:T(8,128)S(1)}, u32[]{:S(2)}, u32[]{:S(2)}) %collective-permute-start.1) | collective-permute-done | bytes 45088 | tf_op jit(solution)/shard_map/ppermute | solution.py:393
  11.2 0.0 copy-start
  11.2 1.6 %collective-permute-start.4 = (f32[112,128]{1,0:T(8,128)S(1)}, f32[112,128]{1,0:T(8,128)S(1)}, u32[]{:S(2)}, u32[]{:S(2)}) collective-permute-start(f32[112,128]{1,0:T(8,128)S(1)} %merge.1.rest_0_), channel_id=1, source_target_pairs={{0,2},{1,17},{2,0},{3,19},{4,6},{5,21},{6,4},{7,23},{8,10},{9,25},... | collective-permute-start | bytes 172040 | tf_op jit(solution)/shard_map/ppermute | solution.py:393
  12.8 2.6 %collective-permute-done.4.rest_1_ = f32[112,128]{1,0:T(8,128)S(1)} collective-permute-done((f32[112,128]{1,0:T(8,128)S(1)}, f32[112,128]{1,0:T(8,128)S(1)}, u32[]{:S(2)}, u32[]{:S(2)}) %collective-permute-start.4) | collective-permute-done | bytes 57376 | tf_op jit(solution)/shard_map/ppermute | solution.py:393
  15.5 0.0 copy-done
  15.5 0.6 %first_step.1 = (f32[72,128]{1,0:T(8,128)S(1)}, f32[64,128]{1,0:T(8,128)S(1)}, f32[16,128]{1,0:T(8,128)S(1)}, f32[4,512]{1,0:T(4,128)S(1)}, f32[4,128]{1,0:T(4,128)S(1)}) custom-call(s32[2,128]{1,0:T(2,128)S(1)} %get-tuple-element.23.meta_ref, bf16[48,128,128]{2,1,0:T(8,128)(2,1)S(1)} %get-tuple-element.24.one_ref, ...), custom_call_target="tpu_custom_call" | custom-call | tf_op jit(solution)/shard_map/first_step/pallas_call | solution.py:502
  16.0 1.6 %collective-permute-start.7 = (f32[72,128]{1,0:T(8,128)S(1)}, f32[72,128]{1,0:T(8,128)S(1)}, u32[]{:S(2)}, u32[]{:S(2)}) collective-permute-start(f32[72,128]{1,0:T(8,128)S(1)} %get-tuple-element.31), channel_id=1, source_target_pairs={{0,2},{1,13},{2,0},{3,15},{4,6},{5,9},{6,4},{7,11},{8,10},{9,5},{1... | collective-permute-start | bytes 110600 | tf_op jit(solution)/shard_map/ppermute | solution.py:393
  17.6 0.5 %collective-permute-start.6 = (f32[72,128]{1,0:T(8,128)S(1)}, f32[72,128]{1,0:T(8,128)S(1)}, u32[]{:S(2)}, u32[]{:S(2)}) collective-permute-start(f32[72,128]{1,0:T(8,128)S(1)} %get-tuple-element.31), channel_id=1, source_target_pairs={{0,2},{1,9},{2,0},{3,11},{4,6},{5,13},{6,4},{7,15},{8,10},{9,1},{1... | collective-permute-start | bytes 110600 | tf_op jit(solution)/shard_map/ppermute | solution.py:393
  18.1 1.5 %collective-permute-start.5 = (f32[72,128]{1,0:T(8,128)S(1)}, f32[72,128]{1,0:T(8,128)S(1)}, u32[]{:S(2)}, u32[]{:S(2)}) collective-permute-start(f32[72,128]{1,0:T(8,128)S(1)} %get-tuple-element.31), channel_id=1, source_target_pairs={{0,2},{1,5},{2,0},{3,7},{4,6},{5,1},{6,4},{7,3},{8,10},{9,13},{10,... | collective-permute-start | bytes 110600 | tf_op jit(solution)/shard_map/ppermute | solution.py:393
  19.7 0.4 %collective-permute-done.7 = f32[72,128]{1,0:T(8,128)S(1)} collective-permute-done((f32[72,128]{1,0:T(8,128)S(1)}, f32[72,128]{1,0:T(8,128)S(1)}, u32[]{:S(2)}, u32[]{:S(2)}) %collective-permute-start.7) | collective-permute-done | bytes 36896 | tf_op jit(solution)/shard_map/ppermute | solution.py:393
  20.1 1.5 %collective-permute-done.6 = f32[72,128]{1,0:T(8,128)S(1)} collective-permute-done((f32[72,128]{1,0:T(8,128)S(1)}, f32[72,128]{1,0:T(8,128)S(1)}, u32[]{:S(2)}, u32[]{:S(2)}) %collective-permute-start.6) | collective-permute-done | bytes 36896 | tf_op jit(solution)/shard_map/ppermute | solution.py:393
  21.6 0.5 %collective-permute-done.5 = f32[72,128]{1,0:T(8,128)S(1)} collective-permute-done((f32[72,128]{1,0:T(8,128)S(1)}, f32[72,128]{1,0:T(8,128)S(1)}, u32[]{:S(2)}, u32[]{:S(2)}) %collective-permute-start.5) | collective-permute-done | bytes 36896 | tf_op jit(solution)/shard_map/ppermute | solution.py:393
  22.1 1.6 %collective-permute-start.8 = (f32[72,128]{1,0:T(8,128)S(1)}, f32[72,128]{1,0:T(8,128)S(1)}, u32[]{:S(2)}, u32[]{:S(2)}) collective-permute-start(f32[72,128]{1,0:T(8,128)S(1)} %add_add_fusion.rest_0_), channel_id=1, source_target_pairs={{0,2},{1,17},{2,0},{3,19},{4,6},{5,21},{6,4},{7,23},{8,10},{9,25},... | collective-permute-start | bytes 110600 | tf_op jit(solution)/shard_map/ppermute | solution.py:393
  23.7 2.4 %collective-permute-done.8.rest_1_ = f32[72,128]{1,0:T(8,128)S(1)} collective-permute-done((f32[72,128]{1,0:T(8,128)S(1)}, f32[72,128]{1,0:T(8,128)S(1)}, u32[]{:S(2)}, u32[]{:S(2)}) %collective-permute-start.8) | collective-permute-done | bytes 36896 | tf_op jit(solution)/shard_map/ppermute | solution.py:393
  26.1 0.6 %second_step.1 = (f32[2,768]{1,0:T(2,128)S(1)}, f32[2,768]{1,0:T(2,128)S(1)}) custom-call(s32[2,128]{1,0:T(2,128)S(1)} %get-tuple-element.23.meta_ref, bf16[128,128,128]{2,1,0:T(8,128)(2,1)S(1)} %turn.1.turned_ref, f32[72,128]{1,0:T(8,128)S(1)} %add_add_fusion.rest_0_, f32[72,128]{1,0:T(8,128)S(1)} %collective-permute-done.8.rest_1_, ...), custom_call_target="tpu_custom_call" | custom-call | tf_op jit(solution)/shard_map/second_step/pallas_call | solution.py:521
  26.7 3.8 %collective-permute-start.9 = (f32[2,768]{1,0:T(2,128)S(1)}, f32[2,768]{1,0:T(2,128)S(1)}, u32[]{:S(2)}, u32[]{:S(2)}) collective-permute-start(f32[2,768]{1,0:T(2,128)S(1)} %get-tuple-element.37), channel_id=1, source_target_pairs={{0,1},{1,0},{2,3},{3,2},{4,5},{5,4},{6,7},{7,6},{8,9},{9,8},{10,11... | collective-permute-start | bytes 18440 | tf_op jit(solution)/shard_map/ppermute | solution.py:380
  30.5 0.8 %collective-permute-done.9.got_ref = f32[2,768]{1,0:T(2,128)S(1)} collective-permute-done((f32[2,768]{1,0:T(2,128)S(1)}, f32[2,768]{1,0:T(2,128)S(1)}, u32[]{:S(2)}, u32[]{:S(2)}) %collective-permute-start.9) | collective-permute-done | bytes 6176 | tf_op jit(solution)/shard_map/ppermute | solution.py:380
  31.3 0.6 %finish.1 = (f32[2,256]{1,0:T(2,128)}, f32[2,512]{1,0:T(2,128)}) custom-call(f32[2,768]{1,0:T(2,128)S(1)} %get-tuple-element.36.mine_ref, f32[2,768]{1,0:T(2,128)S(1)} %collective-permute-done.9.got_ref), custom_call_target="tpu_custom_call" | custom-call | tf_op jit(solution)/shard_map/finish/pallas_call | solution.py:531
  (3 shorter events, 0.0 us)
Async XLA Ops:
  1.5 2.2 %collective-permute-start = (f32[2,1024]{1,0:T(2,128)S(1)}, f32[2,1024]{1,0:T(2,128)S(1)}, u32[]{:S(2)}, u32[]{:S(2)}) collective-permute-start(f32[2,1024]{1,0:T(2,128)S(1)} %get-tuple-element.28.mine_ref), channel_id=1, source_target_pairs={{0,1},{1,0},{2,3},{3,2},{4,5},{5,4},{6,7},{7,6},{8,9},{9,8},{10,11... | collective-permute-start | bytes 24584 | tf_op jit(solution)/shard_map/ppermute | solution.py:380
  4.3 4.4 %collective-permute-start.3 = (f32[88,128]{1,0:T(8,128)S(1)}, f32[88,128]{1,0:T(8,128)S(1)}, u32[]{:S(2)}, u32[]{:S(2)}) collective-permute-start(f32[88,128]{1,0:T(8,128)S(1)} %get-tuple-element.29.refs_0_), channel_id=1, source_target_pairs={{0,2},{1,13},{2,0},{3,15},{4,6},{5,9},{6,4},{7,11},{8,10},{9,5},{1... | collective-permute-start | bytes 135176 | tf_op jit(solution)/shard_map/ppermute | solution.py:393
  6.7 4.0 %collective-permute-start.2 = (f32[88,128]{1,0:T(8,128)S(1)}, f32[88,128]{1,0:T(8,128)S(1)}, u32[]{:S(2)}, u32[]{:S(2)}) collective-permute-start(f32[88,128]{1,0:T(8,128)S(1)} %get-tuple-element.29.refs_0_), channel_id=1, source_target_pairs={{0,2},{1,9},{2,0},{3,11},{4,6},{5,13},{6,4},{7,15},{8,10},{9,1},{1... | collective-permute-start | bytes 135176 | tf_op jit(solution)/shard_map/ppermute | solution.py:393
  6.7 4.5 %collective-permute-start.1 = (f32[88,128]{1,0:T(8,128)S(1)}, f32[88,128]{1,0:T(8,128)S(1)}, u32[]{:S(2)}, u32[]{:S(2)}) collective-permute-start(f32[88,128]{1,0:T(8,128)S(1)} %get-tuple-element.29.refs_0_), channel_id=1, source_target_pairs={{0,2},{1,5},{2,0},{3,7},{4,6},{5,1},{6,4},{7,3},{8,10},{9,13},{10,... | collective-permute-start | bytes 135176 | tf_op jit(solution)/shard_map/ppermute | solution.py:393
  11.2 4.3 %copy-start = (f32[512]{0:T(512)S(1)}, f32[512]{0:T(512)}, u32[]{:S(2)}) copy-start(f32[512]{0:T(512)} %param.13) | copy-start | bytes 6148
  11.2 4.2 %collective-permute-start.4 = (f32[112,128]{1,0:T(8,128)S(1)}, f32[112,128]{1,0:T(8,128)S(1)}, u32[]{:S(2)}, u32[]{:S(2)}) collective-permute-start(f32[112,128]{1,0:T(8,128)S(1)} %merge.1.rest_0_), channel_id=1, source_target_pairs={{0,2},{1,17},{2,0},{3,19},{4,6},{5,21},{6,4},{7,23},{8,10},{9,25},... | collective-permute-start | bytes 172040 | tf_op jit(solution)/shard_map/ppermute | solution.py:393
  16.0 4.0 %collective-permute-start.7 = (f32[72,128]{1,0:T(8,128)S(1)}, f32[72,128]{1,0:T(8,128)S(1)}, u32[]{:S(2)}, u32[]{:S(2)}) collective-permute-start(f32[72,128]{1,0:T(8,128)S(1)} %get-tuple-element.31), channel_id=1, source_target_pairs={{0,2},{1,13},{2,0},{3,15},{4,6},{5,9},{6,4},{7,11},{8,10},{9,5},{1... | collective-permute-start | bytes 110600 | tf_op jit(solution)/shard_map/ppermute | solution.py:393
  17.6 4.0 %collective-permute-start.6 = (f32[72,128]{1,0:T(8,128)S(1)}, f32[72,128]{1,0:T(8,128)S(1)}, u32[]{:S(2)}, u32[]{:S(2)}) collective-permute-start(f32[72,128]{1,0:T(8,128)S(1)} %get-tuple-element.31), channel_id=1, source_target_pairs={{0,2},{1,9},{2,0},{3,11},{4,6},{5,13},{6,4},{7,15},{8,10},{9,1},{1... | collective-permute-start | bytes 110600 | tf_op jit(solution)/shard_map/ppermute | solution.py:393
  18.1 4.0 %collective-permute-start.5 = (f32[72,128]{1,0:T(8,128)S(1)}, f32[72,128]{1,0:T(8,128)S(1)}, u32[]{:S(2)}, u32[]{:S(2)}) collective-permute-start(f32[72,128]{1,0:T(8,128)S(1)} %get-tuple-element.31), channel_id=1, source_target_pairs={{0,2},{1,5},{2,0},{3,7},{4,6},{5,1},{6,4},{7,3},{8,10},{9,13},{10,... | collective-permute-start | bytes 110600 | tf_op jit(solution)/shard_map/ppermute | solution.py:393
  22.1 4.0 %collective-permute-start.8 = (f32[72,128]{1,0:T(8,128)S(1)}, f32[72,128]{1,0:T(8,128)S(1)}, u32[]{:S(2)}, u32[]{:S(2)}) collective-permute-start(f32[72,128]{1,0:T(8,128)S(1)} %add_add_fusion.rest_0_), channel_id=1, source_target_pairs={{0,2},{1,17},{2,0},{3,19},{4,6},{5,21},{6,4},{7,23},{8,10},{9,25},... | collective-permute-start | bytes 110600 | tf_op jit(solution)/shard_map/ppermute | solution.py:393
  26.7 4.6 %collective-permute-start.9 = (f32[2,768]{1,0:T(2,128)S(1)}, f32[2,768]{1,0:T(2,128)S(1)}, u32[]{:S(2)}, u32[]{:S(2)}) collective-permute-start(f32[2,768]{1,0:T(2,128)S(1)} %get-tuple-element.37), channel_id=1, source_target_pairs={{0,1},{1,0},{2,3},{3,2},{4,5},{5,4},{6,7},{7,6},{8,9},{9,8},{10,11... | collective-permute-start | bytes 18440 | tf_op jit(solution)/shard_map/ppermute | solution.py:380

commit v4 on v3

--- a/solution.py
+++ b/solution.py
@@ -70,130 +70,110 @@
         flat[pl.ds(VECS * s + v, blocks, stride=KEPT), :] = term
 
 
-def tile_pass(meta_ref, tiles_refs, left_ref, of_row, into_refs, each=None):
+def row_of(meta_ref, count_ref, t):
+    return jnp.where(t < count_ref[0], meta_ref[0, t], ROWBLK)
+
+
+def tile_pass(meta_ref, count_ref, tiles_ref, left_ref, of_row, into_refs):
     count = left_ref.shape[0] // 2
-    first = 0
-    for tiles_ref in tiles_refs:
-        ntile = tiles_ref.shape[0]
-        for t in range(0, ntile, 2):
-            rows = [meta_ref[0, first + t], meta_ref[0, first + t + 1]]
-            cols = [meta_ref[1, first + t], meta_ref[1, first + t + 1]]
-            source, place = (rows, cols) if of_row else (cols, rows)
-            left = jnp.concatenate([left_ref[source[0]], left_ref[count + source[1]]], axis=1)
-            pair = tiles_ref[t : t + 2].reshape(2 * EDGE, EDGE)
-            product = jnp.dot(left, pair, preferred_element_type=jnp.float32)
-            for u in range(2):
-                part = product[u * KEPT : (u + 1) * KEPT]
-                into_refs[u][place[u]] += jnp.where(rows[u] < ROWBLK, part, 0.0)
-                if each is not None:
-                    each(tiles_ref[t + u], rows[u], cols[u], u)
-        first += ntile
-
-
-def fetch(tiles_ref, held_ref, sems, first, g):
-    from_part, to_part = pl.ds(g * FETCH, FETCH), pl.ds((g - first) * FETCH, FETCH)
-    return pltpu.make_async_copy(tiles_ref.at[from_part], held_ref.at[to_part], sems.at[g - first])
-
-
-def row_peaks(row_at, held_ref, peak_refs, first, g):
-    for u in range(FETCH):
-        t = g * FETCH + u
-        r = row_at(t)
-        ref = peak_refs[u % 2]
-        ref[r] = jnp.maximum(ref[r], jnp.abs(held_ref[t - first * FETCH]))
-
-
-def pack_kernel(
-    rows_ref, cols_ref, y_ref, x_ref, cost_ref, tiles_ref,
-    meta_ref, own_ref, held_ref, even_ref, odd_ref,
-    small_sems, sems, rows_s_ref,
+    for t in range(0, tiles_ref.shape[0], 2):
+        rows = [row_of(meta_ref, count_ref, t + u) for u in range(2)]
+        cols = [meta_ref[1, t + u] for u in range(2)]
+        source, place = (rows, cols) if of_row else (cols, rows)
+        left = jnp.concatenate([left_ref[source[0]], left_ref[count + source[1]]], axis=1)
+        pair = tiles_ref[t : t + 2].reshape(2 * EDGE, EDGE)
+        product = jnp.dot(left, pair, preferred_element_type=jnp.float32)
+        for u in range(2):
+            part = product[u * KEPT : (u + 1) * KEPT]
+            into_refs[u][place[u]] += jnp.where(rows[u] < ROWBLK, part, 0.0)
+
+
+def scale_kernel(
+    rows_ref, cols_ref, count_ref, y_ref, x_ref, cost_ref, tiles_ref,
+    meta_ref, own_ref, held_ref, spread_ref, rscale_ref,
+    small_sems, sems, even_ref, odd_ref,
 ):
     nrow, ncol = y_ref.shape[1], x_ref.shape[1]
-    groups = held_ref.shape[0] // FETCH
-    copies = [
-        pltpu.make_async_copy(rows_ref, rows_s_ref, small_sems.at[0]),
-        pltpu.make_async_copy(rows_ref, meta_ref.at[0:1], small_sems.at[1]),
-        pltpu.make_async_copy(cols_ref, meta_ref.at[1:2], small_sems.at[2]),
-        pltpu.make_async_copy(y_ref, own_ref.at[:, 0:nrow], small_sems.at[3]),
-        pltpu.make_async_copy(x_ref, own_ref.at[:, nrow : nrow + ncol], small_sems.at[4]),
-        pltpu.make_async_copy(cost_ref, own_ref.at[:, nrow + ncol :], small_sems.at[5]),
+    parts = sems.shape[0]
+    per = held_ref.shape[0] // parts
+    places = [
+        pltpu.make_async_copy(rows_ref, meta_ref.at[0:1], small_sems.at[0]),
+        pltpu.make_async_copy(cols_ref, meta_ref.at[1:2], small_sems.at[1]),
     ]
-    for copy in copies:
+    vectors = [
+        pltpu.make_async_copy(y_ref, own_ref.at[:, 0:nrow], small_sems.at[2]),
+        pltpu.make_async_copy(x_ref, own_ref.at[:, nrow : nrow + ncol], small_sems.at[3]),
+        pltpu.make_async_copy(cost_ref, own_ref.at[:, nrow + ncol :], small_sems.at[4]),
+    ]
+    for copy in places:
         copy.start()
 
     @pl.when(leads())
     def _():
-        for g in range(groups):
-            fetch(tiles_ref, held_ref, sems, 0, g).start()
-        for ref in (even_ref, odd_ref):
+        peak_refs = (even_ref, odd_ref)
+        fetches = []
+        for g in range(parts):
+            part = pl.ds(g * per, per)
+            fetches.append(pltpu.make_async_copy(tiles_ref.at[part], held_ref.at[part], sems.at[g]))
+            fetches[g].start()
+        for copy in vectors:
+            copy.start()
+        for ref in peak_refs:
             ref[...] = jnp.zeros_like(ref)
-
-    for copy in copies:
-        copy.wait()
-
-    @pl.when(leads())
-    def _():
-        def group(g, carry):
-            fetch(tiles_ref, held_ref, sems, 0, g).wait()
-            row_peaks(lambda t: rows_s_ref[0, t], held_ref, (even_ref, odd_ref), 0, g)
-            return carry
-
-        lax.fori_loop(0, groups, group, 0)
-
-
-def scale_kernel(
-    meta_ref, count_ref, even_in_ref, odd_in_ref, tiles_ref,
-    meta_out_ref, held_ref, spread_ref, rscale_ref,
-    meta_sem, sems, meta_s_ref, even_ref, odd_ref,
-):
-    groups = tiles_ref.shape[0] // FETCH
-    first = groups - held_ref.shape[0] // FETCH
-
-    @pl.when(leads())
-    def _():
-        for g in range(first, groups):
-            fetch(tiles_ref, held_ref, sems, first, g).start()
-        index = lax.broadcasted_iota(jnp.int32, (1, tiles_ref.shape[0]), 1)
-        meta_out_ref[0:1, :] = jnp.where(index < count_ref[...], meta_ref[0:1, :], ROWBLK)
-        meta_out_ref[1:2, :] = meta_ref[1:2, :]
-        copy = pltpu.make_async_copy(meta_out_ref, meta_s_ref, meta_sem)
-        copy.start()
-        even_ref[...] = even_in_ref[...]
-        odd_ref[...] = odd_in_ref[...]
         spread_ref[ROWBLK] = jnp.zeros((EDGE, EDGE), jnp.float32)
-        copy.wait()
-
-        def group(g, carry):
-            fetch(tiles_ref, held_ref, sems, first, g).wait()
-            row_peaks(lambda t: meta_s_ref[0, t], held_ref, (even_ref, odd_ref), first, g)
-            return carry
-
-        lax.fori_loop(first, groups, group, 0)
+        for copy in places:
+            copy.wait()
+        for t in range(held_ref.shape[0]):
+            if t % per == 0:
+                fetches[t // per].wait()
+            r = row_of(meta_ref, count_ref, t)
+            tile = held_ref[t]
+            ref = peak_refs[t % 2]
+            ref[r] = jnp.maximum(ref[r], jnp.maximum(tile, -tile))
         for r in range(ROWBLK):
             peak = jnp.maximum(even_ref[r], odd_ref[r]).astype(jnp.float32)
             scale = lax.rsqrt(jnp.max(peak, axis=1, keepdims=True))
             spread_ref[r] = jnp.broadcast_to(scale, (EDGE, EDGE))
             rscale_ref[r : r + 1, :] = lax.rsqrt(jnp.max(peak.T, axis=0, keepdims=True))
-
-
-def turn_kernel(one_ref, two_ref, turned_ref):
+        for copy in vectors:
+            copy.wait()
+
+    @pl.when(jnp.logical_not(leads()))
+    def _():
+        for copy in vectors:
+            copy.start()
+        for copy in places + vectors:
+            copy.wait()
+
+
+def columns_kernel(meta_ref, count_ref, held_ref, spread_ref, top_out_ref, even_ref, odd_ref):
     @pl.when(leads())
     def _():
-        first = 0
-        for ref in (one_ref, two_ref):
-            for t in range(ref.shape[0]):
-                turned_ref[first + t] = ref[t].T
-            first += ref.shape[0]
+        for ref in (even_ref, odd_ref):
+            ref[...] = jnp.zeros_like(ref)
+        for t in range(held_ref.shape[0]):
+            c = meta_ref[1, t]
+            scaled = jnp.abs(held_ref[t].astype(jnp.float32)) * spread_ref[row_of(meta_ref, count_ref, t)]
+            peak = jnp.max(scaled.reshape(EDGE // 8, 8, EDGE), axis=0)
+            ref = (even_ref, odd_ref)[t % 2]
+            ref[c] = jnp.maximum(ref[c], peak)
+        top_out_ref[...] = jnp.max(jnp.maximum(even_ref[...], odd_ref[...]), axis=1)
+
+
+def turn_kernel(tiles_ref, turned_ref):
+    @pl.when(leads())
+    def _():
+        for t in range(tiles_ref.shape[0]):
+            turned_ref[t] = tiles_ref[t].T
 
 
 def start_kernel(
-    meta_ref, one_ref, two_ref, spread_ref, rscale_ref, mine_ref, other_ref,
+    meta_ref, count_ref, tiles_ref, rscale_ref, top_ref, mine_ref, other_ref,
     send_ref, both_ref,
-    left_ref, top_ref, top_two_ref, sums_ref, sums_two_ref,
+    left_ref, sums_ref, sums_two_ref,
 ):
     blocks = sums_ref.shape[0]
     sums_refs = (sums_ref, sums_two_ref)
-    top_refs = (top_ref, top_two_ref)
     nrow = ROWBLK * EDGE
     ncol = COLBLK * EDGE
 
@@ -201,23 +181,15 @@
     def _():
         both = jnp.concatenate([mine_ref[...], other_ref[...]], axis=0)
         both_ref[...] = both
-        for ref in top_refs:
-            ref[...] = jnp.zeros_like(ref)
         clear_left(left_ref)
         adjoint_start(sums_refs, both[:, nrow + ncol :], lax.axis_index("band"))
         for r in range(ROWBLK):
             put_left(left_ref, r, both[:, r * EDGE : (r + 1) * EDGE] * rscale_ref[r : r + 1, :])
+        send_ref[0:blocks, :] = top_ref[...]
         for j in range(COLBLK):
             at = (1 + VECS) * blocks + j * VECS
             send_ref[at : at + VECS, :] = both[:, nrow + j * EDGE : nrow + (j + 1) * EDGE]
-
-        def column_peaks(tile, r, c, u):
-            scaled = jnp.abs(tile).astype(jnp.float32) * spread_ref[r]
-            peak = jnp.max(scaled.reshape(EDGE // 8, 8, EDGE), axis=0)
-            top_refs[u][c] = jnp.maximum(top_refs[u][c], peak)
-
-        tile_pass(meta_ref, (one_ref, two_ref), left_ref, True, sums_refs, column_peaks)
-        send_ref[0:blocks, :] = jnp.max(jnp.maximum(top_ref[...], top_two_ref[...]), axis=1)
+        tile_pass(meta_ref, count_ref, tiles_ref, left_ref, True, sums_refs)
         for v in range(VECS):
             send_ref[(1 + v) * blocks : (2 + v) * blocks, :] = adjoint_sum(sums_refs, v)
 
@@ -240,7 +212,7 @@
 
 
 def step_kernel(
-    offsets, parts, meta_ref, one_ref, two_ref, turned_ref, *rest,
+    offsets, parts, meta_ref, count_ref, tiles_ref, turned_ref, *rest,
 ):
     got_refs = rest[:parts]
     (
@@ -284,7 +256,7 @@
 
         for ref in (out_ref, out_two_ref):
             ref[...] = jnp.zeros_like(ref)
-        tile_pass(meta_ref, (turned_ref,), right_ref, False, (out_ref, out_two_ref))
+        tile_pass(meta_ref, count_ref, turned_ref, right_ref, False, (out_ref, out_two_ref))
 
         moved = jnp.zeros((VECS, EDGE), jnp.float32)
         for r in range(ROWBLK):
@@ -298,14 +270,14 @@
             moved += (after - before) ** 2
             put_left(left_ref, r, after * scale)
 
-        tile_pass(meta_ref, (one_ref, two_ref), left_ref, True, sums_refs)
+        tile_pass(meta_ref, count_ref, tiles_ref, left_ref, True, sums_refs)
         for v in range(VECS):
             send_ref[v * blocks : (v + 1) * blocks, :] = adjoint_sum(sums_refs, v)
         send_ref[VECS * blocks :, :] = jnp.zeros((8, EDGE), jnp.float32)
         send_ref[VECS * blocks : VECS * blocks + VECS, :] = moved
 
 
-def last_kernel(parts, meta_ref, turned_ref, *rest):
+def last_kernel(parts, meta_ref, count_ref, turned_ref, *rest):
     got_refs = rest[:parts]
     (
         rscale_ref, y_ref, bound_ref, x_one_ref, cscale_ref, moved_ref,
@@ -343,7 +315,7 @@
 
         for ref in (out_ref, out_two_ref):
             ref[...] = jnp.zeros_like(ref)
-        tile_pass(meta_ref, (turned_ref,), right_ref, False, (out_ref, out_two_ref))
+        tile_pass(meta_ref, count_ref, turned_ref, right_ref, False, (out_ref, out_two_ref))
 
         for r in range(ROWBLK):
             span = slice(r * EDGE, (r + 1) * EDGE)
@@ -424,65 +396,60 @@
     params = pltpu.CompilerParams(vmem_limit_bytes=32 * 1024 * 1024)
     in_hbm = lambda value: pltpu.with_memory_space_constraint(value, pltpu.HBM)
 
-    early = ntile * 3 // 8
-    small = (tile_row, tile_col, y_start, x_start, cost)
-    peaks = [v16(ROWBLK + 1, EDGE, EDGE)] * 2
-    tiles = in_hbm(tiles)
-    meta, mine, one, *tops = pl.pallas_call(
-        pack_kernel,
-        out_shape=(
-            pltpu.VMEM((2, ntile), jnp.int32), v32(VECS // 2, nrow + 2 * COLBLK * EDGE), v16(early, EDGE, EDGE), *peaks,
-        ),
-        in_specs=hbm(6),
-        out_specs=tuple(vmem(5)),
-        scratch_shapes=[
-            pltpu.SemaphoreType.DMA((6,)),
-            pltpu.SemaphoreType.DMA((early // FETCH,)),
-            pltpu.SMEM((1, ntile), jnp.int32),
-        ],
-        compiler_params=params,
-        name="pack",
-    )(*map(in_hbm, small), tiles)
-    other = swap(mine)
-
-    late = ntile - early
-    meta, two, spread, rscale = pl.pallas_call(
+    tile_cost = pl.CostEstimate(flops=0, bytes_accessed=tiles.nbytes, transcendentals=0)
+    meta, mine, held, spread, rscale = pl.pallas_call(
         scale_kernel,
         out_shape=(
-            pltpu.VMEM((2, ntile), jnp.int32), v16(late, EDGE, EDGE), v32(ROWBLK + 1, EDGE, EDGE), v32(ROWBLK, EDGE),
+            pltpu.SMEM((2, ntile), jnp.int32),
+            v32(VECS // 2, nrow + 2 * COLBLK * EDGE),
+            v16(*tiles.shape),
+            v32(ROWBLK + 1, EDGE, EDGE),
+            v32(ROWBLK, EDGE),
         ),
-        in_specs=vmem(4) + hbm(1),
-        out_specs=tuple(vmem(4)),
+        in_specs=hbm(2) + smem + hbm(4),
+        out_specs=tuple(smem + vmem(4)),
         scratch_shapes=[
-            pltpu.SemaphoreType.DMA,
-            pltpu.SemaphoreType.DMA((late // FETCH,)),
-            pltpu.SMEM((2, ntile), jnp.int32),
-            *peaks,
+            pltpu.SemaphoreType.DMA((5,)),
+            pltpu.SemaphoreType.DMA((ntile // FETCH,)),
+            v16(ROWBLK + 1, EDGE, EDGE),
+            v16(ROWBLK + 1, EDGE, EDGE),
         ],
         compiler_params=params,
-        cost_estimate=pl.CostEstimate(flops=0, bytes_accessed=tiles.nbytes, transcendentals=0),
+        cost_estimate=tile_cost,
         name="row_scales",
-    )(meta, tile_count.reshape(1, 1), *tops, tiles)
+    )(in_hbm(tile_row), in_hbm(tile_col), tile_count, *map(in_hbm, (y_start, x_start, cost, tiles)))
+    other = swap(mine)
+
+    top = pl.pallas_call(
+        columns_kernel,
+        out_shape=v32(blocks, EDGE),
+        in_specs=smem * 2 + vmem(2),
+        out_specs=vmem(1)[0],
+        scratch_shapes=[v32(blocks, 8, EDGE)] * 2,
+        compiler_params=params,
+        cost_estimate=tile_cost,
+        name="columns",
+    )(meta, tile_count, held, spread)
 
     turned = pl.pallas_call(
         turn_kernel,
         out_shape=v16(*tiles.shape),
-        in_specs=vmem(2),
+        in_specs=vmem(1),
         out_specs=vmem(1)[0],
         compiler_params=params,
-        cost_estimate=pl.CostEstimate(flops=0, bytes_accessed=tiles.nbytes, transcendentals=0),
+        cost_estimate=tile_cost,
         name="turn",
-    )(one, two)
+    )(held)
 
     message, both = pl.pallas_call(
         start_kernel,
         out_shape=(f32((1 + VECS) * blocks + COLBLK * VECS, EDGE), v32(VECS, mine.shape[1])),
-        in_specs=smem + vmem(6),
+        in_specs=smem * 2 + vmem(5),
         out_specs=tuple(vmem(2)),
-        scratch_shapes=left + [v32(blocks, 8, EDGE)] * 2 + sums,
+        scratch_shapes=left + sums,
         compiler_params=params,
         name="start",
-    )(meta, one, two, spread, rscale, mine, other)
+    )(meta, tile_count, held, rscale, top, mine, other)
 
     rounds = rounds_of(bands)
     offsets = [0]
@@ -504,12 +471,12 @@
         out_shape=(
             f32(VECS * blocks + 8, EDGE), v32(VECS * blocks, EDGE), v32(blocks, EDGE), v32(VECS, nrow), v32(VECS, EDGE),
         ),
-        in_specs=smem + vmem(6 + len(messages)),
+        in_specs=smem * 2 + vmem(5 + len(messages)),
         out_specs=tuple(vmem(5)),
         scratch_shapes=[v32(blocks, 8, EDGE)] + right + rows_out + left + sums,
         compiler_params=params,
         name="first_step",
-    )(meta, one, two, turned, *messages, rscale, both, bound)
+    )(meta, tile_count, held, turned, *messages, rscale, both, bound)
 
     for index, hops in enumerate(rounds):
         messages = [message] + [from_band(message, hop) for hop in hops]
@@ -521,12 +488,12 @@
     mine, other = pl.pallas_call(
         functools.partial(last_kernel, len(messages)),
         out_shape=(v32(half, width), v32(half, width)),
-        in_specs=smem + vmem(7 + len(messages)),
+        in_specs=smem * 2 + vmem(7 + len(messages)),
         out_specs=tuple(vmem(2)),
         scratch_shapes=right + rows_out,
         compiler_params=params,
         name="second_step",
-    )(meta, turned, *messages, rscale, y_one, bound, x_one, cscale, moved)
+    )(meta, tile_count, turned, *messages, rscale, y_one, bound, x_one, cscale, moved)
 
     return pl.pallas_call(
         finish_kernel,

time: 32.1 us -> 29.5 us (0.919)
  Pallas kernels: 3.22 us -> 1.48 us
  starting transfers between devices: 16.4 us -> 14.9 us
  waiting for transfers between devices: 10.9 us -> 11.6 us
    ppermute x2, starting transfers between devices: 5.17 us -> 3.81 us  [swap(): return lax.ppermute(value, 'batch', [(i, i ^ 1) for i in range(count)])]
    ppermute x2, waiting for transfers between devices: 0.92 us -> 1.65 us  [swap(): return lax.ppermute(value, 'batch', [(i, i ^ 1) for i in range(count)])]
    pallas_call x1, Pallas kernels: 0.56 us -> 0.01 us  [shards(): pl.pallas_call(functools.partial(step_kernel, offsets, len(messages)), ou...]
    pallas_call x1, Pallas kernels: 0.56 us -> 0.01 us  [shards(): pl.pallas_call(functools.partial(last_kernel, len(messages)), out_shape=(...]
    pallas_call x1, Pallas kernels: 0.56 us -> 0.01 us  [shards(): pl.pallas_call(start_kernel, out_shape=(f32((1 + VECS) * blocks + COLBLK...]
where the time goes in v4:
time: 29.5 us; the launch traced here: 29.4 us
  starting transfers between devices  14.9 us (51%)
  waiting for transfers between devices  11.6 us (39%)
  Pallas kernels  1.48 us (5%)
  between operations  1.31 us (4%)
    ppermute x8, starting transfers between devices, from_band(): return lax.ppermute(value, ('band', 'batch'), pairs)  11.1 us
    ppermute x8, waiting for transfers between devices, from_band(): return lax.ppermute(value, ('band', 'batch'), pairs)  9.96 us
    ppermute x2, starting transfers between devices, swap(): return lax.ppermute(value, 'batch', [(i, i ^ 1) for i in range(count)])  3.81 us
    ppermute x2, waiting for transfers between devices, swap(): return lax.ppermute(value, 'batch', [(i, i ^ 1) for i in range(count)])  1.65 us
    pallas_call x1, Pallas kernels, shards(): pl.pallas_call(scale_kernel, out_shape=(pltpu.SMEM((2, ntile), jnp.int32)...  0.85 us
    pallas_call x1, Pallas kernels, shards(): pl.pallas_call(finish_kernel, out_shape=(f32(*x_start.shape), f32(*y_star...  0.61 us
  transfers between devices with their start and end apart: 10, of which 9 were waited for; matrix products, arithmetic and copies ran while one was open for 0% of the time, Pallas kernels for 0%

profile of v4, /device:TPU:0, one launch (start us, length us, event | category | flops | bytes accessed | tf_op | source)
XLA Modules:
  0.0 29.4 jit_solution(10408940164958019039)
XLA Ops:
  1.3 0.8 %row_scales.1 = (s32[2,128]{1,0:T(2,128)S(4)}, f32[2,1024]{1,0:T(2,128)S(1)}, bf16[128,128,128]{2,1,0:T(8,128)(2,1)S(1)}, f32[5,128,128]{2,1,0:T(8,128)S(1)}, f32[4,128]{1,0:T(4,128)S(1)}) custom-call(s32[1,128]{1,0:T(1,128)} %rows_ref.1, s32[1,128]{1,0:T(1,128)} %cols_ref.1, s32[1]{0:T(128)S(6)} %copy.10.count_ref, f32[2,512]{1,0:T(2,128)} %y_ref.1, ...), custom_call_target="tpu_custom_call" | custom-call | bytes 4194304 | tf_op jit(solution)/shard_map/row_scales/pallas_call | solution.py:400
  2.1 2.3 %collective-permute-start = (f32[2,1024]{1,0:T(2,128)S(1)}, f32[2,1024]{1,0:T(2,128)S(1)}, u32[]{:S(2)}, u32[]{:S(2)}) collective-permute-start(f32[2,1024]{1,0:T(2,128)S(1)} %get-tuple-element.20.mine_ref), channel_id=1, source_target_pairs={{0,1},{1,0},{2,3},{3,2},{4,5},{5,4},{6,7},{7,6},{8,9},{9,8},{10,11... | collective-permute-start | bytes 24584 | tf_op jit(solution)/shard_map/ppermute | solution.py:352
  4.5 0.8 %collective-permute-done.other_ref = f32[2,1024]{1,0:T(2,128)S(1)} collective-permute-done((f32[2,1024]{1,0:T(2,128)S(1)}, f32[2,1024]{1,0:T(2,128)S(1)}, u32[]{:S(2)}, u32[]{:S(2)}) %collective-permute-start) | collective-permute-done | bytes 8224 | tf_op jit(solution)/shard_map/ppermute | solution.py:352
  5.3 2.3 %collective-permute-start.3 = (f32[88,128]{1,0:T(8,128)S(1)}, f32[88,128]{1,0:T(8,128)S(1)}, u32[]{:S(2)}, u32[]{:S(2)}) collective-permute-start(f32[88,128]{1,0:T(8,128)S(1)} %get-tuple-element.21.refs_0_), channel_id=1, source_target_pairs={{0,2},{1,13},{2,0},{3,15},{4,6},{5,9},{6,4},{7,11},{8,10},{9,5},{1... | collective-permute-start | bytes 135176 | tf_op jit(solution)/shard_map/ppermute | solution.py:365
  7.6 0.0 collective-permute-start.2
  7.6 2.0 %collective-permute-start.1 = (f32[88,128]{1,0:T(8,128)S(1)}, f32[88,128]{1,0:T(8,128)S(1)}, u32[]{:S(2)}, u32[]{:S(2)}) collective-permute-start(f32[88,128]{1,0:T(8,128)S(1)} %get-tuple-element.21.refs_0_), channel_id=1, source_target_pairs={{0,2},{1,5},{2,0},{3,7},{4,6},{5,1},{6,4},{7,3},{8,10},{9,13},{10,... | collective-permute-start | bytes 135176 | tf_op jit(solution)/shard_map/ppermute | solution.py:365
  9.6 0.0 collective-permute-done.3.refs_3_
  9.6 2.0 %collective-permute-done.2.refs_2_ = f32[88,128]{1,0:T(8,128)S(1)} collective-permute-done((f32[88,128]{1,0:T(8,128)S(1)}, f32[88,128]{1,0:T(8,128)S(1)}, u32[]{:S(2)}, u32[]{:S(2)}) %collective-permute-start.2) | collective-permute-done | bytes 45088 | tf_op jit(solution)/shard_map/ppermute | solution.py:365
  11.7 0.5 %collective-permute-done.1.refs_1_ = f32[88,128]{1,0:T(8,128)S(1)} collective-permute-done((f32[88,128]{1,0:T(8,128)S(1)}, f32[88,128]{1,0:T(8,128)S(1)}, u32[]{:S(2)}, u32[]{:S(2)}) %collective-permute-start.1) | collective-permute-done | bytes 45088 | tf_op jit(solution)/shard_map/ppermute | solution.py:365
  12.2 0.0 copy-start
  12.2 1.6 %collective-permute-start.4 = (f32[112,128]{1,0:T(8,128)S(1)}, f32[112,128]{1,0:T(8,128)S(1)}, u32[]{:S(2)}, u32[]{:S(2)}) collective-permute-start(f32[112,128]{1,0:T(8,128)S(1)} %merge.1.rest_0_), channel_id=1, source_target_pairs={{0,2},{1,17},{2,0},{3,19},{4,6},{5,21},{6,4},{7,23},{8,10},{9,25},... | collective-permute-start | bytes 172040 | tf_op jit(solution)/shard_map/ppermute | solution.py:365
  13.8 2.6 %collective-permute-done.4.rest_1_ = f32[112,128]{1,0:T(8,128)S(1)} collective-permute-done((f32[112,128]{1,0:T(8,128)S(1)}, f32[112,128]{1,0:T(8,128)S(1)}, u32[]{:S(2)}, u32[]{:S(2)}) %collective-permute-start.4) | collective-permute-done | bytes 57376 | tf_op jit(solution)/shard_map/ppermute | solution.py:365
  16.4 0.0 copy-done
  16.4 1.5 %collective-permute-start.7 = (f32[72,128]{1,0:T(8,128)S(1)}, f32[72,128]{1,0:T(8,128)S(1)}, u32[]{:S(2)}, u32[]{:S(2)}) collective-permute-start(f32[72,128]{1,0:T(8,128)S(1)} %get-tuple-element.23), channel_id=1, source_target_pairs={{0,2},{1,13},{2,0},{3,15},{4,6},{5,9},{6,4},{7,11},{8,10},{9,5},{1... | collective-permute-start | bytes 110600 | tf_op jit(solution)/shard_map/ppermute | solution.py:365
  18.0 0.5 %collective-permute-start.6 = (f32[72,128]{1,0:T(8,128)S(1)}, f32[72,128]{1,0:T(8,128)S(1)}, u32[]{:S(2)}, u32[]{:S(2)}) collective-permute-start(f32[72,128]{1,0:T(8,128)S(1)} %get-tuple-element.23), channel_id=1, source_target_pairs={{0,2},{1,9},{2,0},{3,11},{4,6},{5,13},{6,4},{7,15},{8,10},{9,1},{1... | collective-permute-start | bytes 110600 | tf_op jit(solution)/shard_map/ppermute | solution.py:365
  18.4 1.5 %collective-permute-start.5 = (f32[72,128]{1,0:T(8,128)S(1)}, f32[72,128]{1,0:T(8,128)S(1)}, u32[]{:S(2)}, u32[]{:S(2)}) collective-permute-start(f32[72,128]{1,0:T(8,128)S(1)} %get-tuple-element.23), channel_id=1, source_target_pairs={{0,2},{1,5},{2,0},{3,7},{4,6},{5,1},{6,4},{7,3},{8,10},{9,13},{10,... | collective-permute-start | bytes 110600 | tf_op jit(solution)/shard_map/ppermute | solution.py:365
  20.0 0.4 %collective-permute-done.7 = f32[72,128]{1,0:T(8,128)S(1)} collective-permute-done((f32[72,128]{1,0:T(8,128)S(1)}, f32[72,128]{1,0:T(8,128)S(1)}, u32[]{:S(2)}, u32[]{:S(2)}) %collective-permute-start.7) | collective-permute-done | bytes 36896 | tf_op jit(solution)/shard_map/ppermute | solution.py:365
  20.4 1.5 %collective-permute-done.6 = f32[72,128]{1,0:T(8,128)S(1)} collective-permute-done((f32[72,128]{1,0:T(8,128)S(1)}, f32[72,128]{1,0:T(8,128)S(1)}, u32[]{:S(2)}, u32[]{:S(2)}) %collective-permute-start.6) | collective-permute-done | bytes 36896 | tf_op jit(solution)/shard_map/ppermute | solution.py:365
  21.9 0.5 %collective-permute-done.5 = f32[72,128]{1,0:T(8,128)S(1)} collective-permute-done((f32[72,128]{1,0:T(8,128)S(1)}, f32[72,128]{1,0:T(8,128)S(1)}, u32[]{:S(2)}, u32[]{:S(2)}) %collective-permute-start.5) | collective-permute-done | bytes 36896 | tf_op jit(solution)/shard_map/ppermute | solution.py:365
  22.4 1.6 %collective-permute-start.8 = (f32[72,128]{1,0:T(8,128)S(1)}, f32[72,128]{1,0:T(8,128)S(1)}, u32[]{:S(2)}, u32[]{:S(2)}) collective-permute-start(f32[72,128]{1,0:T(8,128)S(1)} %add_add_fusion.rest_0_), channel_id=1, source_target_pairs={{0,2},{1,17},{2,0},{3,19},{4,6},{5,21},{6,4},{7,23},{8,10},{9,25},... | collective-permute-start | bytes 110600 | tf_op jit(solution)/shard_map/ppermute | solution.py:365
  24.0 2.4 %collective-permute-done.8.rest_1_ = f32[72,128]{1,0:T(8,128)S(1)} collective-permute-done((f32[72,128]{1,0:T(8,128)S(1)}, f32[72,128]{1,0:T(8,128)S(1)}, u32[]{:S(2)}, u32[]{:S(2)}) %collective-permute-start.8) | collective-permute-done | bytes 36896 | tf_op jit(solution)/shard_map/ppermute | solution.py:365
  26.4 1.5 %collective-permute-start.9 = (f32[2,768]{1,0:T(2,128)S(1)}, f32[2,768]{1,0:T(2,128)S(1)}, u32[]{:S(2)}, u32[]{:S(2)}) collective-permute-start(f32[2,768]{1,0:T(2,128)S(1)} %get-tuple-element.29), channel_id=1, source_target_pairs={{0,1},{1,0},{2,3},{3,2},{4,5},{5,4},{6,7},{7,6},{8,9},{9,8},{10,11... | collective-permute-start | bytes 18440 | tf_op jit(solution)/shard_map/ppermute | solution.py:352
  27.9 0.8 %collective-permute-done.9.got_ref = f32[2,768]{1,0:T(2,128)S(1)} collective-permute-done((f32[2,768]{1,0:T(2,128)S(1)}, f32[2,768]{1,0:T(2,128)S(1)}, u32[]{:S(2)}, u32[]{:S(2)}) %collective-permute-start.9) | collective-permute-done | bytes 6176 | tf_op jit(solution)/shard_map/ppermute | solution.py:352
  28.7 0.6 %finish.1 = (f32[2,256]{1,0:T(2,128)}, f32[2,512]{1,0:T(2,128)}) custom-call(f32[2,768]{1,0:T(2,128)S(1)} %get-tuple-element.28.mine_ref, f32[2,768]{1,0:T(2,128)S(1)} %collective-permute-done.9.got_ref), custom_call_target="tpu_custom_call" | custom-call | tf_op jit(solution)/shard_map/finish/pallas_call | solution.py:498
  (7 shorter events, 0.0 us)
Async XLA Ops:
  2.1 3.2 %collective-permute-start = (f32[2,1024]{1,0:T(2,128)S(1)}, f32[2,1024]{1,0:T(2,128)S(1)}, u32[]{:S(2)}, u32[]{:S(2)}) collective-permute-start(f32[2,1024]{1,0:T(2,128)S(1)} %get-tuple-element.20.mine_ref), channel_id=1, source_target_pairs={{0,1},{1,0},{2,3},{3,2},{4,5},{5,4},{6,7},{7,6},{8,9},{9,8},{10,11... | collective-permute-start | bytes 24584 | tf_op jit(solution)/shard_map/ppermute | solution.py:352
  5.3 4.4 %collective-permute-start.3 = (f32[88,128]{1,0:T(8,128)S(1)}, f32[88,128]{1,0:T(8,128)S(1)}, u32[]{:S(2)}, u32[]{:S(2)}) collective-permute-start(f32[88,128]{1,0:T(8,128)S(1)} %get-tuple-element.21.refs_0_), channel_id=1, source_target_pairs={{0,2},{1,13},{2,0},{3,15},{4,6},{5,9},{6,4},{7,11},{8,10},{9,5},{1... | collective-permute-start | bytes 135176 | tf_op jit(solution)/shard_map/ppermute | solution.py:365
  7.6 4.0 %collective-permute-start.2 = (f32[88,128]{1,0:T(8,128)S(1)}, f32[88,128]{1,0:T(8,128)S(1)}, u32[]{:S(2)}, u32[]{:S(2)}) collective-permute-start(f32[88,128]{1,0:T(8,128)S(1)} %get-tuple-element.21.refs_0_), channel_id=1, source_target_pairs={{0,2},{1,9},{2,0},{3,11},{4,6},{5,13},{6,4},{7,15},{8,10},{9,1},{1... | collective-permute-start | bytes 135176 | tf_op jit(solution)/shard_map/ppermute | solution.py:365
  7.6 4.5 %collective-permute-start.1 = (f32[88,128]{1,0:T(8,128)S(1)}, f32[88,128]{1,0:T(8,128)S(1)}, u32[]{:S(2)}, u32[]{:S(2)}) collective-permute-start(f32[88,128]{1,0:T(8,128)S(1)} %get-tuple-element.21.refs_0_), channel_id=1, source_target_pairs={{0,2},{1,5},{2,0},{3,7},{4,6},{5,1},{6,4},{7,3},{8,10},{9,13},{10,... | collective-permute-start | bytes 135176 | tf_op jit(solution)/shard_map/ppermute | solution.py:365
  12.2 4.3 %copy-start = (f32[512]{0:T(512)S(1)}, f32[512]{0:T(512)}, u32[]{:S(2)}) copy-start(f32[512]{0:T(512)} %param.13) | copy-start | bytes 6148
  12.2 4.2 %collective-permute-start.4 = (f32[112,128]{1,0:T(8,128)S(1)}, f32[112,128]{1,0:T(8,128)S(1)}, u32[]{:S(2)}, u32[]{:S(2)}) collective-permute-start(f32[112,128]{1,0:T(8,128)S(1)} %merge.1.rest_0_), channel_id=1, source_target_pairs={{0,2},{1,17},{2,0},{3,19},{4,6},{5,21},{6,4},{7,23},{8,10},{9,25},... | collective-permute-start | bytes 172040 | tf_op jit(solution)/shard_map/ppermute | solution.py:365
  16.4 4.0 %collective-permute-start.7 = (f32[72,128]{1,0:T(8,128)S(1)}, f32[72,128]{1,0:T(8,128)S(1)}, u32[]{:S(2)}, u32[]{:S(2)}) collective-permute-start(f32[72,128]{1,0:T(8,128)S(1)} %get-tuple-element.23), channel_id=1, source_target_pairs={{0,2},{1,13},{2,0},{3,15},{4,6},{5,9},{6,4},{7,11},{8,10},{9,5},{1... | collective-permute-start | bytes 110600 | tf_op jit(solution)/shard_map/ppermute | solution.py:365
  18.0 4.0 %collective-permute-start.6 = (f32[72,128]{1,0:T(8,128)S(1)}, f32[72,128]{1,0:T(8,128)S(1)}, u32[]{:S(2)}, u32[]{:S(2)}) collective-permute-start(f32[72,128]{1,0:T(8,128)S(1)} %get-tuple-element.23), channel_id=1, source_target_pairs={{0,2},{1,9},{2,0},{3,11},{4,6},{5,13},{6,4},{7,15},{8,10},{9,1},{1... | collective-permute-start | bytes 110600 | tf_op jit(solution)/shard_map/ppermute | solution.py:365
  18.4 4.0 %collective-permute-start.5 = (f32[72,128]{1,0:T(8,128)S(1)}, f32[72,128]{1,0:T(8,128)S(1)}, u32[]{:S(2)}, u32[]{:S(2)}) collective-permute-start(f32[72,128]{1,0:T(8,128)S(1)} %get-tuple-element.23), channel_id=1, source_target_pairs={{0,2},{1,5},{2,0},{3,7},{4,6},{5,1},{6,4},{7,3},{8,10},{9,13},{10,... | collective-permute-start | bytes 110600 | tf_op jit(solution)/shard_map/ppermute | solution.py:365
  22.4 4.0 %collective-permute-start.8 = (f32[72,128]{1,0:T(8,128)S(1)}, f32[72,128]{1,0:T(8,128)S(1)}, u32[]{:S(2)}, u32[]{:S(2)}) collective-permute-start(f32[72,128]{1,0:T(8,128)S(1)} %add_add_fusion.rest_0_), channel_id=1, source_target_pairs={{0,2},{1,17},{2,0},{3,19},{4,6},{5,21},{6,4},{7,23},{8,10},{9,25},... | collective-permute-start | bytes 110600 | tf_op jit(solution)/shard_map/ppermute | solution.py:365
  26.4 2.3 %collective-permute-start.9 = (f32[2,768]{1,0:T(2,128)S(1)}, f32[2,768]{1,0:T(2,128)S(1)}, u32[]{:S(2)}, u32[]{:S(2)}) collective-permute-start(f32[2,768]{1,0:T(2,128)S(1)} %get-tuple-element.29), channel_id=1, source_target_pairs={{0,1},{1,0},{2,3},{3,2},{4,5},{5,4},{6,7},{7,6},{8,9},{9,8},{10,11... | collective-permute-start | bytes 18440 | tf_op jit(solution)/shard_map/ppermute | solution.py:352

commit v5 on v4

--- a/solution.py
+++ b/solution.py
@@ -13,7 +13,7 @@
 VECS = 4
 TERMS = 2
 KEPT = VECS * TERMS
-FETCH = 16
+FETCH = 8
 
 step_size = 0.0625
 
@@ -131,10 +131,11 @@
             ref = peak_refs[t % 2]
             ref[r] = jnp.maximum(ref[r], jnp.maximum(tile, -tile))
         for r in range(ROWBLK):
-            peak = jnp.maximum(even_ref[r], odd_ref[r]).astype(jnp.float32)
-            scale = lax.rsqrt(jnp.max(peak, axis=1, keepdims=True))
-            spread_ref[r] = jnp.broadcast_to(scale, (EDGE, EDGE))
-            rscale_ref[r : r + 1, :] = lax.rsqrt(jnp.max(peak.T, axis=0, keepdims=True))
+            peak = jnp.maximum(even_ref[r], odd_ref[r])
+            turned = jnp.max(peak.T.astype(jnp.float32), axis=0, keepdims=True)
+            rscale_ref[r : r + 1, :] = lax.rsqrt(turned)
+            peak = jnp.max(peak.astype(jnp.float32), axis=1, keepdims=True)
+            spread_ref[r] = lax.rsqrt(jnp.broadcast_to(peak, (EDGE, EDGE)))
         for copy in vectors:
             copy.wait()
 
@@ -200,7 +201,7 @@
     return peak, functools.reduce(jnp.add, [ref[rows, :] for ref in refs])
 
 
-def merge_kernel(blocks, *refs):
+def merge_kernel(blocks, turned_ref, *refs):
     refs, out_ref = refs[:-1], refs[-1]
     head = (1 + VECS) * blocks
     peak, total = combined(refs, blocks)
@@ -373,7 +374,7 @@
         else:
             rounds.append((bit,))
         bit *= 4
-    return rounds
+    return rounds[::-1]
 
 
 def shards(tiles, tile_row, tile_col, tile_count, cost, bound_vec, x_start, y_start):
@@ -460,11 +461,11 @@
             message = pl.pallas_call(
                 functools.partial(merge_kernel, blocks),
                 out_shape=f32((1 + VECS) * blocks + COLBLK * VECS * len(offsets), EDGE),
-                in_specs=vmem(len(messages)),
+                in_specs=vmem(1 + len(messages)),
                 out_specs=vmem(1)[0],
                 compiler_params=params,
                 name="merge",
-            )(*messages)
+            )(turned, *messages)
 
     message, x_one, cscale, y_one, moved = pl.pallas_call(
         functools.partial(step_kernel, offsets, len(messages)),

time: 29.5 us -> 29.2 us (0.990)
  waiting for transfers between devices: 11.6 us -> 11.2 us
    ppermute x8, waiting for transfers between devices: 9.96 us -> 9.52 us  [from_band(): return lax.ppermute(value, ('band', 'batch'), pairs)]
where the time goes in v5:
time: 29.2 us; the launch traced here: 29 us
  starting transfers between devices  15 us (51%)
  waiting for transfers between devices  11.2 us (38%)
  Pallas kernels  1.54 us (5%)
  between operations  1.3 us (4%)
    ppermute x8, starting transfers between devices, from_band(): return lax.ppermute(value, ('band', 'batch'), pairs)  11.4 us
    ppermute x8, waiting for transfers between devices, from_band(): return lax.ppermute(value, ('band', 'batch'), pairs)  9.52 us
    ppermute x2, starting transfers between devices, swap(): return lax.ppermute(value, 'batch', [(i, i ^ 1) for i in range(count)])  3.6 us
    ppermute x2, waiting for transfers between devices, swap(): return lax.ppermute(value, 'batch', [(i, i ^ 1) for i in range(count)])  1.65 us
    pallas_call x1, Pallas kernels, shards(): pl.pallas_call(scale_kernel, out_shape=(pltpu.SMEM((2, ntile), jnp.int32)...  0.92 us
    pallas_call x1, Pallas kernels, shards(): pl.pallas_call(finish_kernel, out_shape=(f32(*x_start.shape), f32(*y_star...  0.61 us
  transfers between devices with their start and end apart: 10, of which 9 were waited for; matrix products, arithmetic and copies ran while one was open for 0% of the time, Pallas kernels for 0%

profile of v5, /device:TPU:0, one launch (start us, length us, event | category | flops | bytes accessed | tf_op | source)
XLA Modules:
  0.0 29.0 jit_solution(6367721278192322378)
XLA Ops:
  1.3 0.9 %row_scales.1 = (s32[2,128]{1,0:T(2,128)S(4)}, f32[2,1024]{1,0:T(2,128)S(1)}, bf16[128,128,128]{2,1,0:T(8,128)(2,1)S(1)}, f32[5,128,128]{2,1,0:T(8,128)S(1)}, f32[4,128]{1,0:T(4,128)S(1)}) custom-call(s32[1,128]{1,0:T(1,128)} %rows_ref.1, s32[1,128]{1,0:T(1,128)} %cols_ref.1, s32[1]{0:T(128)S(6)} %copy.10.count_ref, f32[2,512]{1,0:T(2,128)} %y_ref.1, ...), custom_call_target="tpu_custom_call" | custom-call | bytes 4194304 | tf_op jit(solution)/shard_map/row_scales/pallas_call | solution.py:401
  2.2 2.2 %collective-permute-start = (f32[2,1024]{1,0:T(2,128)S(1)}, f32[2,1024]{1,0:T(2,128)S(1)}, u32[]{:S(2)}, u32[]{:S(2)}) collective-permute-start(f32[2,1024]{1,0:T(2,128)S(1)} %get-tuple-element.20.mine_ref), channel_id=1, source_target_pairs={{0,1},{1,0},{2,3},{3,2},{4,5},{5,4},{6,7},{7,6},{8,9},{9,8},{10,11... | collective-permute-start | bytes 24584 | tf_op jit(solution)/shard_map/ppermute | solution.py:353
  4.4 0.8 %collective-permute-done.other_ref = f32[2,1024]{1,0:T(2,128)S(1)} collective-permute-done((f32[2,1024]{1,0:T(2,128)S(1)}, f32[2,1024]{1,0:T(2,128)S(1)}, u32[]{:S(2)}, u32[]{:S(2)}) %collective-permute-start) | collective-permute-done | bytes 8224 | tf_op jit(solution)/shard_map/ppermute | solution.py:353
  5.2 2.3 %collective-permute-start.1 = (f32[88,128]{1,0:T(8,128)S(1)}, f32[88,128]{1,0:T(8,128)S(1)}, u32[]{:S(2)}, u32[]{:S(2)}) collective-permute-start(f32[88,128]{1,0:T(8,128)S(1)} %get-tuple-element.21.refs_0_), channel_id=1, source_target_pairs={{0,2},{1,17},{2,0},{3,19},{4,6},{5,21},{6,4},{7,23},{8,10},{9,25},... | collective-permute-start | bytes 135176 | tf_op jit(solution)/shard_map/ppermute | solution.py:366
  7.6 0.0 copy-start
  7.6 2.0 %collective-permute-done.1.refs_1_ = f32[88,128]{1,0:T(8,128)S(1)} collective-permute-done((f32[88,128]{1,0:T(8,128)S(1)}, f32[88,128]{1,0:T(8,128)S(1)}, u32[]{:S(2)}, u32[]{:S(2)}) %collective-permute-start.1) | collective-permute-done | bytes 45088 | tf_op jit(solution)/shard_map/ppermute | solution.py:366
  9.6 2.0 %collective-permute-start.4 = (f32[96,128]{1,0:T(8,128)S(1)}, f32[96,128]{1,0:T(8,128)S(1)}, u32[]{:S(2)}, u32[]{:S(2)}) collective-permute-start(f32[96,128]{1,0:T(8,128)S(1)} %merge.1.rest_0_), channel_id=1, source_target_pairs={{0,2},{1,13},{2,0},{3,15},{4,6},{5,9},{6,4},{7,11},{8,10},{9,5},{1... | collective-permute-start | bytes 147464 | tf_op jit(solution)/shard_map/ppermute | solution.py:366
  11.6 0.1 collective-permute-start.3
  11.7 2.0 %collective-permute-start.2 = (f32[96,128]{1,0:T(8,128)S(1)}, f32[96,128]{1,0:T(8,128)S(1)}, u32[]{:S(2)}, u32[]{:S(2)}) collective-permute-start(f32[96,128]{1,0:T(8,128)S(1)} %merge.1.rest_0_), channel_id=1, source_target_pairs={{0,2},{1,5},{2,0},{3,7},{4,6},{5,1},{6,4},{7,3},{8,10},{9,13},{10,... | collective-permute-start | bytes 147464 | tf_op jit(solution)/shard_map/ppermute | solution.py:366
  13.6 0.0 collective-permute-done.4.rest_3_
  13.7 2.0 %collective-permute-done.3.rest_2_ = f32[96,128]{1,0:T(8,128)S(1)} collective-permute-done((f32[96,128]{1,0:T(8,128)S(1)}, f32[96,128]{1,0:T(8,128)S(1)}, u32[]{:S(2)}, u32[]{:S(2)}) %collective-permute-start.3) | collective-permute-done | bytes 49184 | tf_op jit(solution)/shard_map/ppermute | solution.py:366
  15.7 0.5 %collective-permute-done.2.rest_1_ = f32[96,128]{1,0:T(8,128)S(1)} collective-permute-done((f32[96,128]{1,0:T(8,128)S(1)}, f32[96,128]{1,0:T(8,128)S(1)}, u32[]{:S(2)}, u32[]{:S(2)}) %collective-permute-start.2) | collective-permute-done | bytes 49184 | tf_op jit(solution)/shard_map/ppermute | solution.py:366
  16.2 0.0 copy-done
  16.2 1.5 %collective-permute-start.5 = (f32[72,128]{1,0:T(8,128)S(1)}, f32[72,128]{1,0:T(8,128)S(1)}, u32[]{:S(2)}, u32[]{:S(2)}) collective-permute-start(f32[72,128]{1,0:T(8,128)S(1)} %get-tuple-element.23), channel_id=1, source_target_pairs={{0,2},{1,17},{2,0},{3,19},{4,6},{5,21},{6,4},{7,23},{8,10},{9,25},... | collective-permute-start | bytes 110600 | tf_op jit(solution)/shard_map/ppermute | solution.py:366
  17.7 2.5 %collective-permute-done.5 = f32[72,128]{1,0:T(8,128)S(1)} collective-permute-done((f32[72,128]{1,0:T(8,128)S(1)}, f32[72,128]{1,0:T(8,128)S(1)}, u32[]{:S(2)}, u32[]{:S(2)}) %collective-permute-start.5) | collective-permute-done | bytes 36896 | tf_op jit(solution)/shard_map/ppermute | solution.py:366
  20.2 1.5 %collective-permute-start.8 = (f32[72,128]{1,0:T(8,128)S(1)}, f32[72,128]{1,0:T(8,128)S(1)}, u32[]{:S(2)}, u32[]{:S(2)}) collective-permute-start(f32[72,128]{1,0:T(8,128)S(1)} %add.3.rest_0_), channel_id=1, source_target_pairs={{0,2},{1,13},{2,0},{3,15},{4,6},{5,9},{6,4},{7,11},{8,10},{9,5},{1... | collective-permute-start | bytes 110600 | tf_op jit(solution)/shard_map/ppermute | solution.py:366
  21.7 0.5 %collective-permute-start.7 = (f32[72,128]{1,0:T(8,128)S(1)}, f32[72,128]{1,0:T(8,128)S(1)}, u32[]{:S(2)}, u32[]{:S(2)}) collective-permute-start(f32[72,128]{1,0:T(8,128)S(1)} %add.3.rest_0_), channel_id=1, source_target_pairs={{0,2},{1,9},{2,0},{3,11},{4,6},{5,13},{6,4},{7,15},{8,10},{9,1},{1... | collective-permute-start | bytes 110600 | tf_op jit(solution)/shard_map/ppermute | solution.py:366
  22.2 1.5 %collective-permute-start.6 = (f32[72,128]{1,0:T(8,128)S(1)}, f32[72,128]{1,0:T(8,128)S(1)}, u32[]{:S(2)}, u32[]{:S(2)}) collective-permute-start(f32[72,128]{1,0:T(8,128)S(1)} %add.3.rest_0_), channel_id=1, source_target_pairs={{0,2},{1,5},{2,0},{3,7},{4,6},{5,1},{6,4},{7,3},{8,10},{9,13},{10,... | collective-permute-start | bytes 110600 | tf_op jit(solution)/shard_map/ppermute | solution.py:366
  23.7 0.4 %collective-permute-done.8.rest_3_ = f32[72,128]{1,0:T(8,128)S(1)} collective-permute-done((f32[72,128]{1,0:T(8,128)S(1)}, f32[72,128]{1,0:T(8,128)S(1)}, u32[]{:S(2)}, u32[]{:S(2)}) %collective-permute-start.8) | collective-permute-done | bytes 36896 | tf_op jit(solution)/shard_map/ppermute | solution.py:366
  24.2 1.5 %collective-permute-done.7.rest_2_ = f32[72,128]{1,0:T(8,128)S(1)} collective-permute-done((f32[72,128]{1,0:T(8,128)S(1)}, f32[72,128]{1,0:T(8,128)S(1)}, u32[]{:S(2)}, u32[]{:S(2)}) %collective-permute-start.7) | collective-permute-done | bytes 36896 | tf_op jit(solution)/shard_map/ppermute | solution.py:366
  25.7 0.5 %collective-permute-done.6.rest_1_ = f32[72,128]{1,0:T(8,128)S(1)} collective-permute-done((f32[72,128]{1,0:T(8,128)S(1)}, f32[72,128]{1,0:T(8,128)S(1)}, u32[]{:S(2)}, u32[]{:S(2)}) %collective-permute-start.6) | collective-permute-done | bytes 36896 | tf_op jit(solution)/shard_map/ppermute | solution.py:366
  26.2 1.4 %collective-permute-start.9 = (f32[2,768]{1,0:T(2,128)S(1)}, f32[2,768]{1,0:T(2,128)S(1)}, u32[]{:S(2)}, u32[]{:S(2)}) collective-permute-start(f32[2,768]{1,0:T(2,128)S(1)} %get-tuple-element.29), channel_id=1, source_target_pairs={{0,1},{1,0},{2,3},{3,2},{4,5},{5,4},{6,7},{7,6},{8,9},{9,8},{10,11... | collective-permute-start | bytes 18440 | tf_op jit(solution)/shard_map/ppermute | solution.py:353
  27.6 0.8 %collective-permute-done.9.got_ref = f32[2,768]{1,0:T(2,128)S(1)} collective-permute-done((f32[2,768]{1,0:T(2,128)S(1)}, f32[2,768]{1,0:T(2,128)S(1)}, u32[]{:S(2)}, u32[]{:S(2)}) %collective-permute-start.9) | collective-permute-done | bytes 6176 | tf_op jit(solution)/shard_map/ppermute | solution.py:353
  28.4 0.6 %finish.1 = (f32[2,256]{1,0:T(2,128)}, f32[2,512]{1,0:T(2,128)}) custom-call(f32[2,768]{1,0:T(2,128)S(1)} %get-tuple-element.28.mine_ref, f32[2,768]{1,0:T(2,128)S(1)} %collective-permute-done.9.got_ref), custom_call_target="tpu_custom_call" | custom-call | tf_op jit(solution)/shard_map/finish/pallas_call | solution.py:499
  (7 shorter events, 0.0 us)
Async XLA Ops:
  2.2 3.0 %collective-permute-start = (f32[2,1024]{1,0:T(2,128)S(1)}, f32[2,1024]{1,0:T(2,128)S(1)}, u32[]{:S(2)}, u32[]{:S(2)}) collective-permute-start(f32[2,1024]{1,0:T(2,128)S(1)} %get-tuple-element.20.mine_ref), channel_id=1, source_target_pairs={{0,1},{1,0},{2,3},{3,2},{4,5},{5,4},{6,7},{7,6},{8,9},{9,8},{10,11... | collective-permute-start | bytes 24584 | tf_op jit(solution)/shard_map/ppermute | solution.py:353
  5.2 4.3 %collective-permute-start.1 = (f32[88,128]{1,0:T(8,128)S(1)}, f32[88,128]{1,0:T(8,128)S(1)}, u32[]{:S(2)}, u32[]{:S(2)}) collective-permute-start(f32[88,128]{1,0:T(8,128)S(1)} %get-tuple-element.21.refs_0_), channel_id=1, source_target_pairs={{0,2},{1,17},{2,0},{3,19},{4,6},{5,21},{6,4},{7,23},{8,10},{9,25},... | collective-permute-start | bytes 135176 | tf_op jit(solution)/shard_map/ppermute | solution.py:366
  7.6 8.7 %copy-start = (f32[512]{0:T(512)S(1)}, f32[512]{0:T(512)}, u32[]{:S(2)}) copy-start(f32[512]{0:T(512)} %param.13) | copy-start | bytes 6148
  9.6 4.1 %collective-permute-start.4 = (f32[96,128]{1,0:T(8,128)S(1)}, f32[96,128]{1,0:T(8,128)S(1)}, u32[]{:S(2)}, u32[]{:S(2)}) collective-permute-start(f32[96,128]{1,0:T(8,128)S(1)} %merge.1.rest_0_), channel_id=1, source_target_pairs={{0,2},{1,13},{2,0},{3,15},{4,6},{5,9},{6,4},{7,11},{8,10},{9,5},{1... | collective-permute-start | bytes 147464 | tf_op jit(solution)/shard_map/ppermute | solution.py:366
  11.6 4.1 %collective-permute-start.3 = (f32[96,128]{1,0:T(8,128)S(1)}, f32[96,128]{1,0:T(8,128)S(1)}, u32[]{:S(2)}, u32[]{:S(2)}) collective-permute-start(f32[96,128]{1,0:T(8,128)S(1)} %merge.1.rest_0_), channel_id=1, source_target_pairs={{0,2},{1,9},{2,0},{3,11},{4,6},{5,13},{6,4},{7,15},{8,10},{9,1},{1... | collective-permute-start | bytes 147464 | tf_op jit(solution)/shard_map/ppermute | solution.py:366
  11.7 4.5 %collective-permute-start.2 = (f32[96,128]{1,0:T(8,128)S(1)}, f32[96,128]{1,0:T(8,128)S(1)}, u32[]{:S(2)}, u32[]{:S(2)}) collective-permute-start(f32[96,128]{1,0:T(8,128)S(1)} %merge.1.rest_0_), channel_id=1, source_target_pairs={{0,2},{1,5},{2,0},{3,7},{4,6},{5,1},{6,4},{7,3},{8,10},{9,13},{10,... | collective-permute-start | bytes 147464 | tf_op jit(solution)/shard_map/ppermute | solution.py:366
  16.2 4.0 %collective-permute-start.5 = (f32[72,128]{1,0:T(8,128)S(1)}, f32[72,128]{1,0:T(8,128)S(1)}, u32[]{:S(2)}, u32[]{:S(2)}) collective-permute-start(f32[72,128]{1,0:T(8,128)S(1)} %get-tuple-element.23), channel_id=1, source_target_pairs={{0,2},{1,17},{2,0},{3,19},{4,6},{5,21},{6,4},{7,23},{8,10},{9,25},... | collective-permute-start | bytes 110600 | tf_op jit(solution)/shard_map/ppermute | solution.py:366
  20.2 4.0 %collective-permute-start.8 = (f32[72,128]{1,0:T(8,128)S(1)}, f32[72,128]{1,0:T(8,128)S(1)}, u32[]{:S(2)}, u32[]{:S(2)}) collective-permute-start(f32[72,128]{1,0:T(8,128)S(1)} %add.3.rest_0_), channel_id=1, source_target_pairs={{0,2},{1,13},{2,0},{3,15},{4,6},{5,9},{6,4},{7,11},{8,10},{9,5},{1... | collective-permute-start | bytes 110600 | tf_op jit(solution)/shard_map/ppermute | solution.py:366
  21.7 4.0 %collective-permute-start.7 = (f32[72,128]{1,0:T(8,128)S(1)}, f32[72,128]{1,0:T(8,128)S(1)}, u32[]{:S(2)}, u32[]{:S(2)}) collective-permute-start(f32[72,128]{1,0:T(8,128)S(1)} %add.3.rest_0_), channel_id=1, source_target_pairs={{0,2},{1,9},{2,0},{3,11},{4,6},{5,13},{6,4},{7,15},{8,10},{9,1},{1... | collective-permute-start | bytes 110600 | tf_op jit(solution)/shard_map/ppermute | solution.py:366
  22.2 4.0 %collective-permute-start.6 = (f32[72,128]{1,0:T(8,128)S(1)}, f32[72,128]{1,0:T(8,128)S(1)}, u32[]{:S(2)}, u32[]{:S(2)}) collective-permute-start(f32[72,128]{1,0:T(8,128)S(1)} %add.3.rest_0_), channel_id=1, source_target_pairs={{0,2},{1,5},{2,0},{3,7},{4,6},{5,1},{6,4},{7,3},{8,10},{9,13},{10,... | collective-permute-start | bytes 110600 | tf_op jit(solution)/shard_map/ppermute | solution.py:366
  26.2 2.2 %collective-permute-start.9 = (f32[2,768]{1,0:T(2,128)S(1)}, f32[2,768]{1,0:T(2,128)S(1)}, u32[]{:S(2)}, u32[]{:S(2)}) collective-permute-start(f32[2,768]{1,0:T(2,128)S(1)} %get-tuple-element.29), channel_id=1, source_target_pairs={{0,1},{1,0},{2,3},{3,2},{4,5},{5,4},{6,7},{7,6},{8,9},{9,8},{10,11... | collective-permute-start | bytes 18440 | tf_op jit(solution)/shard_map/ppermute | solution.py:353

commit v6 on v5

--- a/solution.py
+++ b/solution.py
@@ -201,7 +201,7 @@
     return peak, functools.reduce(jnp.add, [ref[rows, :] for ref in refs])
 
 
-def merge_kernel(blocks, turned_ref, *refs):
+def merge_kernel(blocks, *refs):
     refs, out_ref = refs[:-1], refs[-1]
     head = (1 + VECS) * blocks
     peak, total = combined(refs, blocks)
@@ -353,17 +353,18 @@
     return lax.ppermute(value, "batch", [(i, i ^ 1) for i in range(count)])
 
 
-def from_band(value, hop):
+def relayed(value, hop, side):
     bands, batches = lax.axis_size("band"), lax.axis_size("batch")
     pairs = []
     for band in range(bands):
         for batch in range(batches):
-            if batch % 2 == 1:
-                to = (band ^ hop) * batches + batch
-            else:
-                to = band * batches + (batch + 2) % batches if batches % 4 == 0 else (band ^ hop) * batches + batch
-            pairs.append((band * batches + batch, to))
+            to = band ^ hop if batch % 2 == side else band
+            pairs.append((band * batches + batch, to * batches + (batch ^ 1)))
     return lax.ppermute(value, ("band", "batch"), pairs)
+
+
+def gathered(value, hops, side):
+    return [swap(value)] + [relayed(value, hop, side) for hop in hops]
 
 
 def rounds_of(bands):
@@ -374,7 +375,7 @@
         else:
             rounds.append((bit,))
         bit *= 4
-    return rounds[::-1]
+    return rounds if len(rounds) % 2 == 0 else rounds + [()]
 
 
 def shards(tiles, tile_row, tile_col, tile_count, cost, bound_vec, x_start, y_start):
@@ -455,17 +456,17 @@
     rounds = rounds_of(bands)
     offsets = [0]
     for index, hops in enumerate(rounds):
-        messages = [message] + [from_band(message, hop) for hop in hops]
+        messages = gathered(message, hops, (index + 1) % 2)
         offsets = [hop ^ offset for hop in (0, *hops) for offset in offsets]
         if index < len(rounds) - 1:
             message = pl.pallas_call(
                 functools.partial(merge_kernel, blocks),
                 out_shape=f32((1 + VECS) * blocks + COLBLK * VECS * len(offsets), EDGE),
-                in_specs=vmem(1 + len(messages)),
+                in_specs=vmem(len(messages)),
                 out_specs=vmem(1)[0],
                 compiler_params=params,
                 name="merge",
-            )(turned, *messages)
+            )(*messages)
 
     message, x_one, cscale, y_one, moved = pl.pallas_call(
         functools.partial(step_kernel, offsets, len(messages)),
@@ -480,7 +481,7 @@
     )(meta, tile_count, held, turned, *messages, rscale, both, bound)
 
     for index, hops in enumerate(rounds):
-        messages = [message] + [from_band(message, hop) for hop in hops]
+        messages = gathered(message, hops, (index + 1) % 2)
         if index < len(rounds) - 1:
             message = functools.reduce(jnp.add, messages)
 

time: 29.2 us -> 27.4 us (0.938)
  starting transfers between devices: 15 us -> 13.6 us
  waiting for transfers between devices: 11.2 us -> 10.7 us
    ppermute x8, starting transfers between devices: 11.4 us -> 8.88 us  [relayed(): return lax.ppermute(value, ('band', 'batch'), pairs)]
    ppermute x2 -> x6, starting transfers between devices: 3.6 us -> 4.69 us  [swap(): return lax.ppermute(value, 'batch', [(i, i ^ 1) for i in range(count)])]
    ppermute x8, waiting for transfers between devices: 9.52 us -> 9.04 us  [relayed(): return lax.ppermute(value, ('band', 'batch'), pairs)]
    ppermute x2 -> x6, waiting for transfers between devices: 1.65 us -> 1.66 us  [swap(): return lax.ppermute(value, 'batch', [(i, i ^ 1) for i in range(count)])]
  transfers between devices with their start and end apart: 10 -> 14, of which waited for: 9 -> 9; matrix products, arithmetic and copies ran while one was open for 0% -> 0% of each run, Pallas kernels for 0% -> 0%
where the time goes in v6:
time: 27.4 us; the launch traced here: 27.2 us
  starting transfers between devices  13.6 us (50%)
  waiting for transfers between devices  10.7 us (39%)
  Pallas kernels  1.55 us (6%)
  between operations  1.32 us (5%)
    ppermute x8, waiting for transfers between devices, relayed(): return lax.ppermute(value, ('band', 'batch'), pairs)  9.04 us
    ppermute x8, starting transfers between devices, relayed(): return lax.ppermute(value, ('band', 'batch'), pairs)  8.88 us
    ppermute x6, starting transfers between devices, swap(): return lax.ppermute(value, 'batch', [(i, i ^ 1) for i in range(count)])  4.69 us
    ppermute x6, waiting for transfers between devices, swap(): return lax.ppermute(value, 'batch', [(i, i ^ 1) for i in range(count)])  1.66 us
    pallas_call x1, Pallas kernels, shards(): pl.pallas_call(scale_kernel, out_shape=(pltpu.SMEM((2, ntile), jnp.int32)...  0.92 us
    pallas_call x1, Pallas kernels, shards(): pl.pallas_call(finish_kernel, out_shape=(f32(*x_start.shape), f32(*y_star...  0.61 us
  transfers between devices with their start and end apart: 14, of which 9 were waited for; matrix products, arithmetic and copies ran while one was open for 0% of the time, Pallas kernels for 0%

profile of v6, /device:TPU:0, one launch (start us, length us, event | category | flops | bytes accessed | tf_op | source)
XLA Modules:
  0.0 27.2 jit_solution(7239357566162899005)
XLA Ops:
  1.3 0.9 %row_scales.1 = (s32[2,128]{1,0:T(2,128)S(4)}, f32[2,1024]{1,0:T(2,128)S(1)}, bf16[128,128,128]{2,1,0:T(8,128)(2,1)S(1)}, f32[5,128,128]{2,1,0:T(8,128)S(1)}, f32[4,128]{1,0:T(4,128)S(1)}) custom-call(s32[1,128]{1,0:T(1,128)} %rows_ref.1, s32[1,128]{1,0:T(1,128)} %cols_ref.1, s32[1]{0:T(128)S(6)} %copy.10.count_ref, f32[2,512]{1,0:T(2,128)} %y_ref.1, ...), custom_call_target="tpu_custom_call" | custom-call | bytes 4194304 | tf_op jit(solution)/shard_map/row_scales/pallas_call | solution.py:402
  2.2 2.2 %collective-permute-start = (f32[2,1024]{1,0:T(2,128)S(1)}, f32[2,1024]{1,0:T(2,128)S(1)}, u32[]{:S(2)}, u32[]{:S(2)}) collective-permute-start(f32[2,1024]{1,0:T(2,128)S(1)} %get-tuple-element.20.mine_ref), channel_id=1, source_target_pairs={{0,1},{1,0},{2,3},{3,2},{4,5},{5,4},{6,7},{7,6},{8,9},{9,8},{10,11... | collective-permute-start | bytes 24584 | tf_op jit(solution)/shard_map/ppermute | solution.py:353
  4.4 0.8 %collective-permute-done.other_ref = f32[2,1024]{1,0:T(2,128)S(1)} collective-permute-done((f32[2,1024]{1,0:T(2,128)S(1)}, f32[2,1024]{1,0:T(2,128)S(1)}, u32[]{:S(2)}, u32[]{:S(2)}) %collective-permute-start) | collective-permute-done | bytes 8224 | tf_op jit(solution)/shard_map/ppermute | solution.py:353
  5.2 1.3 %collective-permute-start.4 = (f32[88,128]{1,0:T(8,128)S(1)}, f32[88,128]{1,0:T(8,128)S(1)}, u32[]{:S(2)}, u32[]{:S(2)}) collective-permute-start(f32[88,128]{1,0:T(8,128)S(1)} %get-tuple-element.21), channel_id=1, source_target_pairs={{0,1},{1,12},{2,3},{3,14},{4,5},{5,8},{6,7},{7,10},{8,9},{9,4},{10... | collective-permute-start | bytes 135176 | tf_op jit(solution)/shard_map/ppermute | solution.py:363
  6.6 2.2 %collective-permute-start.3 = (f32[88,128]{1,0:T(8,128)S(1)}, f32[88,128]{1,0:T(8,128)S(1)}, u32[]{:S(2)}, u32[]{:S(2)}) collective-permute-start(f32[88,128]{1,0:T(8,128)S(1)} %get-tuple-element.21), channel_id=1, source_target_pairs={{0,1},{1,8},{2,3},{3,10},{4,5},{5,12},{6,7},{7,14},{8,9},{9,0},{10... | collective-permute-start | bytes 135176 | tf_op jit(solution)/shard_map/ppermute | solution.py:363
  8.7 0.3 %collective-permute-start.2 = (f32[88,128]{1,0:T(8,128)S(1)}, f32[88,128]{1,0:T(8,128)S(1)}, u32[]{:S(2)}, u32[]{:S(2)}) collective-permute-start(f32[88,128]{1,0:T(8,128)S(1)} %get-tuple-element.21), channel_id=1, source_target_pairs={{0,1},{1,4},{2,3},{3,6},{4,5},{5,0},{6,7},{7,2},{8,9},{9,12},{10,1... | collective-permute-start | bytes 135176 | tf_op jit(solution)/shard_map/ppermute | solution.py:363
  9.0 0.3 %collective-permute-start.1 = (f32[88,128]{1,0:T(8,128)S(1)}, f32[88,128]{1,0:T(8,128)S(1)}, u32[]{:S(2)}, u32[]{:S(2)}) collective-permute-start(f32[88,128]{1,0:T(8,128)S(1)} %get-tuple-element.21), channel_id=1, source_target_pairs={{0,1},{1,0},{2,3},{3,2},{4,5},{5,4},{6,7},{7,6},{8,9},{9,8},{10,11... | collective-permute-start | bytes 135176 | tf_op jit(solution)/shard_map/ppermute | solution.py:353
  9.3 1.9 %collective-permute-done.4.refs_3_ = f32[88,128]{1,0:T(8,128)S(1)} collective-permute-done((f32[88,128]{1,0:T(8,128)S(1)}, f32[88,128]{1,0:T(8,128)S(1)}, u32[]{:S(2)}, u32[]{:S(2)}) %collective-permute-start.4) | collective-permute-done | bytes 45088 | tf_op jit(solution)/shard_map/ppermute | solution.py:363
  11.2 0.0 collective-permute-done.3.refs_2_
  11.3 0.9 %collective-permute-done.2.refs_1_ = f32[88,128]{1,0:T(8,128)S(1)} collective-permute-done((f32[88,128]{1,0:T(8,128)S(1)}, f32[88,128]{1,0:T(8,128)S(1)}, u32[]{:S(2)}, u32[]{:S(2)}) %collective-permute-start.2) | collective-permute-done | bytes 45088 | tf_op jit(solution)/shard_map/ppermute | solution.py:363
  12.2 0.0 collective-permute-done.1.refs_0_
  12.2 0.0 copy-start
  12.2 0.6 %collective-permute-start.6 = (f32[112,128]{1,0:T(8,128)S(1)}, f32[112,128]{1,0:T(8,128)S(1)}, u32[]{:S(2)}, u32[]{:S(2)}) collective-permute-start(f32[112,128]{1,0:T(8,128)S(1)} %merge.1), channel_id=1, source_target_pairs={{0,17},{1,0},{2,19},{3,2},{4,21},{5,4},{6,23},{7,6},{8,25},{9,8},{... | collective-permute-start | bytes 172040 | tf_op jit(solution)/shard_map/ppermute | solution.py:363
  12.8 0.0 collective-permute-start.5
  12.8 1.8 %collective-permute-done.6.rest_1_ = f32[112,128]{1,0:T(8,128)S(1)} collective-permute-done((f32[112,128]{1,0:T(8,128)S(1)}, f32[112,128]{1,0:T(8,128)S(1)}, u32[]{:S(2)}, u32[]{:S(2)}) %collective-permute-start.6) | collective-permute-done | bytes 57376 | tf_op jit(solution)/shard_map/ppermute | solution.py:363
  14.7 0.0 collective-permute-done.5.rest_0_
  14.7 0.0 copy-done
  14.7 4.3 %collective-permute-start.10 = (f32[72,128]{1,0:T(8,128)S(1)}, f32[72,128]{1,0:T(8,128)S(1)}, u32[]{:S(2)}, u32[]{:S(2)}) collective-permute-start(f32[72,128]{1,0:T(8,128)S(1)} %get-tuple-element.23), channel_id=1, source_target_pairs={{0,1},{1,12},{2,3},{3,14},{4,5},{5,8},{6,7},{7,10},{8,9},{9,4},{10... | collective-permute-start | bytes 110600 | tf_op jit(solution)/shard_map/ppermute | solution.py:363
  19.0 0.1 collective-permute-start.9
  19.0 0.1 collective-permute-start.8
  19.1 0.1 collective-permute-start.7
  19.2 1.8 %collective-permute-done.10 = f32[72,128]{1,0:T(8,128)S(1)} collective-permute-done((f32[72,128]{1,0:T(8,128)S(1)}, f32[72,128]{1,0:T(8,128)S(1)}, u32[]{:S(2)}, u32[]{:S(2)}) %collective-permute-start.10) | collective-permute-done | bytes 36896 | tf_op jit(solution)/shard_map/ppermute | solution.py:363
  21.0 1.4 %collective-permute-done.9 = f32[72,128]{1,0:T(8,128)S(1)} collective-permute-done((f32[72,128]{1,0:T(8,128)S(1)}, f32[72,128]{1,0:T(8,128)S(1)}, u32[]{:S(2)}, u32[]{:S(2)}) %collective-permute-start.9) | collective-permute-done | bytes 36896 | tf_op jit(solution)/shard_map/ppermute | solution.py:363
  22.3 0.1 collective-permute-done.8
  22.4 0.0 collective-permute-done.7
  22.4 0.1 collective-permute-start.12
  22.5 0.5 %collective-permute-start.11 = (f32[72,128]{1,0:T(8,128)S(1)}, f32[72,128]{1,0:T(8,128)S(1)}, u32[]{:S(2)}, u32[]{:S(2)}) collective-permute-start(f32[72,128]{1,0:T(8,128)S(1)} %add_add_fusion), channel_id=1, source_target_pairs={{0,1},{1,0},{2,3},{3,2},{4,5},{5,4},{6,7},{7,6},{8,9},{9,8},{10,11... | collective-permute-start | bytes 110600 | tf_op jit(solution)/shard_map/ppermute | solution.py:353
  23.0 1.1 %collective-permute-done.12.rest_1_ = f32[72,128]{1,0:T(8,128)S(1)} collective-permute-done((f32[72,128]{1,0:T(8,128)S(1)}, f32[72,128]{1,0:T(8,128)S(1)}, u32[]{:S(2)}, u32[]{:S(2)}) %collective-permute-start.12) | collective-permute-done | bytes 36896 | tf_op jit(solution)/shard_map/ppermute | solution.py:363
  24.1 0.0 collective-permute-done.11.rest_0_
  24.1 1.6 %collective-permute-start.13 = (f32[2,768]{1,0:T(2,128)S(1)}, f32[2,768]{1,0:T(2,128)S(1)}, u32[]{:S(2)}, u32[]{:S(2)}) collective-permute-start(f32[2,768]{1,0:T(2,128)S(1)} %get-tuple-element.29), channel_id=1, source_target_pairs={{0,1},{1,0},{2,3},{3,2},{4,5},{5,4},{6,7},{7,6},{8,9},{9,8},{10,11... | collective-permute-start | bytes 18440 | tf_op jit(solution)/shard_map/ppermute | solution.py:353
  25.7 0.8 %collective-permute-done.13.got_ref = f32[2,768]{1,0:T(2,128)S(1)} collective-permute-done((f32[2,768]{1,0:T(2,128)S(1)}, f32[2,768]{1,0:T(2,128)S(1)}, u32[]{:S(2)}, u32[]{:S(2)}) %collective-permute-start.13) | collective-permute-done | bytes 6176 | tf_op jit(solution)/shard_map/ppermute | solution.py:353
  26.6 0.6 %finish.1 = (f32[2,256]{1,0:T(2,128)}, f32[2,512]{1,0:T(2,128)}) custom-call(f32[2,768]{1,0:T(2,128)S(1)} %get-tuple-element.28.mine_ref, f32[2,768]{1,0:T(2,128)S(1)} %collective-permute-done.13.got_ref), custom_call_target="tpu_custom_call" | custom-call | tf_op jit(solution)/shard_map/finish/pallas_call | solution.py:500
  (7 shorter events, 0.0 us)
Async XLA Ops:
  2.2 3.0 %collective-permute-start = (f32[2,1024]{1,0:T(2,128)S(1)}, f32[2,1024]{1,0:T(2,128)S(1)}, u32[]{:S(2)}, u32[]{:S(2)}) collective-permute-start(f32[2,1024]{1,0:T(2,128)S(1)} %get-tuple-element.20.mine_ref), channel_id=1, source_target_pairs={{0,1},{1,0},{2,3},{3,2},{4,5},{5,4},{6,7},{7,6},{8,9},{9,8},{10,11... | collective-permute-start | bytes 24584 | tf_op jit(solution)/shard_map/ppermute | solution.py:353
  5.2 6.0 %collective-permute-start.4 = (f32[88,128]{1,0:T(8,128)S(1)}, f32[88,128]{1,0:T(8,128)S(1)}, u32[]{:S(2)}, u32[]{:S(2)}) collective-permute-start(f32[88,128]{1,0:T(8,128)S(1)} %get-tuple-element.21), channel_id=1, source_target_pairs={{0,1},{1,12},{2,3},{3,14},{4,5},{5,8},{6,7},{7,10},{8,9},{9,4},{10... | collective-permute-start | bytes 135176 | tf_op jit(solution)/shard_map/ppermute | solution.py:363
  6.6 4.7 %collective-permute-start.3 = (f32[88,128]{1,0:T(8,128)S(1)}, f32[88,128]{1,0:T(8,128)S(1)}, u32[]{:S(2)}, u32[]{:S(2)}) collective-permute-start(f32[88,128]{1,0:T(8,128)S(1)} %get-tuple-element.21), channel_id=1, source_target_pairs={{0,1},{1,8},{2,3},{3,10},{4,5},{5,12},{6,7},{7,14},{8,9},{9,0},{10... | collective-permute-start | bytes 135176 | tf_op jit(solution)/shard_map/ppermute | solution.py:363
  8.7 3.5 %collective-permute-start.2 = (f32[88,128]{1,0:T(8,128)S(1)}, f32[88,128]{1,0:T(8,128)S(1)}, u32[]{:S(2)}, u32[]{:S(2)}) collective-permute-start(f32[88,128]{1,0:T(8,128)S(1)} %get-tuple-element.21), channel_id=1, source_target_pairs={{0,1},{1,4},{2,3},{3,6},{4,5},{5,0},{6,7},{7,2},{8,9},{9,12},{10,1... | collective-permute-start | bytes 135176 | tf_op jit(solution)/shard_map/ppermute | solution.py:363
  9.0 3.2 %collective-permute-start.1 = (f32[88,128]{1,0:T(8,128)S(1)}, f32[88,128]{1,0:T(8,128)S(1)}, u32[]{:S(2)}, u32[]{:S(2)}) collective-permute-start(f32[88,128]{1,0:T(8,128)S(1)} %get-tuple-element.21), channel_id=1, source_target_pairs={{0,1},{1,0},{2,3},{3,2},{4,5},{5,4},{6,7},{7,6},{8,9},{9,8},{10,11... | collective-permute-start | bytes 135176 | tf_op jit(solution)/shard_map/ppermute | solution.py:353
  12.2 2.5 %copy-start = (f32[512]{0:T(512)S(1)}, f32[512]{0:T(512)}, u32[]{:S(2)}) copy-start(f32[512]{0:T(512)} %param.13) | copy-start | bytes 6148
  12.2 2.4 %collective-permute-start.6 = (f32[112,128]{1,0:T(8,128)S(1)}, f32[112,128]{1,0:T(8,128)S(1)}, u32[]{:S(2)}, u32[]{:S(2)}) collective-permute-start(f32[112,128]{1,0:T(8,128)S(1)} %merge.1), channel_id=1, source_target_pairs={{0,17},{1,0},{2,19},{3,2},{4,21},{5,4},{6,23},{7,6},{8,25},{9,8},{... | collective-permute-start | bytes 172040 | tf_op jit(solution)/shard_map/ppermute | solution.py:363
  12.8 1.8 %collective-permute-start.5 = (f32[112,128]{1,0:T(8,128)S(1)}, f32[112,128]{1,0:T(8,128)S(1)}, u32[]{:S(2)}, u32[]{:S(2)}) collective-permute-start(f32[112,128]{1,0:T(8,128)S(1)} %merge.1), channel_id=1, source_target_pairs={{0,1},{1,0},{2,3},{3,2},{4,5},{5,4},{6,7},{7,6},{8,9},{9,8},{10,11... | collective-permute-start | bytes 172040 | tf_op jit(solution)/shard_map/ppermute | solution.py:353
  14.7 6.3 %collective-permute-start.10 = (f32[72,128]{1,0:T(8,128)S(1)}, f32[72,128]{1,0:T(8,128)S(1)}, u32[]{:S(2)}, u32[]{:S(2)}) collective-permute-start(f32[72,128]{1,0:T(8,128)S(1)} %get-tuple-element.23), channel_id=1, source_target_pairs={{0,1},{1,12},{2,3},{3,14},{4,5},{5,8},{6,7},{7,10},{8,9},{9,4},{10... | collective-permute-start | bytes 110600 | tf_op jit(solution)/shard_map/ppermute | solution.py:363
  19.0 3.4 %collective-permute-start.9 = (f32[72,128]{1,0:T(8,128)S(1)}, f32[72,128]{1,0:T(8,128)S(1)}, u32[]{:S(2)}, u32[]{:S(2)}) collective-permute-start(f32[72,128]{1,0:T(8,128)S(1)} %get-tuple-element.23), channel_id=1, source_target_pairs={{0,1},{1,8},{2,3},{3,10},{4,5},{5,12},{6,7},{7,14},{8,9},{9,0},{10... | collective-permute-start | bytes 110600 | tf_op jit(solution)/shard_map/ppermute | solution.py:363
  19.0 3.4 %collective-permute-start.8 = (f32[72,128]{1,0:T(8,128)S(1)}, f32[72,128]{1,0:T(8,128)S(1)}, u32[]{:S(2)}, u32[]{:S(2)}) collective-permute-start(f32[72,128]{1,0:T(8,128)S(1)} %get-tuple-element.23), channel_id=1, source_target_pairs={{0,1},{1,4},{2,3},{3,6},{4,5},{5,0},{6,7},{7,2},{8,9},{9,12},{10,1... | collective-permute-start | bytes 110600 | tf_op jit(solution)/shard_map/ppermute | solution.py:363
  19.1 3.3 %collective-permute-start.7 = (f32[72,128]{1,0:T(8,128)S(1)}, f32[72,128]{1,0:T(8,128)S(1)}, u32[]{:S(2)}, u32[]{:S(2)}) collective-permute-start(f32[72,128]{1,0:T(8,128)S(1)} %get-tuple-element.23), channel_id=1, source_target_pairs={{0,1},{1,0},{2,3},{3,2},{4,5},{5,4},{6,7},{7,6},{8,9},{9,8},{10,11... | collective-permute-start | bytes 110600 | tf_op jit(solution)/shard_map/ppermute | solution.py:353
  22.4 1.7 %collective-permute-start.12 = (f32[72,128]{1,0:T(8,128)S(1)}, f32[72,128]{1,0:T(8,128)S(1)}, u32[]{:S(2)}, u32[]{:S(2)}) collective-permute-start(f32[72,128]{1,0:T(8,128)S(1)} %add_add_fusion), channel_id=1, source_target_pairs={{0,17},{1,0},{2,19},{3,2},{4,21},{5,4},{6,23},{7,6},{8,25},{9,8},{... | collective-permute-start | bytes 110600 | tf_op jit(solution)/shard_map/ppermute | solution.py:363
  22.5 1.6 %collective-permute-start.11 = (f32[72,128]{1,0:T(8,128)S(1)}, f32[72,128]{1,0:T(8,128)S(1)}, u32[]{:S(2)}, u32[]{:S(2)}) collective-permute-start(f32[72,128]{1,0:T(8,128)S(1)} %add_add_fusion), channel_id=1, source_target_pairs={{0,1},{1,0},{2,3},{3,2},{4,5},{5,4},{6,7},{7,6},{8,9},{9,8},{10,11... | collective-permute-start | bytes 110600 | tf_op jit(solution)/shard_map/ppermute | solution.py:353
  24.1 2.4 %collective-permute-start.13 = (f32[2,768]{1,0:T(2,128)S(1)}, f32[2,768]{1,0:T(2,128)S(1)}, u32[]{:S(2)}, u32[]{:S(2)}) collective-permute-start(f32[2,768]{1,0:T(2,128)S(1)} %get-tuple-element.29), channel_id=1, source_target_pairs={{0,1},{1,0},{2,3},{3,2},{4,5},{5,4},{6,7},{7,6},{8,9},{9,8},{10,11... | collective-permute-start | bytes 18440 | tf_op jit(solution)/shard_map/ppermute | solution.py:353

commit v7 on v6

--- a/solution.py
+++ b/solution.py
@@ -38,10 +38,6 @@
     ref[count + index] = jnp.concatenate([empty, rows], axis=0).astype(jnp.bfloat16)
 
 
-def put_left(left_ref, index, value):
-    pair_blocks(left_ref, index, jnp.concatenate(split(value), axis=0))
-
-
 def clear_left(left_ref):
     pair_blocks(left_ref, ROWBLK, jnp.zeros((KEPT, EDGE), jnp.float32))
 
@@ -53,21 +49,16 @@
         sums_refs[0][band * COLBLK + j, 0:VECS, :] = -costs[:, j * EDGE : (j + 1) * EDGE]
 
 
-def adjoint_sum(sums_refs, v):
-    blocks = sums_refs[0].shape[0]
-    total = 0.0
-    for ref in sums_refs:
-        flat = ref.reshape(blocks * KEPT, EDGE)
-        for s in range(TERMS):
-            total += flat[pl.ds(VECS * s + v, blocks, stride=KEPT), :]
-    return total
-
-
-def forward_left(right32_ref, v, value):
-    blocks = right32_ref.shape[0]
-    flat = right32_ref.reshape(blocks * KEPT, EDGE)
-    for s, term in enumerate(split(value)):
-        flat[pl.ds(VECS * s + v, blocks, stride=KEPT), :] = term
+def adjoint_sum(sums_refs, c):
+    return sum(joined(ref[c]) for ref in sums_refs)
+
+
+def span(c):
+    return slice(c * EDGE, (c + 1) * EDGE)
+
+
+def put_block(ref, index, value):
+    pair_blocks(ref, index, jnp.concatenate(split(value), axis=0))
 
 
 def row_of(meta_ref, count_ref, t):
@@ -185,31 +176,30 @@
         clear_left(left_ref)
         adjoint_start(sums_refs, both[:, nrow + ncol :], lax.axis_index("band"))
         for r in range(ROWBLK):
-            put_left(left_ref, r, both[:, r * EDGE : (r + 1) * EDGE] * rscale_ref[r : r + 1, :])
-        send_ref[0:blocks, :] = top_ref[...]
-        for j in range(COLBLK):
-            at = (1 + VECS) * blocks + j * VECS
-            send_ref[at : at + VECS, :] = both[:, nrow + j * EDGE : nrow + (j + 1) * EDGE]
+            put_block(left_ref, r, both[:, r * EDGE : (r + 1) * EDGE] * rscale_ref[r : r + 1, :])
+        per = blocks // VECS
+        for m in range(per):
+            send_ref[:, span(blocks + m)] = top_ref[pl.ds(m, VECS, stride=per), :]
+        send_ref[:, (blocks + per) * EDGE :] = both[:, nrow : nrow + ncol]
         tile_pass(meta_ref, count_ref, tiles_ref, left_ref, True, sums_refs)
-        for v in range(VECS):
-            send_ref[(1 + v) * blocks : (2 + v) * blocks, :] = adjoint_sum(sums_refs, v)
-
-
-def combined(refs, blocks):
-    peak = functools.reduce(jnp.maximum, [ref[0:blocks, :] for ref in refs])
-    rows = slice(blocks, (1 + VECS) * blocks)
-    return peak, functools.reduce(jnp.add, [ref[rows, :] for ref in refs])
+        for c in range(blocks):
+            send_ref[:, span(c)] = adjoint_sum(sums_refs, c)
+
+
+def peaks_of(refs, blocks):
+    spot = slice(blocks * EDGE, (blocks + blocks // VECS) * EDGE)
+    return functools.reduce(jnp.maximum, [ref[:, spot] for ref in refs])
 
 
 def merge_kernel(blocks, *refs):
     refs, out_ref = refs[:-1], refs[-1]
-    head = (1 + VECS) * blocks
-    peak, total = combined(refs, blocks)
-    out_ref[0:blocks, :] = peak
-    out_ref[blocks:head, :] = total
-    more = refs[0].shape[0] - head
+    head = (blocks + blocks // VECS) * EDGE
+    out_ref[:, blocks * EDGE : head] = peaks_of(refs, blocks)
+    for c in range(blocks):
+        out_ref[:, span(c)] = functools.reduce(jnp.add, [ref[:, span(c)] for ref in refs])
+    more = refs[0].shape[1] - head
     for i, ref in enumerate(refs):
-        out_ref[head + i * more : head + (i + 1) * more, :] = ref[head:, :]
+        out_ref[:, head + i * more : head + (i + 1) * more] = ref[:, head:]
 
 
 def step_kernel(
@@ -219,10 +209,11 @@
     (
         rscale_ref, both_ref, bound_ref,
         send_ref, x_one_ref, cscale_ref, y_one_ref, moved_ref,
-        start_ref, right32_ref, right_ref, out_ref, out_two_ref, left_ref, sums_ref, sums_two_ref,
+        start_ref, right_ref, out_ref, out_two_ref, left_ref, sums_ref, sums_two_ref,
     ) = rest[parts:]
-    blocks = right32_ref.shape[0]
-    head = (1 + VECS) * blocks
+    blocks = start_ref.shape[0]
+    places = blocks // VECS
+    head = (blocks + places) * EDGE
     sums_refs = (sums_ref, sums_two_ref)
 
     @pl.when(leads())
@@ -233,27 +224,21 @@
         per = len(offsets) // parts
         for m, offset in enumerate(offsets):
             for j in range(COLBLK):
-                at = head + (m % per) * COLBLK * VECS + j * VECS
-                place = (band ^ offset) * COLBLK + j
-                start_ref[place, 0:VECS, :] = got_refs[m // per][at : at + VECS, :]
-        start = start_ref.reshape(blocks * 8, EDGE)
-
-        peak, totals = combined(got_refs, blocks)
-        cscale = lax.rsqrt(peak)
+                at = head + ((m % per) * COLBLK + j) * EDGE
+                start_ref[(band ^ offset) * COLBLK + j] = got_refs[m // per][:, at : at + EDGE]
+
+        cscale = lax.rsqrt(peaks_of(got_refs, blocks))
         cscale_ref[...] = cscale
-        for v in range(VECS):
-            before = start[pl.ds(v, blocks, stride=8), :]
-            after = jnp.maximum(
-                0.0, before + step_size * (cscale * totals[v * blocks : (v + 1) * blocks])
-            )
-            x_one_ref[v * blocks : (v + 1) * blocks, :] = after
-            moved = jnp.sum(
-                jnp.sum((after - before) ** 2, axis=0, keepdims=True), axis=1, keepdims=True
-            )
-            moved_ref[v : v + 1, :] = jnp.broadcast_to(moved, (1, EDGE))
-            forward_left(right32_ref, v, cscale * (2.0 * after - before))
+        moved = jnp.zeros((VECS, EDGE), jnp.float32)
         for c in range(blocks):
-            pair_blocks(right_ref, c, right32_ref[c])
+            scale = cscale[c // places : c // places + 1, span(c % places)]
+            total = functools.reduce(jnp.add, [ref[:, span(c)] for ref in got_refs])
+            before = start_ref[c]
+            after = jnp.maximum(0.0, before + step_size * (scale * total))
+            x_one_ref[:, span(c)] = after
+            moved += (after - before) ** 2
+            put_block(right_ref, c, scale * (2.0 * after - before))
+        moved_ref[...] = moved
 
         for ref in (out_ref, out_two_ref):
             ref[...] = jnp.zeros_like(ref)
@@ -261,21 +246,19 @@
 
         moved = jnp.zeros((VECS, EDGE), jnp.float32)
         for r in range(ROWBLK):
-            span = slice(r * EDGE, (r + 1) * EDGE)
             scale = rscale_ref[r : r + 1, :]
-            before = both_ref[:, span]
+            before = both_ref[:, span(r)]
             after = jnp.maximum(
-                0.0, before + step_size * (scale * (bound_ref[:, span] - joined(out_ref[r] + out_two_ref[r])))
+                0.0, before + step_size * (scale * (bound_ref[:, span(r)] - joined(out_ref[r] + out_two_ref[r])))
             )
-            y_one_ref[:, span] = after
+            y_one_ref[:, span(r)] = after
             moved += (after - before) ** 2
-            put_left(left_ref, r, after * scale)
+            put_block(left_ref, r, after * scale)
 
         tile_pass(meta_ref, count_ref, tiles_ref, left_ref, True, sums_refs)
-        for v in range(VECS):
-            send_ref[v * blocks : (v + 1) * blocks, :] = adjoint_sum(sums_refs, v)
-        send_ref[VECS * blocks :, :] = jnp.zeros((8, EDGE), jnp.float32)
-        send_ref[VECS * blocks : VECS * blocks + VECS, :] = moved
+        for c in range(blocks):
+            send_ref[:, span(c)] = adjoint_sum(sums_refs, c)
+        send_ref[:, blocks * EDGE :] = moved
 
 
 def last_kernel(parts, meta_ref, count_ref, turned_ref, *rest):
@@ -283,48 +266,43 @@
     (
         rscale_ref, y_ref, bound_ref, x_one_ref, cscale_ref, moved_ref,
         mine_ref, other_ref,
-        right32_ref, right_ref, out_ref, out_two_ref,
+        own_ref, right_ref, out_ref, out_two_ref,
     ) = rest[parts:]
-    blocks = right32_ref.shape[0]
+    blocks = own_ref.shape[0]
+    places = blocks // VECS
     half = VECS // 2
     ncol = COLBLK * EDGE
 
     @pl.when(leads())
     def _():
         band = lax.axis_index("band")
-        cscale = cscale_ref[...]
-        row = lax.broadcasted_iota(jnp.int32, (blocks, EDGE), 0)
-        got = functools.reduce(jnp.add, [ref[...] for ref in got_refs])
-        dual = jnp.sum(got[VECS * blocks : VECS * blocks + VECS], axis=1, keepdims=True)
-        ratio = jnp.sqrt((dual + 1e-06) / (moved_ref[...] + 1e-06))
-        for v in range(VECS):
-            before = x_one_ref[v * blocks : (v + 1) * blocks, :]
-            after = jnp.maximum(
-                0.0,
-                before
-                + step_size / ratio[v : v + 1, :] * (cscale * got[v * blocks : (v + 1) * blocks]),
-            )
-            to_ref = mine_ref if v < half else other_ref
-            for j in range(COLBLK):
-                own = jnp.where(row == band * COLBLK + j, after, 0.0)
-                to_ref[v % half : v % half + 1, j * EDGE : (j + 1) * EDGE] = jnp.sum(
-                    own, axis=0, keepdims=True
-                )
-            forward_left(right32_ref, v, cscale * (2.0 * after - before))
+        dual = functools.reduce(jnp.add, [ref[:, blocks * EDGE :] for ref in got_refs])
+        dual = jnp.sum(dual, axis=1, keepdims=True)
+        primal = jnp.sum(moved_ref[...], axis=1, keepdims=True)
+        ratio = jnp.sqrt((dual + 1e-06) / (primal + 1e-06))
+        size = step_size / ratio
         for c in range(blocks):
-            pair_blocks(right_ref, c, right32_ref[c])
+            scale = cscale_ref[c // places : c // places + 1, span(c % places)]
+            total = functools.reduce(jnp.add, [ref[:, span(c)] for ref in got_refs])
+            before = x_one_ref[:, span(c)]
+            after = jnp.maximum(0.0, before + size * (scale * total))
+            own_ref[c] = after
+            put_block(right_ref, c, scale * (2.0 * after - before))
+        for j in range(COLBLK):
+            own = own_ref[band * COLBLK + j]
+            mine_ref[:, span(j)] = own[0:half]
+            other_ref[:, span(j)] = own[half:]
 
         for ref in (out_ref, out_two_ref):
             ref[...] = jnp.zeros_like(ref)
         tile_pass(meta_ref, count_ref, turned_ref, right_ref, False, (out_ref, out_two_ref))
 
         for r in range(ROWBLK):
-            span = slice(r * EDGE, (r + 1) * EDGE)
             scale = rscale_ref[r : r + 1, :]
             after = jnp.maximum(
                 0.0,
-                y_ref[:, span]
-                + step_size * ratio * (scale * (bound_ref[:, span] - joined(out_ref[r] + out_two_ref[r]))),
+                y_ref[:, span(r)]
+                + step_size * ratio * (scale * (bound_ref[:, span(r)] - joined(out_ref[r] + out_two_ref[r]))),
             )
             place = slice(ncol + r * EDGE, ncol + (r + 1) * EDGE)
             mine_ref[:, place] = after[0:half]
@@ -383,6 +361,7 @@
     ntile = tiles.shape[0]
     bands = lax.axis_size("band")
     blocks = bands * COLBLK
+    head = (blocks + blocks // VECS) * EDGE
     bound = bound_vec.reshape(1, -1)
     nrow = bound.shape[1]
     f32 = lambda *shape: jax.ShapeDtypeStruct(shape, jnp.float32)
@@ -392,7 +371,7 @@
     hbm = lambda n: [pl.BlockSpec(memory_space=pltpu.HBM)] * n
     vmem = lambda n: [pl.BlockSpec(memory_space=pltpu.VMEM)] * n
     left = [v16(2 * (ROWBLK + 1), 2 * KEPT, EDGE)]
-    right = [v32(blocks, KEPT, EDGE), v16(2 * blocks, 2 * KEPT, EDGE)]
+    right = [v32(blocks, VECS, EDGE), v16(2 * blocks, 2 * KEPT, EDGE)]
     rows_out = [v32(ROWBLK + 1, KEPT, EDGE)] * 2
     sums = [v32(blocks, KEPT, EDGE)] * 2
     params = pltpu.CompilerParams(vmem_limit_bytes=32 * 1024 * 1024)
@@ -445,7 +424,7 @@
 
     message, both = pl.pallas_call(
         start_kernel,
-        out_shape=(f32((1 + VECS) * blocks + COLBLK * VECS, EDGE), v32(VECS, mine.shape[1])),
+        out_shape=(f32(VECS, head + COLBLK * EDGE), v32(VECS, mine.shape[1])),
         in_specs=smem * 2 + vmem(5),
         out_specs=tuple(vmem(2)),
         scratch_shapes=left + sums,
@@ -461,7 +440,7 @@
         if index < len(rounds) - 1:
             message = pl.pallas_call(
                 functools.partial(merge_kernel, blocks),
-                out_shape=f32((1 + VECS) * blocks + COLBLK * VECS * len(offsets), EDGE),
+                out_shape=f32(VECS, head + len(offsets) * COLBLK * EDGE),
                 in_specs=vmem(len(messages)),
                 out_specs=vmem(1)[0],
                 compiler_params=params,
@@ -471,11 +450,11 @@
     message, x_one, cscale, y_one, moved = pl.pallas_call(
         functools.partial(step_kernel, offsets, len(messages)),
         out_shape=(
-            f32(VECS * blocks + 8, EDGE), v32(VECS * blocks, EDGE), v32(blocks, EDGE), v32(VECS, nrow), v32(VECS, EDGE),
+            f32(VECS, (blocks + 1) * EDGE), v32(VECS, blocks * EDGE), v32(VECS, blocks // VECS * EDGE), v32(VECS, nrow), v32(VECS, EDGE),
         ),
         in_specs=smem * 2 + vmem(5 + len(messages)),
         out_specs=tuple(vmem(5)),
-        scratch_shapes=[v32(blocks, 8, EDGE)] + right + rows_out + left + sums,
+        scratch_shapes=right + rows_out + left + sums,
         compiler_params=params,
         name="first_step",
     )(meta, tile_count, held, turned, *messages, rscale, both, bound)

time: 27.4 us -> 27.3 us (level)
  no operation moved by 1% of the time
where the time goes in v7:
time: 27.3 us; the launch traced here: 27.2 us
  starting transfers between devices  13.6 us (50%)
  waiting for transfers between devices  10.7 us (39%)
  Pallas kernels  1.55 us (6%)
  between operations  1.32 us (5%)
    ppermute x8, waiting for transfers between devices, relayed(): return lax.ppermute(value, ('band', 'batch'), pairs)  9 us
    ppermute x8, starting transfers between devices, relayed(): return lax.ppermute(value, ('band', 'batch'), pairs)  8.92 us
    ppermute x6, starting transfers between devices, swap(): return lax.ppermute(value, 'batch', [(i, i ^ 1) for i in range(count)])  4.67 us
    ppermute x6, waiting for transfers between devices, swap(): return lax.ppermute(value, 'batch', [(i, i ^ 1) for i in range(count)])  1.66 us
    pallas_call x1, Pallas kernels, shards(): pl.pallas_call(scale_kernel, out_shape=(pltpu.SMEM((2, ntile), jnp.int32)...  0.92 us
    pallas_call x1, Pallas kernels, shards(): pl.pallas_call(finish_kernel, out_shape=(f32(*x_start.shape), f32(*y_star...  0.61 us
  transfers between devices with their start and end apart: 14, of which 9 were waited for; matrix products, arithmetic and copies ran while one was open for 0% of the time, Pallas kernels for 0%

profile of v7, /device:TPU:0, one launch (start us, length us, event | category | flops | bytes accessed | tf_op | source)
XLA Modules:
  0.0 27.2 jit_solution(10173386078733444685)
XLA Ops:
  1.3 0.9 %row_scales.1 = (s32[2,128]{1,0:T(2,128)S(4)}, f32[2,1024]{1,0:T(2,128)S(1)}, bf16[128,128,128]{2,1,0:T(8,128)(2,1)S(1)}, f32[5,128,128]{2,1,0:T(8,128)S(1)}, f32[4,128]{1,0:T(4,128)S(1)}) custom-call(s32[1,128]{1,0:T(1,128)} %rows_ref.1, s32[1,128]{1,0:T(1,128)} %cols_ref.1, s32[1]{0:T(128)S(6)} %copy.10.count_ref, f32[2,512]{1,0:T(2,128)} %y_ref.1, ...), custom_call_target="tpu_custom_call" | custom-call | bytes 4194304 | tf_op jit(solution)/shard_map/row_scales/pallas_call | solution.py:381
  2.2 2.2 %collective-permute-start = (f32[2,1024]{1,0:T(2,128)S(1)}, f32[2,1024]{1,0:T(2,128)S(1)}, u32[]{:S(2)}, u32[]{:S(2)}) collective-permute-start(f32[2,1024]{1,0:T(2,128)S(1)} %get-tuple-element.20.mine_ref), channel_id=1, source_target_pairs={{0,1},{1,0},{2,3},{3,2},{4,5},{5,4},{6,7},{7,6},{8,9},{9,8},{10,11... | collective-permute-start | bytes 24584 | tf_op jit(solution)/shard_map/ppermute | solution.py:331
  4.4 0.8 %collective-permute-done.other_ref = f32[2,1024]{1,0:T(2,128)S(1)} collective-permute-done((f32[2,1024]{1,0:T(2,128)S(1)}, f32[2,1024]{1,0:T(2,128)S(1)}, u32[]{:S(2)}, u32[]{:S(2)}) %collective-permute-start) | collective-permute-done | bytes 8224 | tf_op jit(solution)/shard_map/ppermute | solution.py:331
  5.2 1.3 %collective-permute-start.4 = (f32[4,2816]{1,0:T(4,128)S(1)}, f32[4,2816]{1,0:T(4,128)S(1)}, u32[]{:S(2)}, u32[]{:S(2)}) collective-permute-start(f32[4,2816]{1,0:T(4,128)S(1)} %get-tuple-element.21), channel_id=1, source_target_pairs={{0,1},{1,12},{2,3},{3,14},{4,5},{5,8},{6,7},{7,10},{8,9},{9,4},{10... | collective-permute-start | bytes 135176 | tf_op jit(solution)/shard_map/ppermute | solution.py:341
  6.6 2.2 %collective-permute-start.3 = (f32[4,2816]{1,0:T(4,128)S(1)}, f32[4,2816]{1,0:T(4,128)S(1)}, u32[]{:S(2)}, u32[]{:S(2)}) collective-permute-start(f32[4,2816]{1,0:T(4,128)S(1)} %get-tuple-element.21), channel_id=1, source_target_pairs={{0,1},{1,8},{2,3},{3,10},{4,5},{5,12},{6,7},{7,14},{8,9},{9,0},{10... | collective-permute-start | bytes 135176 | tf_op jit(solution)/shard_map/ppermute | solution.py:341
  8.7 0.4 %collective-permute-start.2 = (f32[4,2816]{1,0:T(4,128)S(1)}, f32[4,2816]{1,0:T(4,128)S(1)}, u32[]{:S(2)}, u32[]{:S(2)}) collective-permute-start(f32[4,2816]{1,0:T(4,128)S(1)} %get-tuple-element.21), channel_id=1, source_target_pairs={{0,1},{1,4},{2,3},{3,6},{4,5},{5,0},{6,7},{7,2},{8,9},{9,12},{10,1... | collective-permute-start | bytes 135176 | tf_op jit(solution)/shard_map/ppermute | solution.py:341
  9.1 0.3 collective-permute-start.1
  9.3 1.9 %collective-permute-done.4.refs_3_ = f32[4,2816]{1,0:T(4,128)S(1)} collective-permute-done((f32[4,2816]{1,0:T(4,128)S(1)}, f32[4,2816]{1,0:T(4,128)S(1)}, u32[]{:S(2)}, u32[]{:S(2)}) %collective-permute-start.4) | collective-permute-done | bytes 45088 | tf_op jit(solution)/shard_map/ppermute | solution.py:341
  11.2 0.0 collective-permute-done.3.refs_2_
  11.3 0.9 %collective-permute-done.2.refs_1_ = f32[4,2816]{1,0:T(4,128)S(1)} collective-permute-done((f32[4,2816]{1,0:T(4,128)S(1)}, f32[4,2816]{1,0:T(4,128)S(1)}, u32[]{:S(2)}, u32[]{:S(2)}) %collective-permute-start.2) | collective-permute-done | bytes 45088 | tf_op jit(solution)/shard_map/ppermute | solution.py:341
  12.2 0.0 collective-permute-done.1.refs_0_
  12.2 0.0 copy-start
  12.2 0.6 %collective-permute-start.6 = (f32[4,3584]{1,0:T(4,128)S(1)}, f32[4,3584]{1,0:T(4,128)S(1)}, u32[]{:S(2)}, u32[]{:S(2)}) collective-permute-start(f32[4,3584]{1,0:T(4,128)S(1)} %merge.1), channel_id=1, source_target_pairs={{0,17},{1,0},{2,19},{3,2},{4,21},{5,4},{6,23},{7,6},{8,25},{9,8},{... | collective-permute-start | bytes 172040 | tf_op jit(solution)/shard_map/ppermute | solution.py:341
  12.9 0.0 collective-permute-start.5
  12.9 1.8 %collective-permute-done.6.rest_1_ = f32[4,3584]{1,0:T(4,128)S(1)} collective-permute-done((f32[4,3584]{1,0:T(4,128)S(1)}, f32[4,3584]{1,0:T(4,128)S(1)}, u32[]{:S(2)}, u32[]{:S(2)}) %collective-permute-start.6) | collective-permute-done | bytes 57376 | tf_op jit(solution)/shard_map/ppermute | solution.py:341
  14.7 0.0 collective-permute-done.5.rest_0_
  14.7 0.0 copy-done
  14.7 4.3 %collective-permute-start.10 = (f32[4,2176]{1,0:T(4,128)S(1)}, f32[4,2176]{1,0:T(4,128)S(1)}, u32[]{:S(2)}, u32[]{:S(2)}) collective-permute-start(f32[4,2176]{1,0:T(4,128)S(1)} %get-tuple-element.23), channel_id=1, source_target_pairs={{0,1},{1,12},{2,3},{3,14},{4,5},{5,8},{6,7},{7,10},{8,9},{9,4},{10... | collective-permute-start | bytes 104456 | tf_op jit(solution)/shard_map/ppermute | solution.py:341
  19.0 0.1 collective-permute-start.9
  19.0 0.1 collective-permute-start.8
  19.1 0.1 collective-permute-start.7
  19.2 1.8 %collective-permute-done.10 = f32[4,2176]{1,0:T(4,128)S(1)} collective-permute-done((f32[4,2176]{1,0:T(4,128)S(1)}, f32[4,2176]{1,0:T(4,128)S(1)}, u32[]{:S(2)}, u32[]{:S(2)}) %collective-permute-start.10) | collective-permute-done | bytes 34848 | tf_op jit(solution)/shard_map/ppermute | solution.py:341
  21.0 1.4 %collective-permute-done.9 = f32[4,2176]{1,0:T(4,128)S(1)} collective-permute-done((f32[4,2176]{1,0:T(4,128)S(1)}, f32[4,2176]{1,0:T(4,128)S(1)}, u32[]{:S(2)}, u32[]{:S(2)}) %collective-permute-start.9) | collective-permute-done | bytes 34848 | tf_op jit(solution)/shard_map/ppermute | solution.py:341
  22.3 0.1 collective-permute-done.8
  22.4 0.0 collective-permute-done.7
  22.4 0.1 collective-permute-start.12
  22.5 0.5 %collective-permute-start.11 = (f32[4,2176]{1,0:T(4,128)S(1)}, f32[4,2176]{1,0:T(4,128)S(1)}, u32[]{:S(2)}, u32[]{:S(2)}) collective-permute-start(f32[4,2176]{1,0:T(4,128)S(1)} %add_add_fusion), channel_id=1, source_target_pairs={{0,1},{1,0},{2,3},{3,2},{4,5},{5,4},{6,7},{7,6},{8,9},{9,8},{10,11... | collective-permute-start | bytes 104456 | tf_op jit(solution)/shard_map/ppermute | solution.py:331
  23.0 1.1 %collective-permute-done.12.rest_1_ = f32[4,2176]{1,0:T(4,128)S(1)} collective-permute-done((f32[4,2176]{1,0:T(4,128)S(1)}, f32[4,2176]{1,0:T(4,128)S(1)}, u32[]{:S(2)}, u32[]{:S(2)}) %collective-permute-start.12) | collective-permute-done | bytes 34848 | tf_op jit(solution)/shard_map/ppermute | solution.py:341
  24.1 0.0 collective-permute-done.11.rest_0_
  24.1 1.6 %collective-permute-start.13 = (f32[2,768]{1,0:T(2,128)S(1)}, f32[2,768]{1,0:T(2,128)S(1)}, u32[]{:S(2)}, u32[]{:S(2)}) collective-permute-start(f32[2,768]{1,0:T(2,128)S(1)} %get-tuple-element.29), channel_id=1, source_target_pairs={{0,1},{1,0},{2,3},{3,2},{4,5},{5,4},{6,7},{7,6},{8,9},{9,8},{10,11... | collective-permute-start | bytes 18440 | tf_op jit(solution)/shard_map/ppermute | solution.py:331
  25.7 0.8 %collective-permute-done.13.got_ref = f32[2,768]{1,0:T(2,128)S(1)} collective-permute-done((f32[2,768]{1,0:T(2,128)S(1)}, f32[2,768]{1,0:T(2,128)S(1)}, u32[]{:S(2)}, u32[]{:S(2)}) %collective-permute-start.13) | collective-permute-done | bytes 6176 | tf_op jit(solution)/shard_map/ppermute | solution.py:331
  26.6 0.6 %finish.1 = (f32[2,256]{1,0:T(2,128)}, f32[2,512]{1,0:T(2,128)}) custom-call(f32[2,768]{1,0:T(2,128)S(1)} %get-tuple-element.28.mine_ref, f32[2,768]{1,0:T(2,128)S(1)} %collective-permute-done.13.got_ref), custom_call_target="tpu_custom_call" | custom-call | tf_op jit(solution)/shard_map/finish/pallas_call | solution.py:479
  (7 shorter events, 0.0 us)
Async XLA Ops:
  2.2 3.0 %collective-permute-start = (f32[2,1024]{1,0:T(2,128)S(1)}, f32[2,1024]{1,0:T(2,128)S(1)}, u32[]{:S(2)}, u32[]{:S(2)}) collective-permute-start(f32[2,1024]{1,0:T(2,128)S(1)} %get-tuple-element.20.mine_ref), channel_id=1, source_target_pairs={{0,1},{1,0},{2,3},{3,2},{4,5},{5,4},{6,7},{7,6},{8,9},{9,8},{10,11... | collective-permute-start | bytes 24584 | tf_op jit(solution)/shard_map/ppermute | solution.py:331
  5.2 6.0 %collective-permute-start.4 = (f32[4,2816]{1,0:T(4,128)S(1)}, f32[4,2816]{1,0:T(4,128)S(1)}, u32[]{:S(2)}, u32[]{:S(2)}) collective-permute-start(f32[4,2816]{1,0:T(4,128)S(1)} %get-tuple-element.21), channel_id=1, source_target_pairs={{0,1},{1,12},{2,3},{3,14},{4,5},{5,8},{6,7},{7,10},{8,9},{9,4},{10... | collective-permute-start | bytes 135176 | tf_op jit(solution)/shard_map/ppermute | solution.py:341
  6.6 4.7 %collective-permute-start.3 = (f32[4,2816]{1,0:T(4,128)S(1)}, f32[4,2816]{1,0:T(4,128)S(1)}, u32[]{:S(2)}, u32[]{:S(2)}) collective-permute-start(f32[4,2816]{1,0:T(4,128)S(1)} %get-tuple-element.21), channel_id=1, source_target_pairs={{0,1},{1,8},{2,3},{3,10},{4,5},{5,12},{6,7},{7,14},{8,9},{9,0},{10... | collective-permute-start | bytes 135176 | tf_op jit(solution)/shard_map/ppermute | solution.py:341
  8.7 3.5 %collective-permute-start.2 = (f32[4,2816]{1,0:T(4,128)S(1)}, f32[4,2816]{1,0:T(4,128)S(1)}, u32[]{:S(2)}, u32[]{:S(2)}) collective-permute-start(f32[4,2816]{1,0:T(4,128)S(1)} %get-tuple-element.21), channel_id=1, source_target_pairs={{0,1},{1,4},{2,3},{3,6},{4,5},{5,0},{6,7},{7,2},{8,9},{9,12},{10,1... | collective-permute-start | bytes 135176 | tf_op jit(solution)/shard_map/ppermute | solution.py:341
  9.1 3.1 %collective-permute-start.1 = (f32[4,2816]{1,0:T(4,128)S(1)}, f32[4,2816]{1,0:T(4,128)S(1)}, u32[]{:S(2)}, u32[]{:S(2)}) collective-permute-start(f32[4,2816]{1,0:T(4,128)S(1)} %get-tuple-element.21), channel_id=1, source_target_pairs={{0,1},{1,0},{2,3},{3,2},{4,5},{5,4},{6,7},{7,6},{8,9},{9,8},{10,11... | collective-permute-start | bytes 135176 | tf_op jit(solution)/shard_map/ppermute | solution.py:331
  12.2 2.5 %copy-start = (f32[512]{0:T(512)S(1)}, f32[512]{0:T(512)}, u32[]{:S(2)}) copy-start(f32[512]{0:T(512)} %param.13) | copy-start | bytes 6148
  12.2 2.4 %collective-permute-start.6 = (f32[4,3584]{1,0:T(4,128)S(1)}, f32[4,3584]{1,0:T(4,128)S(1)}, u32[]{:S(2)}, u32[]{:S(2)}) collective-permute-start(f32[4,3584]{1,0:T(4,128)S(1)} %merge.1), channel_id=1, source_target_pairs={{0,17},{1,0},{2,19},{3,2},{4,21},{5,4},{6,23},{7,6},{8,25},{9,8},{... | collective-permute-start | bytes 172040 | tf_op jit(solution)/shard_map/ppermute | solution.py:341
  12.9 1.8 %collective-permute-start.5 = (f32[4,3584]{1,0:T(4,128)S(1)}, f32[4,3584]{1,0:T(4,128)S(1)}, u32[]{:S(2)}, u32[]{:S(2)}) collective-permute-start(f32[4,3584]{1,0:T(4,128)S(1)} %merge.1), channel_id=1, source_target_pairs={{0,1},{1,0},{2,3},{3,2},{4,5},{5,4},{6,7},{7,6},{8,9},{9,8},{10,11... | collective-permute-start | bytes 172040 | tf_op jit(solution)/shard_map/ppermute | solution.py:331
  14.7 6.3 %collective-permute-start.10 = (f32[4,2176]{1,0:T(4,128)S(1)}, f32[4,2176]{1,0:T(4,128)S(1)}, u32[]{:S(2)}, u32[]{:S(2)}) collective-permute-start(f32[4,2176]{1,0:T(4,128)S(1)} %get-tuple-element.23), channel_id=1, source_target_pairs={{0,1},{1,12},{2,3},{3,14},{4,5},{5,8},{6,7},{7,10},{8,9},{9,4},{10... | collective-permute-start | bytes 104456 | tf_op jit(solution)/shard_map/ppermute | solution.py:341
  19.0 3.4 %collective-permute-start.9 = (f32[4,2176]{1,0:T(4,128)S(1)}, f32[4,2176]{1,0:T(4,128)S(1)}, u32[]{:S(2)}, u32[]{:S(2)}) collective-permute-start(f32[4,2176]{1,0:T(4,128)S(1)} %get-tuple-element.23), channel_id=1, source_target_pairs={{0,1},{1,8},{2,3},{3,10},{4,5},{5,12},{6,7},{7,14},{8,9},{9,0},{10... | collective-permute-start | bytes 104456 | tf_op jit(solution)/shard_map/ppermute | solution.py:341
  19.0 3.4 %collective-permute-start.8 = (f32[4,2176]{1,0:T(4,128)S(1)}, f32[4,2176]{1,0:T(4,128)S(1)}, u32[]{:S(2)}, u32[]{:S(2)}) collective-permute-start(f32[4,2176]{1,0:T(4,128)S(1)} %get-tuple-element.23), channel_id=1, source_target_pairs={{0,1},{1,4},{2,3},{3,6},{4,5},{5,0},{6,7},{7,2},{8,9},{9,12},{10,1... | collective-permute-start | bytes 104456 | tf_op jit(solution)/shard_map/ppermute | solution.py:341
  19.1 3.3 %collective-permute-start.7 = (f32[4,2176]{1,0:T(4,128)S(1)}, f32[4,2176]{1,0:T(4,128)S(1)}, u32[]{:S(2)}, u32[]{:S(2)}) collective-permute-start(f32[4,2176]{1,0:T(4,128)S(1)} %get-tuple-element.23), channel_id=1, source_target_pairs={{0,1},{1,0},{2,3},{3,2},{4,5},{5,4},{6,7},{7,6},{8,9},{9,8},{10,11... | collective-permute-start | bytes 104456 | tf_op jit(solution)/shard_map/ppermute | solution.py:331
  22.4 1.7 %collective-permute-start.12 = (f32[4,2176]{1,0:T(4,128)S(1)}, f32[4,2176]{1,0:T(4,128)S(1)}, u32[]{:S(2)}, u32[]{:S(2)}) collective-permute-start(f32[4,2176]{1,0:T(4,128)S(1)} %add_add_fusion), channel_id=1, source_target_pairs={{0,17},{1,0},{2,19},{3,2},{4,21},{5,4},{6,23},{7,6},{8,25},{9,8},{... | collective-permute-start | bytes 104456 | tf_op jit(solution)/shard_map/ppermute | solution.py:341
  22.5 1.6 %collective-permute-start.11 = (f32[4,2176]{1,0:T(4,128)S(1)}, f32[4,2176]{1,0:T(4,128)S(1)}, u32[]{:S(2)}, u32[]{:S(2)}) collective-permute-start(f32[4,2176]{1,0:T(4,128)S(1)} %add_add_fusion), channel_id=1, source_target_pairs={{0,1},{1,0},{2,3},{3,2},{4,5},{5,4},{6,7},{7,6},{8,9},{9,8},{10,11... | collective-permute-start | bytes 104456 | tf_op jit(solution)/shard_map/ppermute | solution.py:331
  24.1 2.4 %collective-permute-start.13 = (f32[2,768]{1,0:T(2,128)S(1)}, f32[2,768]{1,0:T(2,128)S(1)}, u32[]{:S(2)}, u32[]{:S(2)}) collective-permute-start(f32[2,768]{1,0:T(2,128)S(1)} %get-tuple-element.29), channel_id=1, source_target_pairs={{0,1},{1,0},{2,3},{3,2},{4,5},{5,4},{6,7},{7,6},{8,9},{9,8},{10,11... | collective-permute-start | bytes 18440 | tf_op jit(solution)/shard_map/ppermute | solution.py:331

commit v8 on v7

--- a/solution.py
+++ b/solution.py
@@ -280,7 +280,7 @@
         dual = jnp.sum(dual, axis=1, keepdims=True)
         primal = jnp.sum(moved_ref[...], axis=1, keepdims=True)
         ratio = jnp.sqrt((dual + 1e-06) / (primal + 1e-06))
-        size = step_size / ratio
+        size = step_size * jnp.sqrt((primal + 1e-06) / (dual + 1e-06))
         for c in range(blocks):
             scale = cscale_ref[c // places : c // places + 1, span(c % places)]
             total = functools.reduce(jnp.add, [ref[:, span(c)] for ref in got_refs])

time: 27.3 us -> 27.4 us (level)
  no operation moved by 1% of the time
where the time goes in v8:
time: 27.4 us; the launch traced here: 27.2 us
  starting transfers between devices  13.6 us (50%)
  waiting for transfers between devices  10.7 us (39%)
  Pallas kernels  1.55 us (6%)
  between operations  1.32 us (5%)
    ppermute x8, waiting for transfers between devices, relayed(): return lax.ppermute(value, ('band', 'batch'), pairs)  9 us
    ppermute x8, starting transfers between devices, relayed(): return lax.ppermute(value, ('band', 'batch'), pairs)  8.89 us
    ppermute x6, starting transfers between devices, swap(): return lax.ppermute(value, 'batch', [(i, i ^ 1) for i in range(count)])  4.69 us
    ppermute x6, waiting for transfers between devices, swap(): return lax.ppermute(value, 'batch', [(i, i ^ 1) for i in range(count)])  1.66 us
    pallas_call x1, Pallas kernels, shards(): pl.pallas_call(scale_kernel, out_shape=(pltpu.SMEM((2, ntile), jnp.int32)...  0.92 us
    pallas_call x1, Pallas kernels, shards(): pl.pallas_call(finish_kernel, out_shape=(f32(*x_start.shape), f32(*y_star...  0.61 us
  transfers between devices with their start and end apart: 14, of which 9 were waited for; matrix products, arithmetic and copies ran while one was open for 0% of the time, Pallas kernels for 0%

profile of v8, /device:TPU:0, one launch (start us, length us, event | category | flops | bytes accessed | tf_op | source)
XLA Modules:
  0.0 27.2 jit_solution(11448466606414677619)
XLA Ops:
  1.3 0.9 %row_scales.1 = (s32[2,128]{1,0:T(2,128)S(4)}, f32[2,1024]{1,0:T(2,128)S(1)}, bf16[128,128,128]{2,1,0:T(8,128)(2,1)S(1)}, f32[5,128,128]{2,1,0:T(8,128)S(1)}, f32[4,128]{1,0:T(4,128)S(1)}) custom-call(s32[1,128]{1,0:T(1,128)} %rows_ref.1, s32[1,128]{1,0:T(1,128)} %cols_ref.1, s32[1]{0:T(128)S(6)} %copy.10.count_ref, f32[2,512]{1,0:T(2,128)} %y_ref.1, ...), custom_call_target="tpu_custom_call" | custom-call | bytes 4194304 | tf_op jit(solution)/shard_map/row_scales/pallas_call | solution.py:381
  2.2 2.2 %collective-permute-start = (f32[2,1024]{1,0:T(2,128)S(1)}, f32[2,1024]{1,0:T(2,128)S(1)}, u32[]{:S(2)}, u32[]{:S(2)}) collective-permute-start(f32[2,1024]{1,0:T(2,128)S(1)} %get-tuple-element.20.mine_ref), channel_id=1, source_target_pairs={{0,1},{1,0},{2,3},{3,2},{4,5},{5,4},{6,7},{7,6},{8,9},{9,8},{10,11... | collective-permute-start | bytes 24584 | tf_op jit(solution)/shard_map/ppermute | solution.py:331
  4.4 0.8 %collective-permute-done.other_ref = f32[2,1024]{1,0:T(2,128)S(1)} collective-permute-done((f32[2,1024]{1,0:T(2,128)S(1)}, f32[2,1024]{1,0:T(2,128)S(1)}, u32[]{:S(2)}, u32[]{:S(2)}) %collective-permute-start) | collective-permute-done | bytes 8224 | tf_op jit(solution)/shard_map/ppermute | solution.py:331
  5.2 1.3 %collective-permute-start.4 = (f32[4,2816]{1,0:T(4,128)S(1)}, f32[4,2816]{1,0:T(4,128)S(1)}, u32[]{:S(2)}, u32[]{:S(2)}) collective-permute-start(f32[4,2816]{1,0:T(4,128)S(1)} %get-tuple-element.21), channel_id=1, source_target_pairs={{0,1},{1,12},{2,3},{3,14},{4,5},{5,8},{6,7},{7,10},{8,9},{9,4},{10... | collective-permute-start | bytes 135176 | tf_op jit(solution)/shard_map/ppermute | solution.py:341
  6.5 2.2 %collective-permute-start.3 = (f32[4,2816]{1,0:T(4,128)S(1)}, f32[4,2816]{1,0:T(4,128)S(1)}, u32[]{:S(2)}, u32[]{:S(2)}) collective-permute-start(f32[4,2816]{1,0:T(4,128)S(1)} %get-tuple-element.21), channel_id=1, source_target_pairs={{0,1},{1,8},{2,3},{3,10},{4,5},{5,12},{6,7},{7,14},{8,9},{9,0},{10... | collective-permute-start | bytes 135176 | tf_op jit(solution)/shard_map/ppermute | solution.py:341
  8.7 0.3 %collective-permute-start.2 = (f32[4,2816]{1,0:T(4,128)S(1)}, f32[4,2816]{1,0:T(4,128)S(1)}, u32[]{:S(2)}, u32[]{:S(2)}) collective-permute-start(f32[4,2816]{1,0:T(4,128)S(1)} %get-tuple-element.21), channel_id=1, source_target_pairs={{0,1},{1,4},{2,3},{3,6},{4,5},{5,0},{6,7},{7,2},{8,9},{9,12},{10,1... | collective-permute-start | bytes 135176 | tf_op jit(solution)/shard_map/ppermute | solution.py:341
  9.1 0.3 %collective-permute-start.1 = (f32[4,2816]{1,0:T(4,128)S(1)}, f32[4,2816]{1,0:T(4,128)S(1)}, u32[]{:S(2)}, u32[]{:S(2)}) collective-permute-start(f32[4,2816]{1,0:T(4,128)S(1)} %get-tuple-element.21), channel_id=1, source_target_pairs={{0,1},{1,0},{2,3},{3,2},{4,5},{5,4},{6,7},{7,6},{8,9},{9,8},{10,11... | collective-permute-start | bytes 135176 | tf_op jit(solution)/shard_map/ppermute | solution.py:331
  9.3 1.9 %collective-permute-done.4.refs_3_ = f32[4,2816]{1,0:T(4,128)S(1)} collective-permute-done((f32[4,2816]{1,0:T(4,128)S(1)}, f32[4,2816]{1,0:T(4,128)S(1)}, u32[]{:S(2)}, u32[]{:S(2)}) %collective-permute-start.4) | collective-permute-done | bytes 45088 | tf_op jit(solution)/shard_map/ppermute | solution.py:341
  11.2 0.0 collective-permute-done.3.refs_2_
  11.2 1.0 %collective-permute-done.2.refs_1_ = f32[4,2816]{1,0:T(4,128)S(1)} collective-permute-done((f32[4,2816]{1,0:T(4,128)S(1)}, f32[4,2816]{1,0:T(4,128)S(1)}, u32[]{:S(2)}, u32[]{:S(2)}) %collective-permute-start.2) | collective-permute-done | bytes 45088 | tf_op jit(solution)/shard_map/ppermute | solution.py:341
  12.2 0.0 collective-permute-done.1.refs_0_
  12.2 0.0 copy-start
  12.2 0.6 %collective-permute-start.6 = (f32[4,3584]{1,0:T(4,128)S(1)}, f32[4,3584]{1,0:T(4,128)S(1)}, u32[]{:S(2)}, u32[]{:S(2)}) collective-permute-start(f32[4,3584]{1,0:T(4,128)S(1)} %merge.1), channel_id=1, source_target_pairs={{0,17},{1,0},{2,19},{3,2},{4,21},{5,4},{6,23},{7,6},{8,25},{9,8},{... | collective-permute-start | bytes 172040 | tf_op jit(solution)/shard_map/ppermute | solution.py:341
  12.9 0.0 collective-permute-start.5
  12.9 1.8 %collective-permute-done.6.rest_1_ = f32[4,3584]{1,0:T(4,128)S(1)} collective-permute-done((f32[4,3584]{1,0:T(4,128)S(1)}, f32[4,3584]{1,0:T(4,128)S(1)}, u32[]{:S(2)}, u32[]{:S(2)}) %collective-permute-start.6) | collective-permute-done | bytes 57376 | tf_op jit(solution)/shard_map/ppermute | solution.py:341
  14.7 0.0 collective-permute-done.5.rest_0_
  14.7 0.0 copy-done
  14.7 4.3 %collective-permute-start.10 = (f32[4,2176]{1,0:T(4,128)S(1)}, f32[4,2176]{1,0:T(4,128)S(1)}, u32[]{:S(2)}, u32[]{:S(2)}) collective-permute-start(f32[4,2176]{1,0:T(4,128)S(1)} %get-tuple-element.23), channel_id=1, source_target_pairs={{0,1},{1,12},{2,3},{3,14},{4,5},{5,8},{6,7},{7,10},{8,9},{9,4},{10... | collective-permute-start | bytes 104456 | tf_op jit(solution)/shard_map/ppermute | solution.py:341
  19.0 0.1 collective-permute-start.9
  19.0 0.1 collective-permute-start.8
  19.1 0.1 collective-permute-start.7
  19.2 1.8 %collective-permute-done.10 = f32[4,2176]{1,0:T(4,128)S(1)} collective-permute-done((f32[4,2176]{1,0:T(4,128)S(1)}, f32[4,2176]{1,0:T(4,128)S(1)}, u32[]{:S(2)}, u32[]{:S(2)}) %collective-permute-start.10) | collective-permute-done | bytes 34848 | tf_op jit(solution)/shard_map/ppermute | solution.py:341
  21.0 1.4 %collective-permute-done.9 = f32[4,2176]{1,0:T(4,128)S(1)} collective-permute-done((f32[4,2176]{1,0:T(4,128)S(1)}, f32[4,2176]{1,0:T(4,128)S(1)}, u32[]{:S(2)}, u32[]{:S(2)}) %collective-permute-start.9) | collective-permute-done | bytes 34848 | tf_op jit(solution)/shard_map/ppermute | solution.py:341
  22.3 0.1 collective-permute-done.8
  22.4 0.0 collective-permute-done.7
  22.4 0.1 collective-permute-start.12
  22.5 0.5 %collective-permute-start.11 = (f32[4,2176]{1,0:T(4,128)S(1)}, f32[4,2176]{1,0:T(4,128)S(1)}, u32[]{:S(2)}, u32[]{:S(2)}) collective-permute-start(f32[4,2176]{1,0:T(4,128)S(1)} %add_add_fusion), channel_id=1, source_target_pairs={{0,1},{1,0},{2,3},{3,2},{4,5},{5,4},{6,7},{7,6},{8,9},{9,8},{10,11... | collective-permute-start | bytes 104456 | tf_op jit(solution)/shard_map/ppermute | solution.py:331
  23.0 1.1 %collective-permute-done.12.rest_1_ = f32[4,2176]{1,0:T(4,128)S(1)} collective-permute-done((f32[4,2176]{1,0:T(4,128)S(1)}, f32[4,2176]{1,0:T(4,128)S(1)}, u32[]{:S(2)}, u32[]{:S(2)}) %collective-permute-start.12) | collective-permute-done | bytes 34848 | tf_op jit(solution)/shard_map/ppermute | solution.py:341
  24.1 0.0 collective-permute-done.11.rest_0_
  24.1 1.6 %collective-permute-start.13 = (f32[2,768]{1,0:T(2,128)S(1)}, f32[2,768]{1,0:T(2,128)S(1)}, u32[]{:S(2)}, u32[]{:S(2)}) collective-permute-start(f32[2,768]{1,0:T(2,128)S(1)} %get-tuple-element.29), channel_id=1, source_target_pairs={{0,1},{1,0},{2,3},{3,2},{4,5},{5,4},{6,7},{7,6},{8,9},{9,8},{10,11... | collective-permute-start | bytes 18440 | tf_op jit(solution)/shard_map/ppermute | solution.py:331
  25.7 0.8 %collective-permute-done.13.got_ref = f32[2,768]{1,0:T(2,128)S(1)} collective-permute-done((f32[2,768]{1,0:T(2,128)S(1)}, f32[2,768]{1,0:T(2,128)S(1)}, u32[]{:S(2)}, u32[]{:S(2)}) %collective-permute-start.13) | collective-permute-done | bytes 6176 | tf_op jit(solution)/shard_map/ppermute | solution.py:331
  26.5 0.6 %finish.1 = (f32[2,256]{1,0:T(2,128)}, f32[2,512]{1,0:T(2,128)}) custom-call(f32[2,768]{1,0:T(2,128)S(1)} %get-tuple-element.28.mine_ref, f32[2,768]{1,0:T(2,128)S(1)} %collective-permute-done.13.got_ref), custom_call_target="tpu_custom_call" | custom-call | tf_op jit(solution)/shard_map/finish/pallas_call | solution.py:479
  (7 shorter events, 0.0 us)
Async XLA Ops:
  2.2 3.0 %collective-permute-start = (f32[2,1024]{1,0:T(2,128)S(1)}, f32[2,1024]{1,0:T(2,128)S(1)}, u32[]{:S(2)}, u32[]{:S(2)}) collective-permute-start(f32[2,1024]{1,0:T(2,128)S(1)} %get-tuple-element.20.mine_ref), channel_id=1, source_target_pairs={{0,1},{1,0},{2,3},{3,2},{4,5},{5,4},{6,7},{7,6},{8,9},{9,8},{10,11... | collective-permute-start | bytes 24584 | tf_op jit(solution)/shard_map/ppermute | solution.py:331
  5.2 6.0 %collective-permute-start.4 = (f32[4,2816]{1,0:T(4,128)S(1)}, f32[4,2816]{1,0:T(4,128)S(1)}, u32[]{:S(2)}, u32[]{:S(2)}) collective-permute-start(f32[4,2816]{1,0:T(4,128)S(1)} %get-tuple-element.21), channel_id=1, source_target_pairs={{0,1},{1,12},{2,3},{3,14},{4,5},{5,8},{6,7},{7,10},{8,9},{9,4},{10... | collective-permute-start | bytes 135176 | tf_op jit(solution)/shard_map/ppermute | solution.py:341
  6.5 4.7 %collective-permute-start.3 = (f32[4,2816]{1,0:T(4,128)S(1)}, f32[4,2816]{1,0:T(4,128)S(1)}, u32[]{:S(2)}, u32[]{:S(2)}) collective-permute-start(f32[4,2816]{1,0:T(4,128)S(1)} %get-tuple-element.21), channel_id=1, source_target_pairs={{0,1},{1,8},{2,3},{3,10},{4,5},{5,12},{6,7},{7,14},{8,9},{9,0},{10... | collective-permute-start | bytes 135176 | tf_op jit(solution)/shard_map/ppermute | solution.py:341
  8.7 3.5 %collective-permute-start.2 = (f32[4,2816]{1,0:T(4,128)S(1)}, f32[4,2816]{1,0:T(4,128)S(1)}, u32[]{:S(2)}, u32[]{:S(2)}) collective-permute-start(f32[4,2816]{1,0:T(4,128)S(1)} %get-tuple-element.21), channel_id=1, source_target_pairs={{0,1},{1,4},{2,3},{3,6},{4,5},{5,0},{6,7},{7,2},{8,9},{9,12},{10,1... | collective-permute-start | bytes 135176 | tf_op jit(solution)/shard_map/ppermute | solution.py:341
  9.1 3.1 %collective-permute-start.1 = (f32[4,2816]{1,0:T(4,128)S(1)}, f32[4,2816]{1,0:T(4,128)S(1)}, u32[]{:S(2)}, u32[]{:S(2)}) collective-permute-start(f32[4,2816]{1,0:T(4,128)S(1)} %get-tuple-element.21), channel_id=1, source_target_pairs={{0,1},{1,0},{2,3},{3,2},{4,5},{5,4},{6,7},{7,6},{8,9},{9,8},{10,11... | collective-permute-start | bytes 135176 | tf_op jit(solution)/shard_map/ppermute | solution.py:331
  12.2 2.5 %copy-start = (f32[512]{0:T(512)S(1)}, f32[512]{0:T(512)}, u32[]{:S(2)}) copy-start(f32[512]{0:T(512)} %param.13) | copy-start | bytes 6148
  12.2 2.4 %collective-permute-start.6 = (f32[4,3584]{1,0:T(4,128)S(1)}, f32[4,3584]{1,0:T(4,128)S(1)}, u32[]{:S(2)}, u32[]{:S(2)}) collective-permute-start(f32[4,3584]{1,0:T(4,128)S(1)} %merge.1), channel_id=1, source_target_pairs={{0,17},{1,0},{2,19},{3,2},{4,21},{5,4},{6,23},{7,6},{8,25},{9,8},{... | collective-permute-start | bytes 172040 | tf_op jit(solution)/shard_map/ppermute | solution.py:341
  12.9 1.8 %collective-permute-start.5 = (f32[4,3584]{1,0:T(4,128)S(1)}, f32[4,3584]{1,0:T(4,128)S(1)}, u32[]{:S(2)}, u32[]{:S(2)}) collective-permute-start(f32[4,3584]{1,0:T(4,128)S(1)} %merge.1), channel_id=1, source_target_pairs={{0,1},{1,0},{2,3},{3,2},{4,5},{5,4},{6,7},{7,6},{8,9},{9,8},{10,11... | collective-permute-start | bytes 172040 | tf_op jit(solution)/shard_map/ppermute | solution.py:331
  14.7 6.3 %collective-permute-start.10 = (f32[4,2176]{1,0:T(4,128)S(1)}, f32[4,2176]{1,0:T(4,128)S(1)}, u32[]{:S(2)}, u32[]{:S(2)}) collective-permute-start(f32[4,2176]{1,0:T(4,128)S(1)} %get-tuple-element.23), channel_id=1, source_target_pairs={{0,1},{1,12},{2,3},{3,14},{4,5},{5,8},{6,7},{7,10},{8,9},{9,4},{10... | collective-permute-start | bytes 104456 | tf_op jit(solution)/shard_map/ppermute | solution.py:341
  19.0 3.4 %collective-permute-start.9 = (f32[4,2176]{1,0:T(4,128)S(1)}, f32[4,2176]{1,0:T(4,128)S(1)}, u32[]{:S(2)}, u32[]{:S(2)}) collective-permute-start(f32[4,2176]{1,0:T(4,128)S(1)} %get-tuple-element.23), channel_id=1, source_target_pairs={{0,1},{1,8},{2,3},{3,10},{4,5},{5,12},{6,7},{7,14},{8,9},{9,0},{10... | collective-permute-start | bytes 104456 | tf_op jit(solution)/shard_map/ppermute | solution.py:341
  19.0 3.4 %collective-permute-start.8 = (f32[4,2176]{1,0:T(4,128)S(1)}, f32[4,2176]{1,0:T(4,128)S(1)}, u32[]{:S(2)}, u32[]{:S(2)}) collective-permute-start(f32[4,2176]{1,0:T(4,128)S(1)} %get-tuple-element.23), channel_id=1, source_target_pairs={{0,1},{1,4},{2,3},{3,6},{4,5},{5,0},{6,7},{7,2},{8,9},{9,12},{10,1... | collective-permute-start | bytes 104456 | tf_op jit(solution)/shard_map/ppermute | solution.py:341
  19.1 3.3 %collective-permute-start.7 = (f32[4,2176]{1,0:T(4,128)S(1)}, f32[4,2176]{1,0:T(4,128)S(1)}, u32[]{:S(2)}, u32[]{:S(2)}) collective-permute-start(f32[4,2176]{1,0:T(4,128)S(1)} %get-tuple-element.23), channel_id=1, source_target_pairs={{0,1},{1,0},{2,3},{3,2},{4,5},{5,4},{6,7},{7,6},{8,9},{9,8},{10,11... | collective-permute-start | bytes 104456 | tf_op jit(solution)/shard_map/ppermute | solution.py:331
  22.4 1.7 %collective-permute-start.12 = (f32[4,2176]{1,0:T(4,128)S(1)}, f32[4,2176]{1,0:T(4,128)S(1)}, u32[]{:S(2)}, u32[]{:S(2)}) collective-permute-start(f32[4,2176]{1,0:T(4,128)S(1)} %add_add_fusion), channel_id=1, source_target_pairs={{0,17},{1,0},{2,19},{3,2},{4,21},{5,4},{6,23},{7,6},{8,25},{9,8},{... | collective-permute-start | bytes 104456 | tf_op jit(solution)/shard_map/ppermute | solution.py:341
  22.5 1.6 %collective-permute-start.11 = (f32[4,2176]{1,0:T(4,128)S(1)}, f32[4,2176]{1,0:T(4,128)S(1)}, u32[]{:S(2)}, u32[]{:S(2)}) collective-permute-start(f32[4,2176]{1,0:T(4,128)S(1)} %add_add_fusion), channel_id=1, source_target_pairs={{0,1},{1,0},{2,3},{3,2},{4,5},{5,4},{6,7},{7,6},{8,9},{9,8},{10,11... | collective-permute-start | bytes 104456 | tf_op jit(solution)/shard_map/ppermute | solution.py:331
  24.1 2.4 %collective-permute-start.13 = (f32[2,768]{1,0:T(2,128)S(1)}, f32[2,768]{1,0:T(2,128)S(1)}, u32[]{:S(2)}, u32[]{:S(2)}) collective-permute-start(f32[2,768]{1,0:T(2,128)S(1)} %get-tuple-element.29), channel_id=1, source_target_pairs={{0,1},{1,0},{2,3},{3,2},{4,5},{5,4},{6,7},{7,6},{8,9},{9,8},{10,11... | collective-permute-start | bytes 18440 | tf_op jit(solution)/shard_map/ppermute | solution.py:331
